TPU v7x, 512 devices: a whole 4x8x8 slice. The times are simulated.
512 devices in a mesh: replica: 32 (over z_hi, x, core), shard: 16 (over z_lo, y).
Axes of the slice: x: 4, y: 8, z: 8 (z_hi: 4, z_lo: 2; z = z_hi * 2 + z_lo), core: 2. Of those that a mesh axis runs over, the one named last changes fastest.
Arguments:
- tokens: bfloat16 [65536, 8192], P(('replica', 'shard')), may hold values from -6 to 6
- cotangent: bfloat16 [65536, 512], P(('replica', 'shard')), may hold values from -0.125 to 0.125
- inner_weight: bfloat16 [32, 8192, 512], P('replica', 'shard'), may hold values from -0.0625 to 0.0625
- fragments: bfloat16 [32, 2, 8192, 512], P('replica', None, 'shard'), may hold values from -12 to 12
- outer_params: float32 [2, 8192, 512], P(None, ('shard', 'replica')), may hold values from -3 to 3
- momentum: float32 [2, 8192, 512], P(None, ('shard', 'replica')), may hold values from -3 to 3
- step_index: int32 [1], replicated, may hold values from 0 to 63
Outputs:
- weight_grad: bfloat16 [32, 8192, 512], P('replica', 'shard')
- new_outer: float32 [2, 8192, 512], P(None, ('shard', 'replica'))
- new_momentum: float32 [2, 8192, 512], P(None, ('shard', 'replica'))
- new_fragment: bfloat16 [32, 8192, 512], P('replica', 'shard')
All inputs are finite; a program needn't handle non-finite values.
Results may differ from a plain program's by a relative error of at most 0.012.
Values may be sent and summed in bfloat16 or wider, within the bound.
No kernel may reach another device: no remote copies, remote signals or barrier semaphores. Data moves between devices by JAX's collectives and lax.ppermute only.
A program may use at most 64 MiB of HBM per device.

v0:
```python
import jax
import jax.numpy as jnp
from jax import lax
from jax.sharding import PartitionSpec as P

NFRAG = 2


base_rate = 0.7
decay_rate = 0.9
mix_weight = 0.5


def body(tokens, cotangent, inner_weight, fragments, outer_params, momentum, step_index):
    outer_round = step_index[0]
    due_index = outer_round % NFRAG
    outer_rate = base_rate / jnp.sqrt(1.0 + (outer_round // NFRAG).astype(jnp.float32))
    features = lax.all_to_all(tokens, "shard", split_axis=1, concat_axis=0, tiled=True)
    weight_block = inner_weight[0]
    projected = jnp.dot(
        tokens,
        lax.all_gather(weight_block, "shard", axis=0, tiled=True),
        preferred_element_type=jnp.float32,
    )
    sigmoid_y = jax.nn.sigmoid(projected)
    out_grad = (
        cotangent.astype(jnp.float32) * sigmoid_y * (1.0 + projected * (1.0 - sigmoid_y))
    ).astype(jnp.bfloat16)
    all_grads = lax.all_gather(out_grad, "shard", axis=0, tiled=True)
    weight_grad = lax.dot_general(
        features, all_grads, (((0,), (0,)), ((), ())), preferred_element_type=jnp.float32
    )
    weight_grad = weight_grad.astype(jnp.bfloat16)[None]
    local_due = lax.dynamic_index_in_dim(fragments[0], due_index, 0, keepdims=False)
    replica_count = lax.axis_size("replica")
    summed = lax.psum_scatter(
        local_due.astype(jnp.float32).astype(jnp.bfloat16),
        "replica",
        scatter_dimension=0,
        tiled=True,
    ).astype(jnp.float32)
    mean_local = summed / replica_count
    outer_due = lax.dynamic_index_in_dim(outer_params, due_index, 0, keepdims=False)
    moment_due = lax.dynamic_index_in_dim(momentum, due_index, 0, keepdims=False)
    pseudo_grad = outer_due - mean_local
    moment_next = decay_rate * moment_due + pseudo_grad
    outer_next = outer_due - outer_rate * (pseudo_grad + decay_rate * moment_next)
    new_momentum = lax.dynamic_update_index_in_dim(momentum, moment_next, due_index, 0)
    new_outer = lax.dynamic_update_index_in_dim(outer_params, outer_next, due_index, 0)
    regathered = lax.all_gather(outer_next.astype(jnp.bfloat16), "replica", axis=0, tiled=True)
    new_fragment = (
        mix_weight * local_due.astype(jnp.float32)
        + (1.0 - mix_weight) * regathered.astype(jnp.float32)
    ).astype(jnp.bfloat16)[None]
    return (weight_grad, new_outer, new_momentum, new_fragment)


def solution(mesh):
    placed = (
        P(("replica", "shard"), None),
        P(("replica", "shard"), None),
        P("replica", "shard", None),
        P("replica", None, "shard", None),
        P(None, ("shard", "replica"), None),
        P(None, ("shard", "replica"), None),
        P(),
    )
    return jax.shard_map(
        body,
        mesh=mesh,
        in_specs=placed,
        out_specs=(
            P("replica", "shard", None),
            P(None, ("shard", "replica"), None),
            P(None, ("shard", "replica"), None),
            P("replica", "shard", None),
        ),
        check_vma=False,
    )
```

profile of v0, /device:TPU:57, one launch (start us, length us, event | category | flops | bytes accessed | tf_op | source)
XLA Modules:
  0.0 257.1 jit_solution(3120018725490174846)
XLA Ops:
  8.0 0.0 all-gather.6.cloned.1.call-start
  8.1 1.0 copy.22
  9.0 0.8 copy.21
  9.9 0.0 all-gather.6.cloned.1.call-update
  9.9 0.0 reduce-scatter.2.cloned.1.call-start
  10.6 1.9 dynamic-slice_bitcast_fusion
  12.5 0.0 reduce-scatter.2.cloned.1.call-update
  12.5 2.5 copy.13
  15.0 8.3 %all-to-all-start = ((bf16[128,16,512]{0,2,1:T(8,128)(2,1)}), bf16[128,16,512]{0,2,1:T(8,128)(2,1)}, u32[]{:S(2)}, u32[]{:S(2)}) async-start(bf16[128,16,512]{0,2,1:T(8,128)(2,1)} %bitcast.42), calls=%async_computation | async-start | bytes 4194304 | tf_op jit(solution)/shard_map/all_to_all | solution.py:18
  23.3 0.0 all-gather.4.cloned.1.call-start
  23.3 133.7 %all-gather.6.cloned.1.call-done = bf16[1,8192,512]{2,1,0:T(8,128)(2,1)} async-done(((bf16[1,512,512]{2,1,0:T(8,128)(2,1)}), bf16[1,8192,512]{2,1,0:T(8,128)(2,1)}) %all-gather.6.cloned.1.call-update) | async-done | bytes 8388624 | tf_op jit(solution)/shard_map/all_gather | solution.py:22
  157.0 5.4 %multiply_convert_fusion.1 = bf16[128,512]{1,0:T(8,128)(2,1)} fusion(bf16[128,8192]{1,0:T(8,128)(2,1)S(1)} %copy-done, bf16[1,8192,512]{2,1,0:T(8,128)(2,1)} %all-gather.6.cloned.1.call-done, bf16[128,512]{1,0:T(8,128)(2,1)S(1)} %copy-done.4), kind=kOutput, calls=%fused_computation.7 | convolution fusion | flops 1074397184 | bytes 10747904 | tf_op jit(solution)/shard_map/dot_general | solution.py:20
  162.4 0.0 all-gather.4.cloned.1.call-update
  162.5 30.2 %reduce-scatter.2.cloned.1.call-done = bf16[16,512]{1,0:T(8,128)(2,1)} async-done(((bf16[512,512]{1,0:T(8,128)(2,1)}), bf16[16,512]{1,0:T(8,128)(2,1)}) %reduce-scatter.2.cloned.1.call-update) | async-done | bytes 16400 | tf_op jit(solution)/shard_map/reduce_scatter | solution.py:36
  192.7 0.7 fusion.6
  193.5 0.0 copy-start.2
  193.5 0.0 copy-start.3
  193.5 48.4 %all_gather.11 = bf16[512,512]{1,0:T(8,128)(2,1)S(1)} all-gather(bf16[16,512]{1,0:T(8,128)(2,1)S(1)} %get-tuple-element.16), channel_id=1, replica_groups=mesh['replica'=32,'shard'=16] {'replica'}, dimensions={0}, use_global_device_ids=true | all-gather | bytes 540672 | tf_op jit(solution)/shard_map/all_gather | solution.py:50
  241.9 1.0 fusion.3
  242.9 0.0 all-to-all-done
  242.9 2.9 %copy.14 = bf16[16,128,512]{2,1,0:T(8,128)(2,1)S(1)} copy(bf16[16,128,512]{1,2,0:T(8,128)(2,1)} %bitcast.2) | data formatting | bytes 4194304 | tf_op jit(solution)/shard_map/all_to_all | solution.py:18
  245.8 0.0 all-gather.4.cloned.1.call-done
  245.8 2.9 %fusion.2 = bf16[1,512,512]{1,2,0:T(8,128)(2,1)S(1)} fusion(bf16[2048,512]{1,0:T(8,128)(2,1)} %all-gather.4.cloned.1.call-done, bf16[2048,512]{1,0:T(8,128)(2,1)S(1)} %bitcast.43), kind=kOutput, calls=%fused_computation.3 | convolution fusion | flops 1074003968 | bytes 4718592 | tf_op jit(solution)/shard_map/dot_general | solution.py:30
  248.7 1.0 copy.15
  (9 shorter events, 0.0 us)
Async XLA Ops:
  8.0 4.5 %copy-start = (bf16[128,8192]{1,0:T(8,128)(2,1)S(1)}, bf16[128,8192]{1,0:T(8,128)(2,1)}, u32[]{:S(2)}) copy-start(bf16[128,8192]{1,0:T(8,128)(2,1)} %param.7) | copy-start | bytes 6291460
  8.0 149.0 %all-gather.6.cloned.1.call-start = ((), (), s32[]{:S(2)}) async-start(), calls=%async_computation.4 | async-start | bytes 8912896 | tf_op jit(solution)/shard_map/all_gather | solution.py:22
  9.9 182.8 %reduce-scatter.2.cloned.1.call-start = ((), (), s32[]{:S(2)}) async-start(), calls=%async_computation.3 | async-start | bytes 540672 | tf_op jit(solution)/shard_map/reduce_scatter | solution.py:36
  15.0 142.0 %copy-start.4 = (bf16[128,512]{1,0:T(8,128)(2,1)S(1)}, bf16[128,512]{1,0:T(8,128)(2,1)}, u32[]{:S(2)}) copy-start(bf16[128,512]{1,0:T(8,128)(2,1)} %param.8) | copy-start | bytes 393220
  15.0 227.9 %all-to-all-start = ((bf16[128,16,512]{0,2,1:T(8,128)(2,1)}), bf16[128,16,512]{0,2,1:T(8,128)(2,1)}, u32[]{:S(2)}, u32[]{:S(2)}) async-start(bf16[128,16,512]{0,2,1:T(8,128)(2,1)} %bitcast.42), calls=%async_computation | async-start | bytes 4194304 | tf_op jit(solution)/shard_map/all_to_all | solution.py:18
  23.3 218.7 %copy-start.1 = (bf16[1,2,512,512]{3,2,1,0:T(8,128)(2,1)S(1)}, bf16[1,2,512,512]{3,2,1,0:T(8,128)(2,1)}, u32[]{:S(2)}) copy-start(bf16[1,2,512,512]{3,2,1,0:T(8,128)(2,1)} %param.10) | copy-start | bytes 3145732
  23.3 222.5 %all-gather.4.cloned.1.call-start = ((), (), s32[]{:S(2)}) async-start(), calls=%async_computation.2 | async-start | bytes 2228224 | tf_op jit(solution)/shard_map/all_gather | solution.py:29
  193.5 52.3 %copy-start.2 = (f32[2,16,512]{2,1,0:T(8,128)}, f32[2,16,512]{2,1,0:T(8,128)S(1)}, u32[]{:S(2)}) copy-start(f32[2,16,512]{2,1,0:T(8,128)S(1)} %get-tuple-element.19) | copy-start | bytes 196612
  193.5 52.3 %copy-start.3 = (f32[2,16,512]{2,1,0:T(8,128)}, f32[2,16,512]{2,1,0:T(8,128)S(1)}, u32[]{:S(2)}) copy-start(f32[2,16,512]{2,1,0:T(8,128)S(1)} %get-tuple-element.20) | copy-start | bytes 196612
Sparse Core Ops, SparseCore 0:
  10.9 146.0 all-gather.5
  162.5 64.0 all-gather.3
Sparse Core Ops, SparseCore 1:
  15.3 177.4 reduce-scatter.1
where the time goes:
time: 258 us; the launch traced here: 257 us
  waiting for transfers between devices  164 us (64%)
  blocking collectives  48.4 us (19%)
  between operations  16.3 us (6%)
  local copies, waits for them, and re-layouts  10 us (4%)
  starting transfers between devices  8.39 us (3%)
  matrix products  8.24 us (3%)
    all_gather x1, waiting for transfers between devices, body(): lax.all_gather(weight_block, 'shard', axis=0, tiled=True)  134 us
    all_gather x1, blocking collectives, body(): lax.all_gather(outer_next.astype(jnp.bfloat16), 'replica', axis=0, tiled=...  48.4 us
    reduce_scatter x1, waiting for transfers between devices, body(): lax.psum_scatter(local_due.astype(jnp.float32).astype(jnp.bfloat16), 'rep...  30.2 us
    all_to_all x1, starting transfers between devices, body(): lax.all_to_all(tokens, 'shard', split_axis=1, concat_axis=0, tiled=True)  8.26 us
    dot_general x1, matrix products, body(): jnp.dot(tokens, lax.all_gather(weight_block, 'shard', axis=0, tiled=True)...  5.38 us
    unnamed x14, local copies, waits for them, and re-layouts  5.31 us
  transfers between devices with their start and end apart: 4, of which 2 were waited for; matrix products, arithmetic and copies ran while one was open for 6% of the time, Pallas kernels for 0%

commit v1 on v0

v1 whole, which is shorter than its diff:
```python
import jax
import jax.numpy as jnp
from jax import lax
from jax.sharding import Mesh
from jax.sharding import PartitionSpec as P

NFRAG = 2
base_rate = 0.7
decay_rate = 0.9
mix_weight = 0.5
REP = ("zh", "x", "c")
SHARD = ("z", "y")
SWAP = [(0, 1), (1, 0)]


def body(tokens, cotangent, inner_weight, fragments, outer_params, momentum, step_index):
    f32, bf16 = jnp.float32, jnp.bfloat16
    z = lax.axis_index("z")
    rows, width = tokens.shape
    ny = lax.axis_size("y")
    feat, cols = inner_weight.shape[1:]
    w = inner_weight[0]

    outer_round = step_index[0]
    due = outer_round % NFRAG
    rate = base_rate / jnp.sqrt(1.0 + (outer_round // NFRAG).astype(f32))

    blocks = tokens.reshape(rows, 2, ny, feat).transpose(2, 0, 1, 3).reshape(ny, rows, 2 * feat)
    x = lax.all_to_all(blocks, "y", split_axis=0, concat_axis=0, tiled=True)
    x = x.reshape(ny * rows, 2 * feat)
    w_other = lax.ppermute(w, "z", SWAP)
    low = jnp.where(z == 0, w, w_other)
    high = jnp.where(z == 0, w_other, w)
    partial = jnp.dot(x, jnp.concatenate([low, high], 0), preferred_element_type=f32)
    partial = partial.astype(bf16).reshape(ny, rows, cols)
    parts = lax.all_to_all(partial, "y", split_axis=0, concat_axis=0, tiled=True)
    y = jnp.sum(parts.astype(f32), 0)
    s = jax.nn.sigmoid(y)
    grad = (cotangent.astype(f32) * s * (1.0 + y * (1.0 - s))).astype(bf16)
    copies = jnp.broadcast_to(grad[None], (ny, rows, cols))
    grads = lax.all_to_all(copies, "y", split_axis=0, concat_axis=0, tiled=True)
    grads = grads.reshape(ny * rows, cols)
    dims = (((0,), (0,)), ((), ()))
    theirs = lax.dynamic_slice_in_dim(x, (1 - z) * feat, feat, 1)
    mine = lax.dynamic_slice_in_dim(x, z * feat, feat, 1)
    away = lax.dot_general(theirs, grads, dims, preferred_element_type=f32).astype(bf16)
    home = lax.dot_general(mine, grads, dims, preferred_element_type=f32)
    weight_grad = (home + lax.ppermute(away, "z", SWAP).astype(f32)).astype(bf16)[None]

    nrep = lax.axis_size(REP)
    own = feat // nrep
    local = lax.dynamic_index_in_dim(fragments[0], due, 0, keepdims=False)
    terms = lax.all_to_all(local.reshape(nrep, own, cols), REP, split_axis=0, concat_axis=0, tiled=True)
    mean_local = jnp.sum(terms.astype(f32), 0) / nrep
    outer_due = lax.dynamic_index_in_dim(outer_params, due, 0, keepdims=False)
    moment_due = lax.dynamic_index_in_dim(momentum, due, 0, keepdims=False)
    pseudo = outer_due - mean_local
    moment_next = decay_rate * moment_due + pseudo
    outer_next = outer_due - rate * (pseudo + decay_rate * moment_next)
    new_momentum = lax.dynamic_update_index_in_dim(momentum, moment_next, due, 0)
    new_outer = lax.dynamic_update_index_in_dim(outer_params, outer_next, due, 0)
    halves = jnp.broadcast_to(outer_next.astype(bf16)[None], (nrep, own, cols))
    half = lax.all_to_all(halves, REP, split_axis=0, concat_axis=0, tiled=True).reshape(feat, cols)
    new_fragment = (mix_weight * local.astype(f32) + (1.0 - mix_weight) * half.astype(f32)).astype(bf16)
    return (weight_grad, new_outer, new_momentum, new_fragment[None])


def solution(mesh):
    fine = Mesh(mesh.devices.reshape(4, 4, 2, 2, 8), REP + SHARD)
    both = REP + SHARD
    placed = (
        P(both, None),
        P(both, None),
        P(REP, SHARD, None),
        P(REP, None, SHARD, None),
        P(None, SHARD + REP, None),
        P(None, SHARD + REP, None),
        P(),
    )
    return jax.shard_map(
        body,
        mesh=fine,
        in_specs=placed,
        out_specs=(P(REP, SHARD, None), P(None, SHARD + REP, None), P(None, SHARD + REP, None), P(REP, SHARD, None)),
        check_vma=False,
    )
```

time: 258 us -> 203 us (0.79)
  the two profiles are of different devices: /device:TPU:57 before, /device:TPU:6 now
where the time goes in v1:
time: 203 us; the launch traced here: 202 us
  waiting for transfers between devices  133 us (66%)
  starting transfers between devices  43.1 us (21%)
  local copies, waits for them, and re-layouts  12.4 us (6%)
  matrix products  8.55 us (4%)
  other arithmetic  3.4 us (2%)
    all_to_all x1, waiting for transfers between devices, body(): x = lax.all_to_all(blocks, 'y', split_axis=0, concat_axis=0, tiled=True)  34.2 us
    all_to_all x1, waiting for transfers between devices, body(): grads = lax.all_to_all(copies, 'y', split_axis=0, concat_axis=0, tiled=True)  27.4 us
    all_to_all x1, waiting for transfers between devices, body(): lax.all_to_all(partial, 'y', split_axis=0, concat_axis=0, tiled=True)  25.5 us
    all_to_all x1, waiting for transfers between devices, body(): lax.all_to_all(local.reshape(nrep, own, cols), REP, split_axis=0, concat_...  17.2 us
    all_to_all x1, starting transfers between devices, body(): lax.all_to_all(local.reshape(nrep, own, cols), REP, split_axis=0, concat_...  13.4 us
    ppermute x1, waiting for transfers between devices, body(): w_other = lax.ppermute(w, 'z', SWAP)  11.6 us
    all_to_all x1, waiting for transfers between devices, body(): lax.all_to_all(halves, REP, split_axis=0, concat_axis=0, tiled=True)  11.5 us
    all_to_all x1, starting transfers between devices, body(): x = lax.all_to_all(blocks, 'y', split_axis=0, concat_axis=0, tiled=True)  7.23 us
  transfers between devices with their start and end apart: 7, of which 7 were waited for; matrix products, arithmetic and copies ran while one was open for 4% of the time, Pallas kernels for 0%

profile of v1, /device:TPU:6, one launch (start us, length us, event | category | flops | bytes accessed | tf_op | source)
XLA Modules:
  0.0 201.9 jit_solution(11777499731233142400)
XLA Ops:
  1.5 3.2 %copy.14 = bf16[128,8192]{0,1:T(8,128)(2,1)S(1)} copy(bf16[128,8192]{1,0:T(8,128)(2,1)} %param.7) | data formatting | bytes 4194304 | tf_op args[0]
  4.7 1.5 copy.15
  6.2 7.2 %all-to-all-start = ((bf16[8,128,1024]{1,2,0:T(8,128)(2,1)}), bf16[8,128,1024]{1,2,0:T(8,128)(2,1)S(1)}, u32[]{:S(2)}, u32[]{:S(2)}) async-start(bf16[8,128,1024]{1,2,0:T(8,128)(2,1)} %bitcast.42), calls=%async_computation | async-start | bytes 4194304 | tf_op jit(solution)/shard_map/all_to_all | solution.py:29
  13.4 4.3 %collective-permute-start = (bf16[512,512]{1,0:T(8,128)(2,1)S(1)}, bf16[512,512]{1,0:T(8,128)(2,1)S(1)}, u32[]{:S(2)}, u32[]{:S(2)}) collective-permute-start(bf16[512,512]{1,0:T(8,128)(2,1)S(1)} %bitcast.48), channel_id=1, source_target_pairs={{0,8},{8,0},{1,9},{9,1},{2,10},{10,2},{3,11},{11,3},{4,12},{12,4},... | collective-permute-start | bytes 1572872 | tf_op jit(solution)/shard_map/ppermute | solution.py:31
  17.7 11.6 %collective-permute-done = bf16[512,512]{1,0:T(8,128)(2,1)S(1)} collective-permute-done((bf16[512,512]{1,0:T(8,128)(2,1)S(1)}, bf16[512,512]{1,0:T(8,128)(2,1)S(1)}, u32[]{:S(2)}, u32[]{:S(2)}) %collective-permute-start) | collective-permute-done | bytes 524320 | tf_op jit(solution)/shard_map/ppermute | solution.py:31
  29.3 1.0 broadcast_select_fusion.1
  30.4 34.2 %all-to-all-done = bf16[8,128,1024]{1,2,0:T(8,128)(2,1)S(1)} async-done(((bf16[8,128,1024]{1,2,0:T(8,128)(2,1)}), bf16[8,128,1024]{1,2,0:T(8,128)(2,1)S(1)}, u32[]{:S(2)}, u32[]{:S(2)}) %all-to-all-start) | async-done | bytes 2097184 | tf_op jit(solution)/shard_map/all_to_all | solution.py:29
  64.6 2.6 %copy.16 = bf16[8,128,1024]{2,1,0:T(8,128)(2,1)} copy(bf16[8,128,1024]{1,2,0:T(8,128)(2,1)S(1)} %all-to-all-done) | data formatting | bytes 4194304 | tf_op jit(solution)/shard_map/all_to_all | solution.py:29
  67.3 2.9 %fusion = bf16[64,8,8,128]{3,2,1,0:T(8,128)(2,1)S(1)} fusion(bf16[1024,1024]{1,0:T(8,128)(2,1)} %bitcast.44, bf16[512,512]{1,0:T(8,128)(2,1)S(1)} %copy-done.4, bf16[512,512]{1,0:T(8,128)(2,1)S(1)} %copy-done.3), kind=kOutput, calls=%fused_computation.2 | convolution fusion | flops 1076363264 | bytes 4194304 | tf_op jit(solution)/shard_map/dot_general | solution.py:34
  70.2 1.2 copy.24
  71.3 3.7 %all-to-all-start.1 = ((bf16[8,128,512]{1,2,0:T(8,128)(2,1)}), bf16[8,128,512]{1,2,0:T(8,128)(2,1)S(1)}, u32[]{:S(2)}, u32[]{:S(2)}) async-start(bf16[8,128,512]{1,2,0:T(8,128)(2,1)} %bitcast.36), calls=%async_computation.1 | async-start | bytes 2097152 | tf_op jit(solution)/shard_map/all_to_all | solution.py:36
  76.5 25.5 %all-to-all-done.1 = bf16[8,128,512]{1,2,0:T(8,128)(2,1)S(1)} async-done(((bf16[8,128,512]{1,2,0:T(8,128)(2,1)}), bf16[8,128,512]{1,2,0:T(8,128)(2,1)S(1)}, u32[]{:S(2)}, u32[]{:S(2)}) %all-to-all-start.1) | async-done | bytes 1048608 | tf_op jit(solution)/shard_map/all_to_all | solution.py:36
  102.0 13.4 %all-to-all-start.3 = ((bf16[32,16,512]{2,1,0:T(8,128)(2,1)}), bf16[32,16,512]{2,1,0:T(8,128)(2,1)S(1)}, u32[]{:S(2)}, u32[]{:S(2)}) async-start(bf16[32,16,512]{2,1,0:T(8,128)(2,1)} %bitcast.9), calls=%async_computation.3 | async-start | bytes 1048576 | tf_op jit(solution)/shard_map/all_to_all | solution.py:53
  116.0 17.2 %all-to-all-done.3 = bf16[32,16,512]{2,1,0:T(8,128)(2,1)S(1)} async-done(((bf16[32,16,512]{2,1,0:T(8,128)(2,1)}), bf16[32,16,512]{2,1,0:T(8,128)(2,1)S(1)}, u32[]{:S(2)}, u32[]{:S(2)}) %all-to-all-start.3) | async-done | bytes 524320 | tf_op jit(solution)/shard_map/all_to_all | solution.py:53
  133.1 1.1 broadcast_in_dim.11
  134.2 4.4 %all-to-all-start.2 = ((bf16[8,128,512]{2,1,0:T(8,128)(2,1)}), bf16[8,128,512]{2,1,0:T(8,128)(2,1)}, u32[]{:S(2)}, u32[]{:S(2)}) async-start(bf16[8,128,512]{2,1,0:T(8,128)(2,1)} %broadcast_in_dim.11), calls=%async_computation.2 | async-start | bytes 2097152 | tf_op jit(solution)/shard_map/all_to_all | solution.py:41
  138.8 27.4 %all-to-all-done.2 = bf16[8,128,512]{2,1,0:T(8,128)(2,1)} async-done(((bf16[8,128,512]{2,1,0:T(8,128)(2,1)}), bf16[8,128,512]{2,1,0:T(8,128)(2,1)}, u32[]{:S(2)}, u32[]{:S(2)}) %all-to-all-start.2) | async-done | bytes 1048608 | tf_op jit(solution)/shard_map/all_to_all | solution.py:41
  167.1 6.4 %all-to-all-start.4 = ((bf16[32,16,512]{2,1,0:T(8,128)(2,1)}), bf16[32,16,512]{2,1,0:T(8,128)(2,1)S(1)}, u32[]{:S(2)}, u32[]{:S(2)}) async-start(bf16[32,16,512]{2,1,0:T(8,128)(2,1)} %broadcast_in_dim.24), calls=%async_computation.4 | async-start | bytes 1048576 | tf_op jit(solution)/shard_map/all_to_all | solution.py:63
  173.5 2.8 %convolution_convert_fusion.1 = bf16[512,512]{1,0:T(8,128)(2,1)} fusion(bf16[1024,512]{1,0:T(8,128)(2,1)} %bitcast.6, bf16[1024,1024]{1,0:T(8,128)(2,1)S(1)} %bitcast.45, s32[]{:T(128)S(6)} %select_n.43), kind=kOutput, calls=%fused_computation.3 | convolution fusion | flops 537133056 | bytes 2621444 | tf_op jit(solution)/shard_map/dot_general | solution.py:46
  176.3 3.7 %collective-permute-start.1 = (bf16[512,512]{1,0:T(8,128)(2,1)}, bf16[512,512]{1,0:T(8,128)(2,1)}, u32[]{:S(2)}, u32[]{:S(2)}) collective-permute-start(bf16[512,512]{1,0:T(8,128)(2,1)} %convolution_convert_fusion.1), channel_id=1, source_target_pairs={{0,8},{8,0},{1,9},{9,1},{2,10},{10,2},{3,11},{11,3},{4,12},{12,4},... | collective-permute-start | bytes 1572872 | tf_op jit(solution)/shard_map/ppermute | solution.py:48
  180.0 11.5 %all-to-all-done.4 = bf16[32,16,512]{2,1,0:T(8,128)(2,1)S(1)} async-done(((bf16[32,16,512]{2,1,0:T(8,128)(2,1)}), bf16[32,16,512]{2,1,0:T(8,128)(2,1)S(1)}, u32[]{:S(2)}, u32[]{:S(2)}) %all-to-all-start.4) | async-done | bytes 524320 | tf_op jit(solution)/shard_map/all_to_all | solution.py:63
  191.6 2.0 fusion.5
  193.6 5.4 %collective-permute-done.1 = bf16[512,512]{1,0:T(8,128)(2,1)} collective-permute-done((bf16[512,512]{1,0:T(8,128)(2,1)}, bf16[512,512]{1,0:T(8,128)(2,1)}, u32[]{:S(2)}, u32[]{:S(2)}) %collective-permute-start.1) | collective-permute-done | bytes 524320 | tf_op jit(solution)/shard_map/ppermute | solution.py:48
  199.0 2.9 %fusion.11 = bf16[1,512,512]{2,1,0:T(8,128)(2,1)} fusion(bf16[512,512]{1,0:T(8,128)(2,1)} %collective-permute-done.1, bf16[1024,512]{1,0:T(8,128)(2,1)} %bitcast.6, bf16[1024,1024]{1,0:T(8,128)(2,1)S(1)} %bitcast.46, s32[]{:T(128)S(6)} %select_n.39), kind=kOutput, calls=%fused_computation.16 | convolution fusion | flops 537657344 | bytes 3145732 | tf_op jit(solution)/shard_map/dot_general | solution.py:47
  (28 shorter events, 3.2 us)
Async XLA Ops:
  6.2 7.2 %copy-start.2 = (bf16[1,512,512]{2,1,0:T(8,128)(2,1)S(1)}, bf16[1,512,512]{2,1,0:T(8,128)(2,1)}, u32[]{:S(2)}) copy-start(bf16[1,512,512]{2,1,0:T(8,128)(2,1)} %param.9) | copy-start | bytes 1572868
  6.2 58.4 %all-to-all-start = ((bf16[8,128,1024]{1,2,0:T(8,128)(2,1)}), bf16[8,128,1024]{1,2,0:T(8,128)(2,1)S(1)}, u32[]{:S(2)}, u32[]{:S(2)}) async-start(bf16[8,128,1024]{1,2,0:T(8,128)(2,1)} %bitcast.42), calls=%async_computation | async-start | bytes 4194304 | tf_op jit(solution)/shard_map/all_to_all | solution.py:29
  13.4 15.9 %collective-permute-start = (bf16[512,512]{1,0:T(8,128)(2,1)S(1)}, bf16[512,512]{1,0:T(8,128)(2,1)S(1)}, u32[]{:S(2)}, u32[]{:S(2)}) collective-permute-start(bf16[512,512]{1,0:T(8,128)(2,1)S(1)} %bitcast.48), channel_id=1, source_target_pairs={{0,8},{8,0},{1,9},{9,1},{2,10},{10,2},{3,11},{11,3},{4,12},{12,4},... | collective-permute-start | bytes 1572872 | tf_op jit(solution)/shard_map/ppermute | solution.py:31
  30.4 36.9 %copy-start.3 = (bf16[512,512]{1,0:T(8,128)(2,1)S(1)}, bf16[512,512]{1,0:T(8,128)(2,1)}, u32[]{:S(2)}) copy-start(bf16[512,512]{1,0:T(8,128)(2,1)} %get-tuple-element.6) | copy-start | bytes 1572868
  30.4 36.9 %copy-start.4 = (bf16[512,512]{1,0:T(8,128)(2,1)S(1)}, bf16[512,512]{1,0:T(8,128)(2,1)}, u32[]{:S(2)}) copy-start(bf16[512,512]{1,0:T(8,128)(2,1)} %get-tuple-element.7) | copy-start | bytes 1572868
  70.1 5.5 %copy-start.1 = (bf16[1,2,512,512]{3,2,1,0:T(8,128)(2,1)S(1)}, bf16[1,2,512,512]{3,2,1,0:T(8,128)(2,1)}, u32[]{:S(2)}) copy-start(bf16[1,2,512,512]{3,2,1,0:T(8,128)(2,1)} %param.10) | copy-start | bytes 3145732
  71.3 44.1 %copy-start.8 = (bf16[128,512]{1,0:T(8,128)(2,1)S(1)}, bf16[128,512]{1,0:T(8,128)(2,1)}, u32[]{:S(2)}) copy-start(bf16[128,512]{1,0:T(8,128)(2,1)} %param.8) | copy-start | bytes 393220
  71.3 30.7 %all-to-all-start.1 = ((bf16[8,128,512]{1,2,0:T(8,128)(2,1)}), bf16[8,128,512]{1,2,0:T(8,128)(2,1)S(1)}, u32[]{:S(2)}, u32[]{:S(2)}) async-start(bf16[8,128,512]{1,2,0:T(8,128)(2,1)} %bitcast.36), calls=%async_computation.1 | async-start | bytes 2097152 | tf_op jit(solution)/shard_map/all_to_all | solution.py:36
  102.0 31.1 %all-to-all-start.3 = ((bf16[32,16,512]{2,1,0:T(8,128)(2,1)}), bf16[32,16,512]{2,1,0:T(8,128)(2,1)S(1)}, u32[]{:S(2)}, u32[]{:S(2)}) async-start(bf16[32,16,512]{2,1,0:T(8,128)(2,1)} %bitcast.9), calls=%async_computation.3 | async-start | bytes 1048576 | tf_op jit(solution)/shard_map/all_to_all | solution.py:53
  115.8 23.0 %copy-start.7 = (f32[2,16,512]{2,1,0:T(8,128)S(1)}, f32[2,16,512]{2,1,0:T(8,128)}, u32[]{:S(2)}) copy-start(f32[2,16,512]{2,1,0:T(8,128)} %param.12) | copy-start | bytes 196612
  134.2 39.3 %copy-start = (bf16[8,128,1024]{2,1,0:T(8,128)(2,1)S(1)}, bf16[8,128,1024]{2,1,0:T(8,128)(2,1)}, u32[]{:S(2)}) copy-start(bf16[8,128,1024]{2,1,0:T(8,128)(2,1)} %copy.16) | copy-start | bytes 6291460
  134.2 32.0 %all-to-all-start.2 = ((bf16[8,128,512]{2,1,0:T(8,128)(2,1)}), bf16[8,128,512]{2,1,0:T(8,128)(2,1)}, u32[]{:S(2)}, u32[]{:S(2)}) async-start(bf16[8,128,512]{2,1,0:T(8,128)(2,1)} %broadcast_in_dim.11), calls=%async_computation.2 | async-start | bytes 2097152 | tf_op jit(solution)/shard_map/all_to_all | solution.py:41
  138.8 37.5 %copy-start.6 = (f32[2,16,512]{2,1,0:T(8,128)}, f32[2,16,512]{2,1,0:T(8,128)S(1)}, u32[]{:S(2)}) copy-start(f32[2,16,512]{2,1,0:T(8,128)S(1)} %get-tuple-element.8) | copy-start | bytes 196612
  167.1 24.5 %all-to-all-start.4 = ((bf16[32,16,512]{2,1,0:T(8,128)(2,1)}), bf16[32,16,512]{2,1,0:T(8,128)(2,1)S(1)}, u32[]{:S(2)}, u32[]{:S(2)}) async-start(bf16[32,16,512]{2,1,0:T(8,128)(2,1)} %broadcast_in_dim.24), calls=%async_computation.4 | async-start | bytes 1048576 | tf_op jit(solution)/shard_map/all_to_all | solution.py:63
  176.3 22.7 %collective-permute-start.1 = (bf16[512,512]{1,0:T(8,128)(2,1)}, bf16[512,512]{1,0:T(8,128)(2,1)}, u32[]{:S(2)}, u32[]{:S(2)}) collective-permute-start(bf16[512,512]{1,0:T(8,128)(2,1)} %convolution_convert_fusion.1), channel_id=1, source_target_pairs={{0,8},{8,0},{1,9},{9,1},{2,10},{10,2},{3,11},{11,3},{4,12},{12,4},... | collective-permute-start | bytes 1572872 | tf_op jit(solution)/shard_map/ppermute | solution.py:48
  180.0 21.9 %copy-start.5 = (f32[2,16,512]{2,1,0:T(8,128)}, f32[2,16,512]{2,1,0:T(8,128)S(1)}, u32[]{:S(2)}) copy-start(f32[2,16,512]{2,1,0:T(8,128)S(1)} %constant_dynamic-update-slice_fusion) | copy-start | bytes 196612

commit v2 on v1

v2 whole, which is shorter than its diff:
```python
import functools

import jax
import jax.numpy as jnp
from jax import lax
from jax.experimental import pallas as pl
from jax.experimental.pallas import tpu as pltpu
from jax.sharding import Mesh
from jax.sharding import PartitionSpec as P

NFRAG = 2
base_rate = 0.7
decay_rate = 0.9
mix_weight = 0.5
REP = ("zh1", "zh0", "x1", "x0", "c")
SHARD = ("z", "y")
SWAP = [(0, 1), (1, 0)]
f32, bf16 = jnp.float32, jnp.bfloat16
VMEM = pl.BlockSpec(memory_space=pltpu.VMEM)
PARAMS = pltpu.CompilerParams(vmem_limit_bytes=24 * 2**20)


def pack(tokens, z, ny, feat):
    rows = tokens.shape[0]

    def kernel(z_ref, t_ref, o_ref):
        for j in range(ny):
            o_ref[j] = t_ref[:, j * feat : (j + 1) * feat]

    return pl.pallas_call(
        kernel,
        out_shape=jax.ShapeDtypeStruct((ny, rows, 2 * feat), tokens.dtype),
        grid_spec=pltpu.PrefetchScalarGridSpec(
            num_scalar_prefetch=1,
            grid=(2,),
            in_specs=[pl.BlockSpec((rows, ny * feat), lambda h, z: (0, (h + 1 + z[0]) % 2))],
            out_specs=pl.BlockSpec((ny, rows, feat), lambda h, z: (0, 0, h)),
        ),
        compiler_params=PARAMS,
    )(z[None], tokens)


def project(x, w_other, w, after):
    ny, rows, feat2 = x.shape
    feat, cols = w.shape

    def kernel(x_ref, wo_ref, w_ref, _, o_ref):
        for j in range(ny):
            acc = jnp.dot(x_ref[j, :, :feat], wo_ref[...], preferred_element_type=f32)
            acc += jnp.dot(x_ref[j, :, feat:], w_ref[...], preferred_element_type=f32)
            o_ref[j] = acc.astype(bf16)

    return pl.pallas_call(
        kernel,
        out_shape=jax.ShapeDtypeStruct((ny, rows, cols), bf16),
        in_specs=[VMEM] * 3 + [pl.BlockSpec(memory_space=pl.ANY)],
        out_specs=VMEM,
        compiler_params=PARAMS,
    )(x, w_other, w, after)


def flip(x):
    toks, feats = x.shape
    step = 256

    return pl.pallas_call(
        lambda x_ref, o_ref: o_ref.__setitem__(..., x_ref[...].T),
        out_shape=jax.ShapeDtypeStruct((feats, toks), x.dtype),
        grid=(feats // step,),
        in_specs=[pl.BlockSpec((toks, step), lambda i: (0, i))],
        out_specs=pl.BlockSpec((step, toks), lambda i: (i, 0)),
        compiler_params=PARAMS,
    )(x)


def gate(parts, cotangent, after):
    ny, rows, cols = parts.shape

    def kernel(p_ref, c_ref, _, o_ref):
        y = p_ref[0].astype(f32)
        for j in range(1, ny):
            y += p_ref[j].astype(f32)
        s = jax.nn.sigmoid(y)
        g = (c_ref[...].astype(f32) * s * (1.0 + y * (1.0 - s))).astype(bf16)
        for j in range(ny):
            o_ref[j] = g

    return pl.pallas_call(
        kernel,
        out_shape=jax.ShapeDtypeStruct((ny, rows, cols), bf16),
        in_specs=[VMEM] * 2 + [pl.BlockSpec(memory_space=pl.ANY)],
        out_specs=VMEM,
        compiler_params=PARAMS,
    )(parts, cotangent, after)


def product(xt, grads, first, count, dtype):
    toks, cols = grads.shape
    step = 256

    def kernel(x_ref, g_ref, o_ref):
        for j in range(count // step):
            at = slice(j * step, (j + 1) * step)
            o_ref[at] = jnp.dot(x_ref[at], g_ref[...], preferred_element_type=f32).astype(dtype)

    return pl.pallas_call(
        kernel,
        out_shape=jax.ShapeDtypeStruct((count, cols), dtype),
        grid=(1,),
        in_specs=[
            pl.BlockSpec((count, toks), lambda i: (first // count, 0)),
            pl.BlockSpec((toks, cols), lambda i: (0, 0)),
        ],
        out_specs=pl.BlockSpec((count, cols), lambda i: (0, 0)),
        compiler_params=PARAMS,
    )(xt, grads)


def pick(array, index, axis):
    return lax.dynamic_index_in_dim(array, index, axis, keepdims=False)


def scatter_sum(local):
    total = local
    for axis in reversed(range(len(REP))):
        me = lax.axis_index(REP[axis])
        away = lax.ppermute(pick(total, 1 - me, axis).astype(bf16), REP[axis], SWAP)
        total = pick(total, me, axis).astype(f32) + away.astype(f32)
    return total


def gather(array, axis):
    first = lax.axis_index(REP[axis]) == 0
    other = lax.ppermute(array, REP[axis], SWAP)
    return jnp.stack([jnp.where(first, array, other), jnp.where(first, other, array)], axis)


def update(total, outer, moment, due, rate, count):
    own, cols = total.shape

    def kernel(due_ref, rate_ref, t_ref, o_ref, m_ref, no_ref, nm_ref, half_ref):
        at = due_ref[0]
        no_ref[...] = o_ref[...]
        nm_ref[...] = m_ref[...]
        pseudo = o_ref[at] - t_ref[...] / count
        moment_next = decay_rate * m_ref[at] + pseudo
        outer_next = o_ref[at] - rate_ref[0] * (pseudo + decay_rate * moment_next)
        no_ref[at] = outer_next
        nm_ref[at] = moment_next
        half_ref[...] = outer_next.astype(bf16)

    smem = pl.BlockSpec(memory_space=pltpu.SMEM)
    whole = jax.ShapeDtypeStruct(outer.shape, f32)
    return pl.pallas_call(
        kernel,
        out_shape=[whole, whole, jax.ShapeDtypeStruct((own, cols), bf16)],
        in_specs=[smem, smem, VMEM, VMEM, VMEM],
        out_specs=[VMEM] * 3,
        compiler_params=PARAMS,
    )(due[None], rate[None], total, outer, moment)


def body(tokens, cotangent, inner_weight, fragments, outer_params, momentum, step_index):
    z = lax.axis_index("z")
    rows, width = tokens.shape
    ny = lax.axis_size("y")
    feat, cols = inner_weight.shape[1:]
    w = inner_weight[0]

    outer_round = step_index[0]
    due = outer_round % NFRAG
    rate = base_rate / jnp.sqrt(1.0 + (outer_round // NFRAG).astype(f32))

    nrep = 2 ** len(REP)
    own = feat // nrep
    local = pick(fragments[0], due, 0)
    total = scatter_sum(local.reshape((2,) * len(REP) + (own, cols)))
    new_outer, new_momentum, merged = update(total, outer_params, momentum, due, rate, nrep)

    swap_y = functools.partial(lax.all_to_all, axis_name="y", split_axis=0, concat_axis=0, tiled=True)
    x = swap_y(pack(tokens, z, ny, feat))
    w_other = lax.ppermute(w, "z", SWAP)
    parts = swap_y(project(x, w_other, w, merged))
    xt = flip(x.reshape(ny * rows, 2 * feat))

    for axis in range(len(REP) - 2):
        merged = gather(merged, axis)
    grads = swap_y(gate(parts, cotangent, merged)).reshape(ny * rows, cols)
    for axis in range(len(REP) - 2, len(REP)):
        merged = gather(merged, axis)
    merged = merged.reshape(feat, cols)
    new_fragment = (mix_weight * local.astype(f32) + (1.0 - mix_weight) * merged.astype(f32)).astype(bf16)
    half = feat // 2
    away = [lax.ppermute(product(xt, grads, i * half, half, bf16), "z", SWAP) for i in range(2)]
    home = product(xt, grads, feat, feat, f32)
    weight_grad = (home + jnp.concatenate(away, 0).astype(f32)).astype(bf16)[None]
    return (weight_grad, new_outer, new_momentum, new_fragment[None])


def solution(mesh):
    fine = Mesh(mesh.devices.reshape((2,) * len(REP) + (2, 8)), REP + SHARD)
    both = REP + SHARD
    placed = (
        P(both, None),
        P(both, None),
        P(REP, SHARD, None),
        P(REP, None, SHARD, None),
        P(None, SHARD + REP, None),
        P(None, SHARD + REP, None),
        P(),
    )
    return jax.shard_map(
        body,
        mesh=fine,
        in_specs=placed,
        out_specs=(P(REP, SHARD, None), P(None, SHARD + REP, None), P(None, SHARD + REP, None), P(REP, SHARD, None)),
        check_vma=False,
    )
```

time: 203 us -> 144 us (0.71)
  waiting for transfers between devices: 133 us -> 51.2 us
  starting transfers between devices: 43.1 us -> 70.1 us
  matrix products: 8.55 us -> 0 us
  Pallas kernels: 0 us -> 7.32 us
  local copies, waits for them, and re-layouts: 12.4 us -> 6.89 us
  other arithmetic: 3.4 us -> 5.63 us
    all_to_all x5 -> x3, waiting for transfers between devices: 116 us -> 11.6 us  [the longest x1 10 us: body(): grads = swap_y(gate(parts, cotangent, merged)).reshape(ny * rows, cols)]
    ppermute x1 -> x12, starting transfers between devices: 3.7 us -> 45.7 us  [the longest x5 23.1 us: scatter_sum(): away = lax.ppermute(pick(total, 1 - me, axis).astype(bf16), REP[axis], SWAP)]
    ppermute x1 -> x12, waiting for transfers between devices: 5.41 us -> 39.5 us  [the longest x5 17.9 us: scatter_sum(): away = lax.ppermute(pick(total, 1 - me, axis).astype(bf16), REP[axis], SWAP)]
    all_to_all x5 -> x3, starting transfers between devices: 35.1 us -> 20.1 us  [the longest x1 7.34 us: body(): parts = swap_y(project(x, w_other, w, merged))]
    ppermute x1, waiting for transfers between devices: 11.6 us -> 0.01 us  [body(): w_other = lax.ppermute(w, 'z', SWAP)]
    dot_general x3 -> x0, matrix products: 8.55 us -> none  [the longest x1 2.9 us: body(): home = lax.dot_general(mine, grads, dims, preferred_element_type=f32)]
    pallas_call x0 -> x8, Pallas kernels: none -> 7.32 us  [the longest x1 2.26 us: project(): pl.pallas_call(kernel, out_shape=jax.ShapeDtypeStruct((ny, rows, cols), b...]
    add x0 -> x5, other arithmetic: none -> 3.48 us  [scatter_sum(): total = pick(total, me, axis).astype(f32) + away.astype(f32)]
  transfers between devices with their start and end apart: 7 -> 16, of which waited for: 7 -> 13; matrix products, arithmetic and copies ran while one was open for 4% -> 5% of each run, Pallas kernels for 0% -> 2%
where the time goes in v2:
time: 144 us; the launch traced here: 143 us
  starting transfers between devices  70.1 us (49%)
  waiting for transfers between devices  51.2 us (36%)
  Pallas kernels  7.32 us (5%)
  local copies, waits for them, and re-layouts  6.89 us (5%)
  other arithmetic  5.63 us (4%)
  between operations  1.79 us (1%)
    ppermute x5, starting transfers between devices, scatter_sum(): away = lax.ppermute(pick(total, 1 - me, axis).astype(bf16), REP[axis], SWAP)  23.1 us
    ppermute x5, waiting for transfers between devices, scatter_sum(): away = lax.ppermute(pick(total, 1 - me, axis).astype(bf16), REP[axis], SWAP)  17.9 us
    ppermute x5, waiting for transfers between devices, gather(): other = lax.ppermute(array, REP[axis], SWAP)  17.6 us
    ppermute x5, starting transfers between devices, gather(): other = lax.ppermute(array, REP[axis], SWAP)  16.7 us
    all_to_all x1, waiting for transfers between devices, body(): grads = swap_y(gate(parts, cotangent, merged)).reshape(ny * rows, cols)  10 us
    all_to_all x1, starting transfers between devices, body(): parts = swap_y(project(x, w_other, w, merged))  7.34 us
    all_to_all x1, starting transfers between devices, body(): x = swap_y(pack(tokens, z, ny, feat))  7.1 us
    ppermute x2, starting transfers between devices, body(): lax.ppermute(product(xt, grads, i * half, half, bf16), 'z', SWAP)  5.97 us
  transfers between devices with their start and end apart: 16, of which 13 were waited for; matrix products, arithmetic and copies ran while one was open for 5% of the time, Pallas kernels for 2%

profile of v2, /device:TPU:6, one launch (start us, length us, event | category | flops | bytes accessed | tf_op | source)
XLA Modules:
  0.0 142.9 jit_solution(11545877941892739827)
XLA Ops:
  4.1 7.1 %all-to-all-start = ((bf16[8,128,1024]{2,1,0:T(8,128)(2,1)}), bf16[8,128,1024]{2,1,0:T(8,128)(2,1)S(1)}, u32[]{:S(2)}, u32[]{:S(2)}) async-start(bf16[8,128,1024]{2,1,0:T(8,128)(2,1)} %copy-done.2), calls=%async_computation | async-start | bytes 4194304 | tf_op jit(solution)/shard_map/all_to_all | solution.py:181
  17.8 2.7 %collective-permute-start.2 = (bf16[2,2,2,16,512]{4,3,0,1,2:T(8,128)(2,1)S(1)}, bf16[2,2,2,16,512]{4,3,0,1,2:T(8,128)(2,1)}, u32[]{:S(2)}, u32[]{:S(2)}) collective-permute-start(bf16[2,2,2,16,512]{4,3,0,1,2:T(8,128)(2,1)S(1)} %fusion.3), channel_id=1, source_target_pairs={{0,32},{32,0},{1,33},{33,1},{2,34},{34,2},{3,35},{35,3},{4,36},{36... | collective-permute-start | bytes 393224 | tf_op jit(solution)/shard_map/ppermute | solution.py:127
  20.6 4.8 %collective-permute-done.2 = bf16[2,2,2,16,512]{4,3,0,1,2:T(8,128)(2,1)} collective-permute-done((bf16[2,2,2,16,512]{4,3,0,1,2:T(8,128)(2,1)S(1)}, bf16[2,2,2,16,512]{4,3,0,1,2:T(8,128)(2,1)}, u32[]{:S(2)}, u32[]{:S(2)}) %collective-permute-start.2) | collective-permute-done | bytes 131104 | tf_op jit(solution)/shard_map/ppermute | solution.py:127
  26.3 4.0 %collective-permute-start.3 = (bf16[2,2,16,512]{3,2,0,1:T(8,128)(2,1)S(1)}, bf16[2,2,16,512]{3,2,0,1:T(8,128)(2,1)S(1)}, u32[]{:S(2)}, u32[]{:S(2)}) collective-permute-start(bf16[2,2,16,512]{3,2,0,1:T(8,128)(2,1)S(1)} %fusion.4), channel_id=1, source_target_pairs={{0,64},{64,0},{1,65},{65,1},{2,66},{66,2},{3,67},{67,3},{4,68},{68... | collective-permute-start | bytes 196616 | tf_op jit(solution)/shard_map/ppermute | solution.py:127
  30.4 3.7 %collective-permute-done.3 = bf16[2,2,16,512]{3,2,0,1:T(8,128)(2,1)S(1)} collective-permute-done((bf16[2,2,16,512]{3,2,0,1:T(8,128)(2,1)S(1)}, bf16[2,2,16,512]{3,2,0,1:T(8,128)(2,1)S(1)}, u32[]{:S(2)}, u32[]{:S(2)}) %collective-permute-start.3) | collective-permute-done | bytes 65568 | tf_op jit(solution)/shard_map/ppermute | solution.py:127
  35.5 6.1 %collective-permute-start.4 = (bf16[2,16,512]{2,1,0:T(8,128)(2,1)S(1)}, bf16[2,16,512]{2,1,0:T(8,128)(2,1)S(1)}, u32[]{:S(2)}, u32[]{:S(2)}) collective-permute-start(bf16[2,16,512]{2,1,0:T(8,128)(2,1)S(1)} %fusion.5), channel_id=1, source_target_pairs={{0,128},{128,0},{1,129},{129,1},{2,130},{130,2},{3,131},{131,3},{4... | collective-permute-start | bytes 98312 | tf_op jit(solution)/shard_map/ppermute | solution.py:127
  41.6 4.3 %collective-permute-start = (bf16[512,512]{1,0:T(8,128)(2,1)S(1)}, bf16[512,512]{1,0:T(8,128)(2,1)S(1)}, u32[]{:S(2)}, u32[]{:S(2)}) collective-permute-start(bf16[512,512]{1,0:T(8,128)(2,1)S(1)} %bitcast.70), channel_id=1, source_target_pairs={{0,8},{8,0},{1,9},{9,1},{2,10},{10,2},{3,11},{11,3},{4,12},{12,4},... | collective-permute-start | bytes 1572872 | tf_op jit(solution)/shard_map/ppermute | solution.py:182
  46.8 8.2 %collective-permute-start.5 = (bf16[16,512]{1,0:T(8,128)(2,1)S(1)}, bf16[16,512]{1,0:T(8,128)(2,1)S(1)}, u32[]{:S(2)}, u32[]{:S(2)}) collective-permute-start(bf16[16,512]{1,0:T(8,128)(2,1)S(1)} %fusion.6), channel_id=1, source_target_pairs={{0,256},{256,0},{1,257},{257,1},{2,258},{258,2},{3,259},{259,3},{4... | collective-permute-start | bytes 49160 | tf_op jit(solution)/shard_map/ppermute | solution.py:127
  55.1 7.8 %collective-permute-done.5 = bf16[16,512]{1,0:T(8,128)(2,1)S(1)} collective-permute-done((bf16[16,512]{1,0:T(8,128)(2,1)S(1)}, bf16[16,512]{1,0:T(8,128)(2,1)S(1)}, u32[]{:S(2)}, u32[]{:S(2)}) %collective-permute-start.5) | collective-permute-done | bytes 16416 | tf_op jit(solution)/shard_map/ppermute | solution.py:127
  63.6 2.3 %shard_map.105 = bf16[8,128,512]{2,1,0:T(8,128)(2,1)} custom-call(bf16[8,128,1024]{2,1,0:T(8,128)(2,1)S(1)} %all-to-all-done.x_ref, bf16[512,512]{1,0:T(8,128)(2,1)S(1)} %collective-permute-done.wo_ref, bf16[512,512]{1,0:T(8,128)(2,1)S(1)} %bitcast.71, bf16[16,512]{1,0:T(8,128)(2,1)S(1)} %get-tuple-element.7._), custom_call_target="tpu_custom_call" | custom-call | tf_op jit(solution)/shard_map/pallas_call | solution.py:53
  65.8 7.3 %all-to-all-start.1 = ((bf16[8,128,512]{2,1,0:T(8,128)(2,1)}), bf16[8,128,512]{2,1,0:T(8,128)(2,1)S(1)}, u32[]{:S(2)}, u32[]{:S(2)}) async-start(bf16[8,128,512]{2,1,0:T(8,128)(2,1)} %shard_map.105), calls=%async_computation.1 | async-start | bytes 2097152 | tf_op jit(solution)/shard_map/all_to_all | solution.py:183
  73.2 6.1 %collective-permute-start.6 = (bf16[16,512]{1,0:T(8,128)(2,1)S(1)}, bf16[16,512]{1,0:T(8,128)(2,1)S(1)}, u32[]{:S(2)}, u32[]{:S(2)}) collective-permute-start(bf16[16,512]{1,0:T(8,128)(2,1)S(1)} %get-tuple-element.7._), channel_id=1, source_target_pairs={{0,256},{256,0},{1,257},{257,1},{2,258},{258,2},{3,259},{259,3},{4... | collective-permute-start | bytes 49160 | tf_op jit(solution)/shard_map/ppermute | solution.py:134
  79.3 3.4 %collective-permute-done.6 = bf16[16,512]{1,0:T(8,128)(2,1)S(1)} collective-permute-done((bf16[16,512]{1,0:T(8,128)(2,1)S(1)}, bf16[16,512]{1,0:T(8,128)(2,1)S(1)}, u32[]{:S(2)}, u32[]{:S(2)}) %collective-permute-start.6) | collective-permute-done | bytes 16416 | tf_op jit(solution)/shard_map/ppermute | solution.py:134
  82.7 2.6 %collective-permute-start.7 = (bf16[2,16,512]{2,1,0:T(8,128)(2,1)S(1)}, bf16[2,16,512]{2,1,0:T(8,128)(2,1)S(1)}, u32[]{:S(2)}, u32[]{:S(2)}) collective-permute-start(bf16[2,16,512]{2,1,0:T(8,128)(2,1)S(1)} %pad_maximum_fusion.3), channel_id=1, source_target_pairs={{0,128},{128,0},{1,129},{129,1},{2,130},{130,2},{3,131},{131,3},{4... | collective-permute-start | bytes 98312 | tf_op jit(solution)/shard_map/ppermute | solution.py:134
  85.4 4.2 %collective-permute-done.7 = bf16[2,16,512]{2,1,0:T(8,128)(2,1)S(1)} collective-permute-done((bf16[2,16,512]{2,1,0:T(8,128)(2,1)S(1)}, bf16[2,16,512]{2,1,0:T(8,128)(2,1)S(1)}, u32[]{:S(2)}, u32[]{:S(2)}) %collective-permute-start.7) | collective-permute-done | bytes 32800 | tf_op jit(solution)/shard_map/ppermute | solution.py:134
  89.6 3.3 %collective-permute-start.8 = (bf16[2,2,16,512]{3,2,1,0:T(8,128)(2,1)S(1)}, bf16[2,2,16,512]{3,2,1,0:T(8,128)(2,1)S(1)}, u32[]{:S(2)}, u32[]{:S(2)}) collective-permute-start(bf16[2,2,16,512]{3,2,1,0:T(8,128)(2,1)S(1)} %pad_maximum_fusion.2), channel_id=1, source_target_pairs={{0,64},{64,0},{1,65},{65,1},{2,66},{66,2},{3,67},{67,3},{4,68},{68... | collective-permute-start | bytes 196616 | tf_op jit(solution)/shard_map/ppermute | solution.py:134
  93.0 4.3 %collective-permute-done.8 = bf16[2,2,16,512]{3,2,1,0:T(8,128)(2,1)S(1)} collective-permute-done((bf16[2,2,16,512]{3,2,1,0:T(8,128)(2,1)S(1)}, bf16[2,2,16,512]{3,2,1,0:T(8,128)(2,1)S(1)}, u32[]{:S(2)}, u32[]{:S(2)}) %collective-permute-start.8) | collective-permute-done | bytes 65568 | tf_op jit(solution)/shard_map/ppermute | solution.py:134
  100.1 5.7 %all-to-all-start.2 = ((bf16[8,128,512]{2,1,0:T(8,128)(2,1)}), bf16[8,128,512]{2,1,0:T(8,128)(2,1)S(1)}, u32[]{:S(2)}, u32[]{:S(2)}) async-start(bf16[8,128,512]{2,1,0:T(8,128)(2,1)} %shard_map.106), calls=%async_computation.2 | async-start | bytes 2097152 | tf_op jit(solution)/shard_map/all_to_all | solution.py:188
  105.8 2.7 %collective-permute-start.11 = (bf16[2,2,2,16,512]{4,3,2,1,0:T(8,128)(2,1)S(1)}, bf16[2,2,2,16,512]{4,3,2,1,0:T(8,128)(2,1)S(1)}, u32[]{:S(2)}, u32[]{:S(2)}) collective-permute-start(bf16[2,2,2,16,512]{4,3,2,1,0:T(8,128)(2,1)S(1)} %pad_maximum_fusion.1._), channel_id=1, source_target_pairs={{0,32},{32,0},{1,33},{33,1},{2,34},{34,2},{3,35},{35,3},{4,36},{36... | collective-permute-start | bytes 393224 | tf_op jit(solution)/shard_map/ppermute | solution.py:134
  108.5 4.1 %collective-permute-done.11 = bf16[2,2,2,16,512]{4,3,2,1,0:T(8,128)(2,1)S(1)} collective-permute-done((bf16[2,2,2,16,512]{4,3,2,1,0:T(8,128)(2,1)S(1)}, bf16[2,2,2,16,512]{4,3,2,1,0:T(8,128)(2,1)S(1)}, u32[]{:S(2)}, u32[]{:S(2)}) %collective-permute-start.11) | collective-permute-done | bytes 131104 | tf_op jit(solution)/shard_map/ppermute | solution.py:134
  119.2 10.0 %all-to-all-done.2 = bf16[8,128,512]{2,1,0:T(8,128)(2,1)S(1)} async-done(((bf16[8,128,512]{2,1,0:T(8,128)(2,1)}), bf16[8,128,512]{2,1,0:T(8,128)(2,1)S(1)}, u32[]{:S(2)}, u32[]{:S(2)}) %all-to-all-start.2) | async-done | bytes 1048608 | tf_op jit(solution)/shard_map/all_to_all | solution.py:188
  130.2 2.4 %collective-permute-start.9 = (bf16[256,512]{1,0:T(8,128)(2,1)S(1)}, bf16[256,512]{1,0:T(8,128)(2,1)S(1)}, u32[]{:S(2)}, u32[]{:S(2)}) collective-permute-start(bf16[256,512]{1,0:T(8,128)(2,1)S(1)} %shard_map.108), channel_id=1, source_target_pairs={{0,8},{8,0},{1,9},{9,1},{2,10},{10,2},{3,11},{11,3},{4,12},{12,4},... | collective-permute-start | bytes 786440 | tf_op jit(solution)/shard_map/ppermute | solution.py:194
  132.6 3.6 %collective-permute-start.10 = (bf16[256,512]{1,0:T(8,128)(2,1)S(1)}, bf16[256,512]{1,0:T(8,128)(2,1)S(1)}, u32[]{:S(2)}, u32[]{:S(2)}) collective-permute-start(bf16[256,512]{1,0:T(8,128)(2,1)S(1)} %shard_map.109), channel_id=1, source_target_pairs={{0,8},{8,0},{1,9},{9,1},{2,10},{10,2},{3,11},{11,3},{4,12},{12,4},... | collective-permute-start | bytes 786440 | tf_op jit(solution)/shard_map/ppermute | solution.py:194
  139.1 2.8 %collective-permute-done.10 = bf16[256,512]{1,0:T(8,128)(2,1)S(1)} collective-permute-done((bf16[256,512]{1,0:T(8,128)(2,1)S(1)}, bf16[256,512]{1,0:T(8,128)(2,1)S(1)}, u32[]{:S(2)}, u32[]{:S(2)}) %collective-permute-start.10) | collective-permute-done | bytes 262176 | tf_op jit(solution)/shard_map/ppermute | solution.py:194
  (61 shorter events, 27.5 us)
Async XLA Ops:
  4.1 59.5 %all-to-all-start = ((bf16[8,128,1024]{2,1,0:T(8,128)(2,1)}), bf16[8,128,1024]{2,1,0:T(8,128)(2,1)S(1)}, u32[]{:S(2)}, u32[]{:S(2)}) async-start(bf16[8,128,1024]{2,1,0:T(8,128)(2,1)} %copy-done.2), calls=%async_computation | async-start | bytes 4194304 | tf_op jit(solution)/shard_map/all_to_all | solution.py:181
  13.0 28.6 %copy-start.4 = (bf16[1,512,512]{2,1,0:T(8,128)(2,1)S(1)}, bf16[1,512,512]{2,1,0:T(8,128)(2,1)}, u32[]{:S(2)}) copy-start(bf16[1,512,512]{2,1,0:T(8,128)(2,1)} %param.9) | copy-start | bytes 1572868
  13.0 49.9 %copy-start.6 = (f32[2,16,512]{2,1,0:T(8,128)S(1)}, f32[2,16,512]{2,1,0:T(8,128)}, u32[]{:S(2)}) copy-start(f32[2,16,512]{2,1,0:T(8,128)} %o_ref.1) | copy-start | bytes 196612
  13.0 49.9 %copy-start.7 = (f32[2,16,512]{2,1,0:T(8,128)S(1)}, f32[2,16,512]{2,1,0:T(8,128)}, u32[]{:S(2)}) copy-start(f32[2,16,512]{2,1,0:T(8,128)} %m_ref.1) | copy-start | bytes 196612
  13.1 3.7 %collective-permute-start.1 = (bf16[2,2,2,2,16,512]{5,4,0,1,2,3:T(8,128)(2,1)S(1)}, bf16[2,2,2,2,16,512]{5,4,0,1,2,3:T(8,128)(2,1)}, u32[]{:S(2)}, u32[]{:S(2)}) collective-permute-start(bf16[2,2,2,2,16,512]{5,4,0,1,2,3:T(8,128)(2,1)S(1)} %bitcast.74), channel_id=1, source_target_pairs={{0,16},{16,0},{1,17},{17,1},{2,18},{18,2},{3,19},{19,3},{4,20},{20... | collective-permute-start | bytes 786440 | tf_op jit(solution)/shard_map/ppermute | solution.py:127
  17.8 7.5 %collective-permute-start.2 = (bf16[2,2,2,16,512]{4,3,0,1,2:T(8,128)(2,1)S(1)}, bf16[2,2,2,16,512]{4,3,0,1,2:T(8,128)(2,1)}, u32[]{:S(2)}, u32[]{:S(2)}) collective-permute-start(bf16[2,2,2,16,512]{4,3,0,1,2:T(8,128)(2,1)S(1)} %fusion.3), channel_id=1, source_target_pairs={{0,32},{32,0},{1,33},{33,1},{2,34},{34,2},{3,35},{35,3},{4,36},{36... | collective-permute-start | bytes 393224 | tf_op jit(solution)/shard_map/ppermute | solution.py:127
  26.3 7.7 %collective-permute-start.3 = (bf16[2,2,16,512]{3,2,0,1:T(8,128)(2,1)S(1)}, bf16[2,2,16,512]{3,2,0,1:T(8,128)(2,1)S(1)}, u32[]{:S(2)}, u32[]{:S(2)}) collective-permute-start(bf16[2,2,16,512]{3,2,0,1:T(8,128)(2,1)S(1)} %fusion.4), channel_id=1, source_target_pairs={{0,64},{64,0},{1,65},{65,1},{2,66},{66,2},{3,67},{67,3},{4,68},{68... | collective-permute-start | bytes 196616 | tf_op jit(solution)/shard_map/ppermute | solution.py:127
  35.5 10.4 %collective-permute-start.4 = (bf16[2,16,512]{2,1,0:T(8,128)(2,1)S(1)}, bf16[2,16,512]{2,1,0:T(8,128)(2,1)S(1)}, u32[]{:S(2)}, u32[]{:S(2)}) collective-permute-start(bf16[2,16,512]{2,1,0:T(8,128)(2,1)S(1)} %fusion.5), channel_id=1, source_target_pairs={{0,128},{128,0},{1,129},{129,1},{2,130},{130,2},{3,131},{131,3},{4... | collective-permute-start | bytes 98312 | tf_op jit(solution)/shard_map/ppermute | solution.py:127
  41.6 22.0 %collective-permute-start = (bf16[512,512]{1,0:T(8,128)(2,1)S(1)}, bf16[512,512]{1,0:T(8,128)(2,1)S(1)}, u32[]{:S(2)}, u32[]{:S(2)}) collective-permute-start(bf16[512,512]{1,0:T(8,128)(2,1)S(1)} %bitcast.70), channel_id=1, source_target_pairs={{0,8},{8,0},{1,9},{9,1},{2,10},{10,2},{3,11},{11,3},{4,12},{12,4},... | collective-permute-start | bytes 1572872 | tf_op jit(solution)/shard_map/ppermute | solution.py:182
  46.8 16.1 %collective-permute-start.5 = (bf16[16,512]{1,0:T(8,128)(2,1)S(1)}, bf16[16,512]{1,0:T(8,128)(2,1)S(1)}, u32[]{:S(2)}, u32[]{:S(2)}) collective-permute-start(bf16[16,512]{1,0:T(8,128)(2,1)S(1)} %fusion.6), channel_id=1, source_target_pairs={{0,256},{256,0},{1,257},{257,1},{2,258},{258,2},{3,259},{259,3},{4... | collective-permute-start | bytes 49160 | tf_op jit(solution)/shard_map/ppermute | solution.py:127
  63.6 2.3 %copy-start = (bf16[8,128,1024]{2,1,0:T(8,128)(2,1)}, bf16[8,128,1024]{2,1,0:T(8,128)(2,1)S(1)}, u32[]{:S(2)}) copy-start(bf16[8,128,1024]{2,1,0:T(8,128)(2,1)S(1)} %all-to-all-done.x_ref) | copy-start | bytes 6291460
  65.8 33.1 %copy-start.5 = (bf16[128,512]{1,0:T(8,128)(2,1)S(1)}, bf16[128,512]{1,0:T(8,128)(2,1)}, u32[]{:S(2)}) copy-start(bf16[128,512]{1,0:T(8,128)(2,1)} %c_ref.1) | copy-start | bytes 393220
  65.8 33.1 %all-to-all-start.1 = ((bf16[8,128,512]{2,1,0:T(8,128)(2,1)}), bf16[8,128,512]{2,1,0:T(8,128)(2,1)S(1)}, u32[]{:S(2)}, u32[]{:S(2)}) async-start(bf16[8,128,512]{2,1,0:T(8,128)(2,1)} %shard_map.105), calls=%async_computation.1 | async-start | bytes 2097152 | tf_op jit(solution)/shard_map/all_to_all | solution.py:183
  73.2 9.5 %collective-permute-start.6 = (bf16[16,512]{1,0:T(8,128)(2,1)S(1)}, bf16[16,512]{1,0:T(8,128)(2,1)S(1)}, u32[]{:S(2)}, u32[]{:S(2)}) collective-permute-start(bf16[16,512]{1,0:T(8,128)(2,1)S(1)} %get-tuple-element.7._), channel_id=1, source_target_pairs={{0,256},{256,0},{1,257},{257,1},{2,258},{258,2},{3,259},{259,3},{4... | collective-permute-start | bytes 49160 | tf_op jit(solution)/shard_map/ppermute | solution.py:134
  82.7 6.9 %collective-permute-start.7 = (bf16[2,16,512]{2,1,0:T(8,128)(2,1)S(1)}, bf16[2,16,512]{2,1,0:T(8,128)(2,1)S(1)}, u32[]{:S(2)}, u32[]{:S(2)}) collective-permute-start(bf16[2,16,512]{2,1,0:T(8,128)(2,1)S(1)} %pad_maximum_fusion.3), channel_id=1, source_target_pairs={{0,128},{128,0},{1,129},{129,1},{2,130},{130,2},{3,131},{131,3},{4... | collective-permute-start | bytes 98312 | tf_op jit(solution)/shard_map/ppermute | solution.py:134
  89.6 7.7 %collective-permute-start.8 = (bf16[2,2,16,512]{3,2,1,0:T(8,128)(2,1)S(1)}, bf16[2,2,16,512]{3,2,1,0:T(8,128)(2,1)S(1)}, u32[]{:S(2)}, u32[]{:S(2)}) collective-permute-start(bf16[2,2,16,512]{3,2,1,0:T(8,128)(2,1)S(1)} %pad_maximum_fusion.2), channel_id=1, source_target_pairs={{0,64},{64,0},{1,65},{65,1},{2,66},{66,2},{3,67},{67,3},{4,68},{68... | collective-permute-start | bytes 196616 | tf_op jit(solution)/shard_map/ppermute | solution.py:134
  100.1 29.2 %all-to-all-start.2 = ((bf16[8,128,512]{2,1,0:T(8,128)(2,1)}), bf16[8,128,512]{2,1,0:T(8,128)(2,1)S(1)}, u32[]{:S(2)}, u32[]{:S(2)}) async-start(bf16[8,128,512]{2,1,0:T(8,128)(2,1)} %shard_map.106), calls=%async_computation.2 | async-start | bytes 2097152 | tf_op jit(solution)/shard_map/all_to_all | solution.py:188
  105.8 6.8 %collective-permute-start.11 = (bf16[2,2,2,16,512]{4,3,2,1,0:T(8,128)(2,1)S(1)}, bf16[2,2,2,16,512]{4,3,2,1,0:T(8,128)(2,1)S(1)}, u32[]{:S(2)}, u32[]{:S(2)}) collective-permute-start(bf16[2,2,2,16,512]{4,3,2,1,0:T(8,128)(2,1)S(1)} %pad_maximum_fusion.1._), channel_id=1, source_target_pairs={{0,32},{32,0},{1,33},{33,1},{2,34},{34,2},{3,35},{35,3},{4,36},{36... | collective-permute-start | bytes 393224 | tf_op jit(solution)/shard_map/ppermute | solution.py:134
  112.7 3.4 %collective-permute-start.12 = (bf16[2,2,2,2,16,512]{5,4,2,1,0,3:T(8,128)(2,1)S(1)}, bf16[2,2,2,2,16,512]{5,4,2,1,0,3:T(8,128)(2,1)S(1)}, u32[]{:S(2)}, u32[]{:S(2)}) collective-permute-start(bf16[2,2,2,2,16,512]{5,4,2,1,0,3:T(8,128)(2,1)S(1)} %pad_maximum_fusion), channel_id=1, source_target_pairs={{0,16},{16,0},{1,17},{17,1},{2,18},{18,2},{3,19},{19,3},{4,20},{20... | collective-permute-start | bytes 786440 | tf_op jit(solution)/shard_map/ppermute | solution.py:134
  116.2 2.0 %copy-start.1 = (bf16[8,128,1024]{2,1,0:T(8,128)(2,1)S(1)}, bf16[8,128,1024]{2,1,0:T(8,128)(2,1)}, u32[]{:S(2)}) copy-start(bf16[8,128,1024]{2,1,0:T(8,128)(2,1)} %copy-done) | copy-start | bytes 6291460
  129.7 6.5 %copy-start.8 = (f32[2,2,2,2,2,16,512]{6,5,4,3,2,1,0:T(8,128)S(1)}, f32[2,2,2,2,2,16,512]{6,5,4,3,2,1,0:T(8,128)}, u32[]{:S(2)}) copy-start(f32[2,2,2,2,2,16,512]{6,5,4,3,2,1,0:T(8,128)} %copy.17) | copy-start | bytes 3145732
  129.7 6.5 %copy-start.9 = (bf16[1,2,512,512]{3,2,1,0:T(8,128)(2,1)S(1)}, bf16[1,2,512,512]{3,2,1,0:T(8,128)(2,1)}, u32[]{:S(2)}) copy-start(bf16[1,2,512,512]{3,2,1,0:T(8,128)(2,1)} %param.10) | copy-start | bytes 3145732
  130.2 8.9 %collective-permute-start.9 = (bf16[256,512]{1,0:T(8,128)(2,1)S(1)}, bf16[256,512]{1,0:T(8,128)(2,1)S(1)}, u32[]{:S(2)}, u32[]{:S(2)}) collective-permute-start(bf16[256,512]{1,0:T(8,128)(2,1)S(1)} %shard_map.108), channel_id=1, source_target_pairs={{0,8},{8,0},{1,9},{9,1},{2,10},{10,2},{3,11},{11,3},{4,12},{12,4},... | collective-permute-start | bytes 786440 | tf_op jit(solution)/shard_map/ppermute | solution.py:194
  132.6 9.3 %collective-permute-start.10 = (bf16[256,512]{1,0:T(8,128)(2,1)S(1)}, bf16[256,512]{1,0:T(8,128)(2,1)S(1)}, u32[]{:S(2)}, u32[]{:S(2)}) collective-permute-start(bf16[256,512]{1,0:T(8,128)(2,1)S(1)} %shard_map.109), channel_id=1, source_target_pairs={{0,8},{8,0},{1,9},{9,1},{2,10},{10,2},{3,11},{11,3},{4,12},{12,4},... | collective-permute-start | bytes 786440 | tf_op jit(solution)/shard_map/ppermute | solution.py:194
  (2 other events, 2.9 us)

commit v3 on v2

v3 whole, which is shorter than its diff:
```python
import jax
import jax.numpy as jnp
from jax import lax
from jax.experimental import pallas as pl
from jax.experimental.pallas import tpu as pltpu
from jax.sharding import Mesh
from jax.sharding import PartitionSpec as P

NFRAG = 2
base_rate = 0.7
decay_rate = 0.9
mix_weight = 0.5
REP = ("zh", "x", "c")
SHARD = ("z", "y")
CHIPS = ("c", "z", "y")
SWAP = [(0, 1), (1, 0)]
NZ, NY = 2, 8
LINE, SHIFT = 4, 2
GROUP = NZ * LINE
f32, bf16 = jnp.float32, jnp.bfloat16
VMEM = pl.BlockSpec(memory_space=pltpu.VMEM)
HBM = pl.BlockSpec(memory_space=pltpu.HBM)
ANY = pl.BlockSpec(memory_space=pl.ANY)
PARAMS = pltpu.CompilerParams(vmem_limit_bytes=8 * 2**20)
BIG = pltpu.CompilerParams(vmem_limit_bytes=60 * 2**20)


def place(core, y):
    turned = (y - SHIFT * core) % NY
    return turned // LINE, turned % LINE


def rank(core, z, turned):
    return (core * NZ + z) * NY + (turned + SHIFT * core) % NY


LINES = [
    [rank(core, z, half * LINE + p) for z in range(NZ) for p in range(LINE)]
    for core in range(2)
    for half in range(NY // LINE)
]
MIRROR = [
    (rank(core, z, t), rank(core, z, NY - 1 - t)) for core in range(2) for z in range(NZ) for t in range(NY)
]


def swap_line(array):
    return lax.all_to_all(
        array, CHIPS, split_axis=0, concat_axis=0, axis_index_groups=LINES, tiled=True
    )


def mirror(array):
    return lax.ppermute(array, CHIPS, MIRROR)


def pack(tokens, core, y, feat):
    rows = tokens.shape[0]

    def kernel(core_ref, y_ref, t_ref, o_ref, held, in_sems, out_sems):
        half, _ = place(core_ref[0], y_ref[0])
        loads, stores = [], []
        for j in range(GROUP):
            turned = half * LINE + j % LINE
            for k, at in enumerate((NY - 1 - turned, turned)):
                block = (j // LINE) * NY + (at + SHIFT * core_ref[0]) % NY
                cols = pl.ds(pl.multiple_of(block * feat, feat), feat)
                loads.append(
                    pltpu.make_async_copy(
                        t_ref.at[:, cols], held.at[j, :, pl.ds(k * feat, feat)], in_sems.at[j, k]
                    )
                )
            stores.append(pltpu.make_async_copy(held.at[j], o_ref.at[j], out_sems.at[j]))
        for load in loads:
            load.start()
        for j in range(GROUP):
            loads[2 * j].wait()
            loads[2 * j + 1].wait()
            stores[j].start()
        for store in stores:
            store.wait()

    smem = pl.BlockSpec(memory_space=pltpu.SMEM)
    shape = (GROUP, rows, 2 * feat)
    return pl.pallas_call(
        kernel,
        out_shape=jax.ShapeDtypeStruct(shape, tokens.dtype),
        in_specs=[smem, smem, ANY],
        out_specs=ANY,
        scratch_shapes=[
            pltpu.VMEM(shape, tokens.dtype),
            pltpu.SemaphoreType.DMA((GROUP, 2)),
            pltpu.SemaphoreType.DMA((GROUP,)),
        ],
        compiler_params=BIG,
    )(core[None], y[None], tokens)


def project(x, w_other, w, after):
    n, rows, feat2 = x.shape
    feat, cols = w.shape

    def kernel(x_ref, wo_ref, w_ref, _, o_ref, buf, sems):
        copies = []
        for j in range(n):
            acc = jnp.dot(x_ref[j, :, :feat], wo_ref[...], preferred_element_type=f32)
            acc += jnp.dot(x_ref[j, :, feat:], w_ref[...], preferred_element_type=f32)
            buf[j] = acc.astype(bf16)
            copies.append(pltpu.make_async_copy(buf.at[j], o_ref.at[j], sems.at[j]))
            copies[j].start()
        for copy in copies:
            copy.wait()

    return pl.pallas_call(
        kernel,
        out_shape=jax.ShapeDtypeStruct((n, rows, cols), bf16),
        in_specs=[VMEM] * 3 + [ANY],
        out_specs=HBM,
        scratch_shapes=[pltpu.VMEM((n, rows, cols), bf16), pltpu.SemaphoreType.DMA((n,))],
        compiler_params=PARAMS,
    )(x, w_other, w, after)


def flip(x):
    toks, feats = x.shape
    step = 256

    return pl.pallas_call(
        lambda x_ref, o_ref: o_ref.__setitem__(..., x_ref[...].T),
        out_shape=jax.ShapeDtypeStruct((feats, toks), x.dtype),
        grid=(feats // step,),
        in_specs=[pl.BlockSpec((toks, step), lambda i: (0, i))],
        out_specs=pl.BlockSpec((step, toks), lambda i: (i, 0)),
        compiler_params=PARAMS,
    )(x)


def gate(parts, cotangent, after):
    n, rows, cols = parts.shape

    def kernel(p_ref, c_ref, _, o_ref, buf, sems):
        y = p_ref[0].astype(f32)
        for j in range(1, n):
            y += p_ref[j].astype(f32)
        s = jax.nn.sigmoid(y)
        buf[...] = (c_ref[...].astype(f32) * s * (1.0 + y * (1.0 - s))).astype(bf16)
        copies = [pltpu.make_async_copy(buf, o_ref.at[j], sems.at[j]) for j in range(n)]
        for copy in copies:
            copy.start()
        for copy in copies:
            copy.wait()

    return pl.pallas_call(
        kernel,
        out_shape=jax.ShapeDtypeStruct((n, rows, cols), bf16),
        in_specs=[VMEM] * 2 + [ANY],
        out_specs=HBM,
        scratch_shapes=[pltpu.VMEM((rows, cols), bf16), pltpu.SemaphoreType.DMA((n,))],
        compiler_params=PARAMS,
    )(parts, cotangent, after)


def product(xt, grads, first, count, dtype):
    toks, cols = grads.shape
    step = 256

    def kernel(x_ref, g_ref, o_ref):
        for j in range(count // step):
            at = slice(j * step, (j + 1) * step)
            o_ref[at] = jnp.dot(x_ref[at], g_ref[...], preferred_element_type=f32).astype(dtype)

    return pl.pallas_call(
        kernel,
        out_shape=jax.ShapeDtypeStruct((count, cols), dtype),
        grid=(1,),
        in_specs=[
            pl.BlockSpec((count, toks), lambda i: (first // count, 0)),
            pl.BlockSpec((toks, cols), lambda i: (0, 0)),
        ],
        out_specs=pl.BlockSpec((count, cols), lambda i: (0, 0)),
        compiler_params=PARAMS,
    )(xt, grads)


def call(kernel, out, ins, scalars=()):
    specs = [pl.BlockSpec(memory_space=pltpu.SMEM)] * len(scalars)
    specs += [ANY if isinstance(array, tuple) else VMEM for array in ins]
    return pl.pallas_call(
        kernel,
        out_shape=[jax.ShapeDtypeStruct(shape, dtype) for shape, dtype in out],
        in_specs=specs,
        out_specs=[VMEM] * len(out),
        compiler_params=PARAMS,
    )(*[s[None] for s in scalars], *[array[0] if isinstance(array, tuple) else array for array in ins])


def shifts(arrays, name):
    n = len(arrays) + 1
    return [
        lax.ppermute(array, name, [(i, (i + k) % n) for i in range(n)]) for k, array in enumerate(arrays, 1)
    ]


def first_terms(fragments, due, core):
    nz, nx, nc, own, cols = fragments.shape[1:]

    def kernel(due_ref, core_ref, f_ref, o_ref):
        for i in range(nz):
            for j in range(nx):
                o_ref[i, j] = f_ref[due_ref[0], i, j, 1 - core_ref[0]]

    return call(kernel, [((nz, nx, own, cols), bf16)], [fragments], [due, core])[0]


def x_terms(fragments, away, due, core, x):
    nz, nx, nc, own, cols = fragments.shape[1:]

    def kernel(due_ref, core_ref, x_ref, f_ref, a_ref, *outs):
        for k in range(nx):
            at = (x_ref[0] + k) % nx
            for i in range(nz):
                term = f_ref[due_ref[0], i, at, core_ref[0]].astype(f32) + a_ref[i, at].astype(f32)
                outs[k][i] = term.astype(outs[k].dtype)

    out = [((nz, own, cols), f32)] + [((nz, own, cols), bf16)] * (nx - 1)
    return call(kernel, out, [fragments, away], [due, core, x])


def z_terms(mine, away, z):
    nz, own, cols = mine.shape

    def kernel(z_ref, m_ref, *refs):
        ins, outs = refs[: len(away)], refs[len(away) :]
        for k in range(nz):
            at = (z_ref[0] + k) % nz
            term = m_ref[at]
            for ref in ins:
                term += ref[at].astype(f32)
            outs[k][...] = term.astype(outs[k].dtype)

    out = [((own, cols), f32)] + [((own, cols), bf16)] * (nz - 1)
    return call(kernel, out, [mine, *away], [z])


def update(mine, away, outer, moment, due, rate, count):
    own, cols = mine.shape

    def kernel(due_ref, rate_ref, t_ref, *refs):
        ins = refs[: len(away)]
        o_ref, m_ref, no_ref, nm_ref, half_ref = refs[len(away) :]
        at = due_ref[0]
        no_ref[...] = o_ref[...]
        nm_ref[...] = m_ref[...]
        total = t_ref[...]
        for ref in ins:
            total += ref[...].astype(f32)
        pseudo = o_ref[at] - total / count
        moment_next = decay_rate * m_ref[at] + pseudo
        outer_next = o_ref[at] - rate_ref[0] * (pseudo + decay_rate * moment_next)
        no_ref[at] = outer_next
        nm_ref[at] = moment_next
        half_ref[...] = outer_next.astype(bf16)

    out = [(outer.shape, f32), (outer.shape, f32), ((own, cols), bf16)]
    return call(kernel, out, [mine, *away, outer, moment], [due, rate])


def z_rows(mine, away, z):
    own, cols = mine.shape
    n = len(away) + 1

    def kernel(z_ref, *refs):
        for k in range(n):
            refs[n][(z_ref[0] + n - k) % n] = refs[k][...]

    return call(kernel, [((n, own, cols), bf16)], [mine, *away], [z])[0]


def x_rows(mine, away, x):
    nz, own, cols = mine.shape
    n = len(away) + 1

    def kernel(x_ref, *refs):
        for k in range(n):
            at = (x_ref[0] + n - k) % n
            for i in range(nz):
                refs[n][i, at] = refs[k][i]

    return call(kernel, [((nz, n, own, cols), bf16)], [mine, *away], [x])[0]


def merge(fragments, mine, away, due, core):
    nz, nx, nc, own, cols = fragments.shape[1:]

    def kernel(due_ref, core_ref, f_ref, m_ref, a_ref, o_ref):
        for i in range(nz):
            for j in range(nx):
                for ref, c in ((m_ref, core_ref[0]), (a_ref, 1 - core_ref[0])):
                    local = f_ref[due_ref[0], i, j, c].astype(f32)
                    mixed = mix_weight * local + (1.0 - mix_weight) * ref[i, j].astype(f32)
                    o_ref[i, j, c] = mixed.astype(bf16)

    return call(kernel, [((nz, nx, nc, own, cols), bf16)], [fragments, mine, away], [due, core])[0]


def body(tokens, cotangent, inner_weight, fragments, outer_params, momentum, step_index):
    rows = tokens.shape[0]
    feat, cols = inner_weight.shape[1:]
    w = inner_weight[0]
    zh, xx, core = (lax.axis_index(name) for name in REP)

    outer_round = step_index[0]
    due = outer_round % NFRAG
    rate = base_rate / jnp.sqrt(1.0 + (outer_round // NFRAG).astype(f32))

    x = swap_line(pack(tokens, core, lax.axis_index("y"), feat))
    w_other = mirror(w)

    sizes = tuple(lax.axis_size(name) for name in REP)
    nrep = sizes[0] * sizes[1] * sizes[2]
    local = fragments.reshape((NFRAG, *sizes, feat // nrep, cols))
    away = lax.ppermute(first_terms(local, due, core), "c", SWAP)
    mine, *sent = x_terms(local, away, due, core, xx)
    mine, *sent = z_terms(mine, shifts(sent, "x"), zh)
    new_outer, new_momentum, half = update(mine, shifts(sent, "zh"), outer_params, momentum, due, rate, nrep)

    parts = swap_line(project(x, w_other, w, half))
    line = z_rows(half, shifts([half] * 3, "zh"), zh)
    grads = swap_line(gate(parts, cotangent, line)).reshape(GROUP * rows, cols)
    plane = x_rows(line, shifts([line] * 3, "x"), xx)
    xt = flip(x.reshape(GROUP * rows, 2 * feat))
    piece = feat // 2
    away = [mirror(product(xt, grads, i * piece, piece, bf16)) for i in range(2)]
    new_fragment = merge(local, plane, lax.ppermute(plane, "c", SWAP), due, core)
    home = product(xt, grads, feat, feat, f32)
    weight_grad = (home + jnp.concatenate(away, 0).astype(f32)).astype(bf16)[None]
    return (weight_grad, new_outer, new_momentum, new_fragment.reshape(1, feat, cols))


def solution(mesh):
    fine = Mesh(mesh.devices.reshape(4, 4, 2, NZ, NY), REP + SHARD)
    both = REP + SHARD
    placed = (
        P(both, None),
        P(both, None),
        P(REP, SHARD, None),
        P(REP, None, SHARD, None),
        P(None, SHARD + REP, None),
        P(None, SHARD + REP, None),
        P(),
    )
    return jax.shard_map(
        body,
        mesh=fine,
        in_specs=placed,
        out_specs=(P(REP, SHARD, None), P(None, SHARD + REP, None), P(None, SHARD + REP, None), P(REP, SHARD, None)),
        check_vma=False,
    )
```

time: 144 us -> 140 us (0.972)
  waiting for transfers between devices: 51.2 us -> 30.9 us
  starting transfers between devices: 70.1 us -> 85.6 us
  Pallas kernels: 7.32 us -> 13.7 us
  other arithmetic: 5.63 us -> 0.95 us
  local copies, waits for them, and re-layouts: 6.89 us -> 4.68 us
    ppermute x13 -> x17, starting transfers between devices: 50 us -> 70.9 us  [the longest x12 53.8 us: shifts(): lax.ppermute(array, name, [(i, (i + k) % n) for i in range(n)])]
    ppermute x13 -> x17, waiting for transfers between devices: 39.5 us -> 24.9 us  [the longest x12 15.2 us: shifts(): lax.ppermute(array, name, [(i, (i + k) % n) for i in range(n)])]
    pallas_call x4 -> x10, Pallas kernels: 4.65 us -> 11 us  [the longest x7 4.09 us: call(): pl.pallas_call(kernel, out_shape=[jax.ShapeDtypeStruct(shape, dtype) for...]
    all_to_all x3, waiting for transfers between devices: 11.6 us -> 6.04 us  [swap_line(): lax.all_to_all(array, CHIPS, split_axis=0, concat_axis=0, axis_index_grou...]
    all_to_all x3, starting transfers between devices: 20.1 us -> 14.7 us  [swap_line(): lax.all_to_all(array, CHIPS, split_axis=0, concat_axis=0, axis_index_grou...]
    add x5 -> x0, other arithmetic: 3.48 us -> none  [scatter_sum(): total = pick(total, me, axis).astype(f32) + away.astype(f32)]
    convert_element_type x5 -> x0, local copies, waits for them, and re-layouts: 1.99 us -> none  [the longest x1 1.09 us: body(): merged.astype(f32)]
    unnamed x20 -> x16, local copies, waits for them, and re-layouts: 3.75 us -> 4.68 us
  transfers between devices with their start and end apart: 16 -> 20, of which waited for: 13 -> 11; matrix products, arithmetic and copies ran while one was open for 5% -> 0% of each run, Pallas kernels for 2% -> 5%
where the time goes in v3:
time: 140 us; the launch traced here: 137 us
  starting transfers between devices  85.6 us (61%)
  waiting for transfers between devices  30.9 us (22%)
  Pallas kernels  13.7 us (10%)
  local copies, waits for them, and re-layouts  4.68 us (3%)
  between operations  1.71 us (1%)
    ppermute x12, starting transfers between devices, shifts(): lax.ppermute(array, name, [(i, (i + k) % n) for i in range(n)])  53.8 us
    ppermute x12, waiting for transfers between devices, shifts(): lax.ppermute(array, name, [(i, (i + k) % n) for i in range(n)])  15.2 us
    all_to_all x3, starting transfers between devices, swap_line(): lax.all_to_all(array, CHIPS, split_axis=0, concat_axis=0, axis_index_grou...  14.7 us
    ppermute x3, starting transfers between devices, mirror(): return lax.ppermute(array, CHIPS, MIRROR)  12.6 us
    ppermute x3, waiting for transfers between devices, mirror(): return lax.ppermute(array, CHIPS, MIRROR)  8.01 us
    all_to_all x3, waiting for transfers between devices, swap_line(): lax.all_to_all(array, CHIPS, split_axis=0, concat_axis=0, axis_index_grou...  6.04 us
    unnamed x16, local copies, waits for them, and re-layouts  4.68 us
    pallas_call x7, Pallas kernels, call(): pl.pallas_call(kernel, out_shape=[jax.ShapeDtypeStruct(shape, dtype) for...  4.09 us
  transfers between devices with their start and end apart: 20, of which 11 were waited for; matrix products, arithmetic and copies ran while one was open for 0% of the time, Pallas kernels for 5%

profile of v3, /device:TPU:6, one launch (start us, length us, event | category | flops | bytes accessed | tf_op | source)
XLA Modules:
  0.0 137.5 jit_solution(11400160664199562153)
XLA Ops:
  0.6 2.6 %shard_map.102 = bf16[8,128,1024]{2,1,0:T(8,128)(2,1)} custom-call(s32[1]{0:T(128)} %bitcast.core_ref, s32[1]{0:T(128)} %bitcast.1.y_ref, bf16[128,8192]{1,0:T(8,128)(2,1)} %t_ref.1), custom_call_target="tpu_custom_call" | custom-call | tf_op jit(solution)/shard_map/pallas_call | solution.py:85
  3.3 6.8 %all-to-all-start = ((bf16[8,128,1024]{2,1,0:T(8,128)(2,1)}), bf16[8,128,1024]{2,1,0:T(8,128)(2,1)S(1)}, u32[]{:S(2)}, u32[]{:S(2)}) async-start(bf16[8,128,1024]{2,1,0:T(8,128)(2,1)} %shard_map.102), calls=%async_computation | async-start | bytes 4194304 | tf_op jit(solution)/shard_map/all_to_all | solution.py:48
  10.1 5.6 %collective-permute-start = (bf16[512,512]{1,0:T(8,128)(2,1)}, bf16[512,512]{1,0:T(8,128)(2,1)}, u32[]{:S(2)}, u32[]{:S(2)}) collective-permute-start(bf16[512,512]{1,0:T(8,128)(2,1)} %bitcast.25), channel_id=1, source_target_pairs={{0,7},{1,6},{2,5},{3,4},{4,3},{5,2},{6,1},{7,0},{8,15},{9,14},{10,... | collective-permute-start | bytes 1572872 | tf_op jit(solution)/shard_map/ppermute | solution.py:54
  21.4 2.4 %collective-permute-start.2 = (bf16[4,16,512]{2,1,0:T(8,128)(2,1)}, bf16[4,16,512]{2,1,0:T(8,128)(2,1)S(1)}, u32[]{:S(2)}, u32[]{:S(2)}) collective-permute-start(bf16[4,16,512]{2,1,0:T(8,128)(2,1)} %get-tuple-element.16), channel_id=1, source_target_pairs={{0,32},{32,64},{64,96},{96,0},{1,33},{33,65},{65,97},{97,1},{2,34}... | collective-permute-start | bytes 196616 | tf_op jit(solution)/shard_map/ppermute | solution.py:200
  23.8 4.3 %collective-permute-start.3 = (bf16[4,16,512]{2,1,0:T(8,128)(2,1)}, bf16[4,16,512]{2,1,0:T(8,128)(2,1)S(1)}, u32[]{:S(2)}, u32[]{:S(2)}) collective-permute-start(bf16[4,16,512]{2,1,0:T(8,128)(2,1)} %get-tuple-element.17), channel_id=1, source_target_pairs={{0,64},{32,96},{64,0},{96,32},{1,65},{33,97},{65,1},{97,33},{2,66}... | collective-permute-start | bytes 196616 | tf_op jit(solution)/shard_map/ppermute | solution.py:200
  31.7 4.0 %collective-permute-done.4.refs_2_ = bf16[4,16,512]{2,1,0:T(8,128)(2,1)S(1)} collective-permute-done((bf16[4,16,512]{2,1,0:T(8,128)(2,1)}, bf16[4,16,512]{2,1,0:T(8,128)(2,1)S(1)}, u32[]{:S(2)}, u32[]{:S(2)}) %collective-permute-start.4) | collective-permute-done | bytes 65568 | tf_op jit(solution)/shard_map/ppermute | solution.py:200
  35.8 6.1 %collective-permute-start.5 = (bf16[16,512]{1,0:T(8,128)(2,1)S(1)}, bf16[16,512]{1,0:T(8,128)(2,1)S(1)}, u32[]{:S(2)}, u32[]{:S(2)}) collective-permute-start(bf16[16,512]{1,0:T(8,128)(2,1)S(1)} %get-tuple-element.20), channel_id=1, source_target_pairs={{0,128},{128,256},{256,384},{384,0},{1,129},{129,257},{257,385},{3... | collective-permute-start | bytes 49160 | tf_op jit(solution)/shard_map/ppermute | solution.py:200
  41.9 8.7 %collective-permute-start.6 = (bf16[16,512]{1,0:T(8,128)(2,1)S(1)}, bf16[16,512]{1,0:T(8,128)(2,1)S(1)}, u32[]{:S(2)}, u32[]{:S(2)}) collective-permute-start(bf16[16,512]{1,0:T(8,128)(2,1)S(1)} %get-tuple-element.21), channel_id=1, source_target_pairs={{0,256},{128,384},{256,0},{384,128},{1,257},{129,385},{257,1},{385... | collective-permute-start | bytes 49160 | tf_op jit(solution)/shard_map/ppermute | solution.py:200
  50.5 3.7 %collective-permute-start.7 = (bf16[16,512]{1,0:T(8,128)(2,1)S(1)}, bf16[16,512]{1,0:T(8,128)(2,1)S(1)}, u32[]{:S(2)}, u32[]{:S(2)}) collective-permute-start(bf16[16,512]{1,0:T(8,128)(2,1)S(1)} %get-tuple-element.22), channel_id=1, source_target_pairs={{0,384},{128,0},{256,128},{384,256},{1,385},{129,1},{257,129},{385... | collective-permute-start | bytes 49160 | tf_op jit(solution)/shard_map/ppermute | solution.py:200
  54.3 2.8 %collective-permute-done.7.refs_2_ = bf16[16,512]{1,0:T(8,128)(2,1)S(1)} collective-permute-done((bf16[16,512]{1,0:T(8,128)(2,1)S(1)}, bf16[16,512]{1,0:T(8,128)(2,1)S(1)}, u32[]{:S(2)}, u32[]{:S(2)}) %collective-permute-start.7) | collective-permute-done | bytes 16416 | tf_op jit(solution)/shard_map/ppermute | solution.py:200
  60.8 3.0 %shard_map.108 = bf16[8,128,512]{2,1,0:T(8,128)(2,1)} custom-call(bf16[8,128,1024]{2,1,0:T(8,128)(2,1)S(1)} %all-to-all-done.x_ref, bf16[512,512]{1,0:T(8,128)(2,1)} %collective-permute-done.wo_ref, bf16[512,512]{1,0:T(8,128)(2,1)S(1)} %bitcast.26, bf16[16,512]{1,0:T(8,128)(2,1)S(1)} %get-tuple-element.23._.refs_0_), custom_call_target="tpu_custom_call" | custom-call | tf_op jit(solution)/shard_map/pallas_call | solution.py:114
  63.9 3.9 %all-to-all-start.1 = ((bf16[8,128,512]{2,1,0:T(8,128)(2,1)}), bf16[8,128,512]{2,1,0:T(8,128)(2,1)S(1)}, u32[]{:S(2)}, u32[]{:S(2)}) async-start(bf16[8,128,512]{2,1,0:T(8,128)(2,1)} %shard_map.108), calls=%async_computation.1 | async-start | bytes 2097152 | tf_op jit(solution)/shard_map/all_to_all | solution.py:48
  67.8 8.8 %collective-permute-start.10 = (bf16[16,512]{1,0:T(8,128)(2,1)S(1)}, bf16[16,512]{1,0:T(8,128)(2,1)S(1)}, u32[]{:S(2)}, u32[]{:S(2)}) collective-permute-start(bf16[16,512]{1,0:T(8,128)(2,1)S(1)} %get-tuple-element.23._.refs_0_), channel_id=1, source_target_pairs={{0,384},{128,0},{256,128},{384,256},{1,385},{129,1},{257,129},{385... | collective-permute-start | bytes 49160 | tf_op jit(solution)/shard_map/ppermute | solution.py:200
  78.6 4.8 %collective-permute-start.8 = (bf16[16,512]{1,0:T(8,128)(2,1)S(1)}, bf16[16,512]{1,0:T(8,128)(2,1)S(1)}, u32[]{:S(2)}, u32[]{:S(2)}) collective-permute-start(bf16[16,512]{1,0:T(8,128)(2,1)S(1)} %get-tuple-element.23._.refs_0_), channel_id=1, source_target_pairs={{0,128},{128,256},{256,384},{384,0},{1,129},{129,257},{257,385},{3... | collective-permute-start | bytes 49160 | tf_op jit(solution)/shard_map/ppermute | solution.py:200
  83.4 4.3 %collective-permute-done.9.refs_2_ = bf16[16,512]{1,0:T(8,128)(2,1)S(1)} collective-permute-done((bf16[16,512]{1,0:T(8,128)(2,1)S(1)}, bf16[16,512]{1,0:T(8,128)(2,1)S(1)}, u32[]{:S(2)}, u32[]{:S(2)}) %collective-permute-start.9) | collective-permute-done | bytes 16416 | tf_op jit(solution)/shard_map/ppermute | solution.py:200
  90.5 3.9 %all-to-all-start.2 = ((bf16[8,128,512]{2,1,0:T(8,128)(2,1)}), bf16[8,128,512]{2,1,0:T(8,128)(2,1)S(1)}, u32[]{:S(2)}, u32[]{:S(2)}) async-start(bf16[8,128,512]{2,1,0:T(8,128)(2,1)} %shard_map.110), calls=%async_computation.2 | async-start | bytes 2097152 | tf_op jit(solution)/shard_map/all_to_all | solution.py:48
  94.4 4.4 %collective-permute-start.15 = (bf16[4,16,512]{2,1,0:T(8,128)(2,1)S(1)}, bf16[4,16,512]{2,1,0:T(8,128)(2,1)S(1)}, u32[]{:S(2)}, u32[]{:S(2)}) collective-permute-start(bf16[4,16,512]{2,1,0:T(8,128)(2,1)S(1)} %shard_map.109._.refs_0_), channel_id=1, source_target_pairs={{0,96},{32,0},{64,32},{96,64},{1,97},{33,1},{65,33},{97,65},{2,98}... | collective-permute-start | bytes 196616 | tf_op jit(solution)/shard_map/ppermute | solution.py:200
  98.8 2.3 %collective-permute-start.14 = (bf16[4,16,512]{2,1,0:T(8,128)(2,1)S(1)}, bf16[4,16,512]{2,1,0:T(8,128)(2,1)S(1)}, u32[]{:S(2)}, u32[]{:S(2)}) collective-permute-start(bf16[4,16,512]{2,1,0:T(8,128)(2,1)S(1)} %shard_map.109._.refs_0_), channel_id=1, source_target_pairs={{0,64},{32,96},{64,0},{96,32},{1,65},{33,97},{65,1},{97,33},{2,66}... | collective-permute-start | bytes 196616 | tf_op jit(solution)/shard_map/ppermute | solution.py:200
  101.2 4.5 %collective-permute-start.13 = (bf16[4,16,512]{2,1,0:T(8,128)(2,1)S(1)}, bf16[4,16,512]{2,1,0:T(8,128)(2,1)S(1)}, u32[]{:S(2)}, u32[]{:S(2)}) collective-permute-start(bf16[4,16,512]{2,1,0:T(8,128)(2,1)S(1)} %shard_map.109._.refs_0_), channel_id=1, source_target_pairs={{0,32},{32,64},{64,96},{96,0},{1,33},{33,65},{65,97},{97,1},{2,34}... | collective-permute-start | bytes 196616 | tf_op jit(solution)/shard_map/ppermute | solution.py:200
  108.0 2.5 %collective-permute-start.16 = (bf16[4,4,16,512]{3,2,1,0:T(8,128)(2,1)S(1)}, bf16[4,4,16,512]{3,2,1,0:T(8,128)(2,1)}, u32[]{:S(2)}, u32[]{:S(2)}) collective-permute-start(bf16[4,4,16,512]{3,2,1,0:T(8,128)(2,1)S(1)} %shard_map.114.m_ref), channel_id=1, source_target_pairs={{0,16},{16,0},{1,17},{17,1},{2,18},{18,2},{3,19},{19,3},{4,20},{20... | collective-permute-start | bytes 786440 | tf_op jit(solution)/shard_map/ppermute | solution.py:334
  113.2 4.7 %all-to-all-done.2 = bf16[8,128,512]{2,1,0:T(8,128)(2,1)S(1)} async-done(((bf16[8,128,512]{2,1,0:T(8,128)(2,1)}), bf16[8,128,512]{2,1,0:T(8,128)(2,1)S(1)}, u32[]{:S(2)}, u32[]{:S(2)}) %all-to-all-start.2) | async-done | bytes 1048608 | tf_op jit(solution)/shard_map/all_to_all | solution.py:48
  120.7 5.1 %collective-permute-start.12 = (bf16[256,512]{1,0:T(8,128)(2,1)S(1)}, bf16[256,512]{1,0:T(8,128)(2,1)S(1)}, u32[]{:S(2)}, u32[]{:S(2)}) collective-permute-start(bf16[256,512]{1,0:T(8,128)(2,1)S(1)} %shard_map.113), channel_id=1, source_target_pairs={{0,7},{1,6},{2,5},{3,4},{4,3},{5,2},{6,1},{7,0},{8,15},{9,14},{10,... | collective-permute-start | bytes 786440 | tf_op jit(solution)/shard_map/ppermute | solution.py:54
  125.9 1.9 %shard_map.115 = bf16[4,4,2,16,512]{4,3,2,1,0:T(8,128)(2,1)} custom-call(s32[1]{0:T(128)} %bitcast.5.due_ref, s32[1]{0:T(128)} %bitcast.core_ref, bf16[2,4,4,2,16,512]{5,4,3,2,1,0:T(8,128)(2,1)S(1)} %bitcast.24, bf16[4,4,16,512]{3,2,1,0:T(8,128)(2,1)S(1)} %shard_map.114.m_ref, bf16[4,4,16,512]{3,2,1,0:T(8,128)(2,1)} %collective-permute-done.16.a_ref), custom_call_target="tpu_custom_call" | custom-call | tf_op jit(solution)/shard_map/pallas_call | solution.py:188
  128.5 8.0 %collective-permute-done.12 = bf16[256,512]{1,0:T(8,128)(2,1)S(1)} collective-permute-done((bf16[256,512]{1,0:T(8,128)(2,1)S(1)}, bf16[256,512]{1,0:T(8,128)(2,1)S(1)}, u32[]{:S(2)}, u32[]{:S(2)}) %collective-permute-start.12) | collective-permute-done | bytes 262176 | tf_op jit(solution)/shard_map/ppermute | solution.py:54
  (47 shorter events, 26.5 us)
Async XLA Ops:
  3.3 13.1 %copy-start.2 = (bf16[1,2,512,512]{3,2,1,0:T(8,128)(2,1)S(1)}, bf16[1,2,512,512]{3,2,1,0:T(8,128)(2,1)}, u32[]{:S(2)}) copy-start(bf16[1,2,512,512]{3,2,1,0:T(8,128)(2,1)} %param.10) | copy-start | bytes 3145732
  3.3 56.1 %all-to-all-start = ((bf16[8,128,1024]{2,1,0:T(8,128)(2,1)}), bf16[8,128,1024]{2,1,0:T(8,128)(2,1)S(1)}, u32[]{:S(2)}, u32[]{:S(2)}) async-start(bf16[8,128,1024]{2,1,0:T(8,128)(2,1)} %shard_map.102), calls=%async_computation | async-start | bytes 4194304 | tf_op jit(solution)/shard_map/all_to_all | solution.py:48
  10.1 49.3 %collective-permute-start = (bf16[512,512]{1,0:T(8,128)(2,1)}, bf16[512,512]{1,0:T(8,128)(2,1)}, u32[]{:S(2)}, u32[]{:S(2)}) collective-permute-start(bf16[512,512]{1,0:T(8,128)(2,1)} %bitcast.25), channel_id=1, source_target_pairs={{0,7},{1,6},{2,5},{3,4},{4,3},{5,2},{6,1},{7,0},{8,15},{9,14},{10,... | collective-permute-start | bytes 1572872 | tf_op jit(solution)/shard_map/ppermute | solution.py:54
  17.1 3.6 %collective-permute-start.1 = (bf16[4,4,16,512]{3,2,1,0:T(8,128)(2,1)}, bf16[4,4,16,512]{3,2,1,0:T(8,128)(2,1)S(1)}, u32[]{:S(2)}, u32[]{:S(2)}) collective-permute-start(bf16[4,4,16,512]{3,2,1,0:T(8,128)(2,1)} %shard_map.104), channel_id=1, source_target_pairs={{0,16},{16,0},{1,17},{17,1},{2,18},{18,2},{3,19},{19,3},{4,20},{20... | collective-permute-start | bytes 786440 | tf_op jit(solution)/shard_map/ppermute | solution.py:322
  21.4 8.7 %collective-permute-start.2 = (bf16[4,16,512]{2,1,0:T(8,128)(2,1)}, bf16[4,16,512]{2,1,0:T(8,128)(2,1)S(1)}, u32[]{:S(2)}, u32[]{:S(2)}) collective-permute-start(bf16[4,16,512]{2,1,0:T(8,128)(2,1)} %get-tuple-element.16), channel_id=1, source_target_pairs={{0,32},{32,64},{64,96},{96,0},{1,33},{33,65},{65,97},{97,1},{2,34}... | collective-permute-start | bytes 196616 | tf_op jit(solution)/shard_map/ppermute | solution.py:200
  23.8 7.9 %collective-permute-start.3 = (bf16[4,16,512]{2,1,0:T(8,128)(2,1)}, bf16[4,16,512]{2,1,0:T(8,128)(2,1)S(1)}, u32[]{:S(2)}, u32[]{:S(2)}) collective-permute-start(bf16[4,16,512]{2,1,0:T(8,128)(2,1)} %get-tuple-element.17), channel_id=1, source_target_pairs={{0,64},{32,96},{64,0},{96,32},{1,65},{33,97},{65,1},{97,33},{2,66}... | collective-permute-start | bytes 196616 | tf_op jit(solution)/shard_map/ppermute | solution.py:200
  28.2 7.6 %collective-permute-start.4 = (bf16[4,16,512]{2,1,0:T(8,128)(2,1)}, bf16[4,16,512]{2,1,0:T(8,128)(2,1)S(1)}, u32[]{:S(2)}, u32[]{:S(2)}) collective-permute-start(bf16[4,16,512]{2,1,0:T(8,128)(2,1)} %get-tuple-element.18), channel_id=1, source_target_pairs={{0,96},{32,0},{64,32},{96,64},{1,97},{33,1},{65,33},{97,65},{2,98}... | collective-permute-start | bytes 196616 | tf_op jit(solution)/shard_map/ppermute | solution.py:200
  35.8 18.5 %collective-permute-start.5 = (bf16[16,512]{1,0:T(8,128)(2,1)S(1)}, bf16[16,512]{1,0:T(8,128)(2,1)S(1)}, u32[]{:S(2)}, u32[]{:S(2)}) collective-permute-start(bf16[16,512]{1,0:T(8,128)(2,1)S(1)} %get-tuple-element.20), channel_id=1, source_target_pairs={{0,128},{128,256},{256,384},{384,0},{1,129},{129,257},{257,385},{3... | collective-permute-start | bytes 49160 | tf_op jit(solution)/shard_map/ppermute | solution.py:200
  41.9 12.4 %collective-permute-start.6 = (bf16[16,512]{1,0:T(8,128)(2,1)S(1)}, bf16[16,512]{1,0:T(8,128)(2,1)S(1)}, u32[]{:S(2)}, u32[]{:S(2)}) collective-permute-start(bf16[16,512]{1,0:T(8,128)(2,1)S(1)} %get-tuple-element.21), channel_id=1, source_target_pairs={{0,256},{128,384},{256,0},{384,128},{1,257},{129,385},{257,1},{385... | collective-permute-start | bytes 49160 | tf_op jit(solution)/shard_map/ppermute | solution.py:200
  50.5 6.5 %collective-permute-start.7 = (bf16[16,512]{1,0:T(8,128)(2,1)S(1)}, bf16[16,512]{1,0:T(8,128)(2,1)S(1)}, u32[]{:S(2)}, u32[]{:S(2)}) collective-permute-start(bf16[16,512]{1,0:T(8,128)(2,1)S(1)} %get-tuple-element.22), channel_id=1, source_target_pairs={{0,384},{128,0},{256,128},{384,256},{1,385},{129,1},{257,129},{385... | collective-permute-start | bytes 49160 | tf_op jit(solution)/shard_map/ppermute | solution.py:200
  59.4 4.4 %copy-start = (bf16[8,128,1024]{2,1,0:T(8,128)(2,1)}, bf16[8,128,1024]{2,1,0:T(8,128)(2,1)S(1)}, u32[]{:S(2)}) copy-start(bf16[8,128,1024]{2,1,0:T(8,128)(2,1)S(1)} %all-to-all-done.x_ref) | copy-start | bytes 6291460
  63.9 25.4 %copy-start.5 = (bf16[128,512]{1,0:T(8,128)(2,1)S(1)}, bf16[128,512]{1,0:T(8,128)(2,1)}, u32[]{:S(2)}) copy-start(bf16[128,512]{1,0:T(8,128)(2,1)} %c_ref.1) | copy-start | bytes 393220
  63.9 25.4 %all-to-all-start.1 = ((bf16[8,128,512]{2,1,0:T(8,128)(2,1)}), bf16[8,128,512]{2,1,0:T(8,128)(2,1)S(1)}, u32[]{:S(2)}, u32[]{:S(2)}) async-start(bf16[8,128,512]{2,1,0:T(8,128)(2,1)} %shard_map.108), calls=%async_computation.1 | async-start | bytes 2097152 | tf_op jit(solution)/shard_map/all_to_all | solution.py:48
  67.8 15.6 %collective-permute-start.10 = (bf16[16,512]{1,0:T(8,128)(2,1)S(1)}, bf16[16,512]{1,0:T(8,128)(2,1)S(1)}, u32[]{:S(2)}, u32[]{:S(2)}) collective-permute-start(bf16[16,512]{1,0:T(8,128)(2,1)S(1)} %get-tuple-element.23._.refs_0_), channel_id=1, source_target_pairs={{0,384},{128,0},{256,128},{384,256},{1,385},{129,1},{257,129},{385... | collective-permute-start | bytes 49160 | tf_op jit(solution)/shard_map/ppermute | solution.py:200
  76.7 11.1 %collective-permute-start.9 = (bf16[16,512]{1,0:T(8,128)(2,1)S(1)}, bf16[16,512]{1,0:T(8,128)(2,1)S(1)}, u32[]{:S(2)}, u32[]{:S(2)}) collective-permute-start(bf16[16,512]{1,0:T(8,128)(2,1)S(1)} %get-tuple-element.23._.refs_0_), channel_id=1, source_target_pairs={{0,256},{128,384},{256,0},{384,128},{1,257},{129,385},{257,1},{385... | collective-permute-start | bytes 49160 | tf_op jit(solution)/shard_map/ppermute | solution.py:200
  78.6 9.3 %collective-permute-start.8 = (bf16[16,512]{1,0:T(8,128)(2,1)S(1)}, bf16[16,512]{1,0:T(8,128)(2,1)S(1)}, u32[]{:S(2)}, u32[]{:S(2)}) collective-permute-start(bf16[16,512]{1,0:T(8,128)(2,1)S(1)} %get-tuple-element.23._.refs_0_), channel_id=1, source_target_pairs={{0,128},{128,256},{256,384},{384,0},{1,129},{129,257},{257,385},{3... | collective-permute-start | bytes 49160 | tf_op jit(solution)/shard_map/ppermute | solution.py:200
  90.5 27.4 %all-to-all-start.2 = ((bf16[8,128,512]{2,1,0:T(8,128)(2,1)}), bf16[8,128,512]{2,1,0:T(8,128)(2,1)S(1)}, u32[]{:S(2)}, u32[]{:S(2)}) async-start(bf16[8,128,512]{2,1,0:T(8,128)(2,1)} %shard_map.110), calls=%async_computation.2 | async-start | bytes 2097152 | tf_op jit(solution)/shard_map/all_to_all | solution.py:48
  94.4 11.3 %collective-permute-start.15 = (bf16[4,16,512]{2,1,0:T(8,128)(2,1)S(1)}, bf16[4,16,512]{2,1,0:T(8,128)(2,1)S(1)}, u32[]{:S(2)}, u32[]{:S(2)}) collective-permute-start(bf16[4,16,512]{2,1,0:T(8,128)(2,1)S(1)} %shard_map.109._.refs_0_), channel_id=1, source_target_pairs={{0,96},{32,0},{64,32},{96,64},{1,97},{33,1},{65,33},{97,65},{2,98}... | collective-permute-start | bytes 196616 | tf_op jit(solution)/shard_map/ppermute | solution.py:200
  98.8 8.1 %collective-permute-start.14 = (bf16[4,16,512]{2,1,0:T(8,128)(2,1)S(1)}, bf16[4,16,512]{2,1,0:T(8,128)(2,1)S(1)}, u32[]{:S(2)}, u32[]{:S(2)}) collective-permute-start(bf16[4,16,512]{2,1,0:T(8,128)(2,1)S(1)} %shard_map.109._.refs_0_), channel_id=1, source_target_pairs={{0,64},{32,96},{64,0},{96,32},{1,65},{33,97},{65,1},{97,33},{2,66}... | collective-permute-start | bytes 196616 | tf_op jit(solution)/shard_map/ppermute | solution.py:200
  101.2 6.8 %collective-permute-start.13 = (bf16[4,16,512]{2,1,0:T(8,128)(2,1)S(1)}, bf16[4,16,512]{2,1,0:T(8,128)(2,1)S(1)}, u32[]{:S(2)}, u32[]{:S(2)}) collective-permute-start(bf16[4,16,512]{2,1,0:T(8,128)(2,1)S(1)} %shard_map.109._.refs_0_), channel_id=1, source_target_pairs={{0,32},{32,64},{64,96},{96,0},{1,33},{33,65},{65,97},{97,1},{2,34}... | collective-permute-start | bytes 196616 | tf_op jit(solution)/shard_map/ppermute | solution.py:200
  108.0 17.9 %collective-permute-start.16 = (bf16[4,4,16,512]{3,2,1,0:T(8,128)(2,1)S(1)}, bf16[4,4,16,512]{3,2,1,0:T(8,128)(2,1)}, u32[]{:S(2)}, u32[]{:S(2)}) collective-permute-start(bf16[4,4,16,512]{3,2,1,0:T(8,128)(2,1)S(1)} %shard_map.114.m_ref), channel_id=1, source_target_pairs={{0,16},{16,0},{1,17},{17,1},{2,18},{18,2},{3,19},{19,3},{4,20},{20... | collective-permute-start | bytes 786440 | tf_op jit(solution)/shard_map/ppermute | solution.py:334
  118.3 7.5 %copy-start.3 = (bf16[1,2,512,512]{3,2,1,0:T(8,128)(2,1)S(1)}, bf16[1,2,512,512]{3,2,1,0:T(8,128)(2,1)}, u32[]{:S(2)}) copy-start(bf16[1,2,512,512]{3,2,1,0:T(8,128)(2,1)} %param.10) | copy-start | bytes 3145732
  118.8 9.7 %collective-permute-start.11 = (bf16[256,512]{1,0:T(8,128)(2,1)S(1)}, bf16[256,512]{1,0:T(8,128)(2,1)S(1)}, u32[]{:S(2)}, u32[]{:S(2)}) collective-permute-start(bf16[256,512]{1,0:T(8,128)(2,1)S(1)} %shard_map.112), channel_id=1, source_target_pairs={{0,7},{1,6},{2,5},{3,4},{4,3},{5,2},{6,1},{7,0},{8,15},{9,14},{10,... | collective-permute-start | bytes 786440 | tf_op jit(solution)/shard_map/ppermute | solution.py:54
  120.7 15.8 %collective-permute-start.12 = (bf16[256,512]{1,0:T(8,128)(2,1)S(1)}, bf16[256,512]{1,0:T(8,128)(2,1)S(1)}, u32[]{:S(2)}, u32[]{:S(2)}) collective-permute-start(bf16[256,512]{1,0:T(8,128)(2,1)S(1)} %shard_map.113), channel_id=1, source_target_pairs={{0,7},{1,6},{2,5},{3,4},{4,3},{5,2},{6,1},{7,0},{8,15},{9,14},{10,... | collective-permute-start | bytes 786440 | tf_op jit(solution)/shard_map/ppermute | solution.py:54
  (4 other events, 4.7 us)

commit v4 on v3

--- a/solution.py
+++ b/solution.py
@@ -100,62 +100,38 @@
     n, rows, feat2 = x.shape
     feat, cols = w.shape
 
-    def kernel(x_ref, wo_ref, w_ref, _, o_ref, buf, sems):
-        copies = []
+    def kernel(x_ref, wo_ref, w_ref, _, o_ref):
         for j in range(n):
             acc = jnp.dot(x_ref[j, :, :feat], wo_ref[...], preferred_element_type=f32)
             acc += jnp.dot(x_ref[j, :, feat:], w_ref[...], preferred_element_type=f32)
-            buf[j] = acc.astype(bf16)
-            copies.append(pltpu.make_async_copy(buf.at[j], o_ref.at[j], sems.at[j]))
-            copies[j].start()
-        for copy in copies:
-            copy.wait()
+            o_ref[j] = acc.astype(bf16)
 
     return pl.pallas_call(
         kernel,
         out_shape=jax.ShapeDtypeStruct((n, rows, cols), bf16),
         in_specs=[VMEM] * 3 + [ANY],
-        out_specs=HBM,
-        scratch_shapes=[pltpu.VMEM((n, rows, cols), bf16), pltpu.SemaphoreType.DMA((n,))],
+        out_specs=VMEM,
         compiler_params=PARAMS,
     )(x, w_other, w, after)
 
 
-def flip(x):
-    toks, feats = x.shape
-    step = 256
-
-    return pl.pallas_call(
-        lambda x_ref, o_ref: o_ref.__setitem__(..., x_ref[...].T),
-        out_shape=jax.ShapeDtypeStruct((feats, toks), x.dtype),
-        grid=(feats // step,),
-        in_specs=[pl.BlockSpec((toks, step), lambda i: (0, i))],
-        out_specs=pl.BlockSpec((step, toks), lambda i: (i, 0)),
-        compiler_params=PARAMS,
-    )(x)
-
-
 def gate(parts, cotangent, after):
     n, rows, cols = parts.shape
 
-    def kernel(p_ref, c_ref, _, o_ref, buf, sems):
+    def kernel(p_ref, c_ref, _, o_ref):
         y = p_ref[0].astype(f32)
         for j in range(1, n):
             y += p_ref[j].astype(f32)
         s = jax.nn.sigmoid(y)
-        buf[...] = (c_ref[...].astype(f32) * s * (1.0 + y * (1.0 - s))).astype(bf16)
-        copies = [pltpu.make_async_copy(buf, o_ref.at[j], sems.at[j]) for j in range(n)]
-        for copy in copies:
-            copy.start()
-        for copy in copies:
-            copy.wait()
+        g = (c_ref[...].astype(f32) * s * (1.0 + y * (1.0 - s))).astype(bf16)
+        for j in range(n):
+            o_ref[j] = g
 
     return pl.pallas_call(
         kernel,
         out_shape=jax.ShapeDtypeStruct((n, rows, cols), bf16),
         in_specs=[VMEM] * 2 + [ANY],
-        out_specs=HBM,
-        scratch_shapes=[pltpu.VMEM((rows, cols), bf16), pltpu.SemaphoreType.DMA((n,))],
+        out_specs=VMEM,
         compiler_params=PARAMS,
     )(parts, cotangent, after)
 
@@ -167,14 +143,14 @@
     def kernel(x_ref, g_ref, o_ref):
         for j in range(count // step):
             at = slice(j * step, (j + 1) * step)
-            o_ref[at] = jnp.dot(x_ref[at], g_ref[...], preferred_element_type=f32).astype(dtype)
+            o_ref[at] = lax.dot_general(x_ref[:, at], g_ref[...], (((0,), (0,)), ((), ())), preferred_element_type=f32).astype(dtype)
 
     return pl.pallas_call(
         kernel,
         out_shape=jax.ShapeDtypeStruct((count, cols), dtype),
         grid=(1,),
         in_specs=[
-            pl.BlockSpec((count, toks), lambda i: (first // count, 0)),
+            pl.BlockSpec((toks, count), lambda i: (0, first // count)),
             pl.BlockSpec((toks, cols), lambda i: (0, 0)),
         ],
         out_specs=pl.BlockSpec((count, cols), lambda i: (0, 0)),
@@ -328,7 +304,7 @@
     line = z_rows(half, shifts([half] * 3, "zh"), zh)
     grads = swap_line(gate(parts, cotangent, line)).reshape(GROUP * rows, cols)
     plane = x_rows(line, shifts([line] * 3, "x"), xx)
-    xt = flip(x.reshape(GROUP * rows, 2 * feat))
+    xt = x.reshape(GROUP * rows, 2 * feat)
     piece = feat // 2
     away = [mirror(product(xt, grads, i * piece, piece, bf16)) for i in range(2)]
     new_fragment = merge(local, plane, lax.ppermute(plane, "c", SWAP), due, core)

time: 140 us -> 138 us (0.986)
  Pallas kernels: 13.7 us -> 10.9 us
  waiting for transfers between devices: 30.9 us -> 32.8 us
    ppermute x12, waiting for transfers between devices: 15.2 us -> 17.1 us  [shifts(): lax.ppermute(array, name, [(i, (i + k) % n) for i in range(n)])]
  transfers between devices with their start and end apart: 20 -> 20, of which waited for: 11 -> 10; matrix products, arithmetic and copies ran while one was open for 0% -> 0% of each run, Pallas kernels for 5% -> 4%
where the time goes in v4:
time: 138 us; the launch traced here: 137 us
  starting transfers between devices  85.5 us (62%)
  waiting for transfers between devices  32.8 us (24%)
  Pallas kernels  10.9 us (8%)
  local copies, waits for them, and re-layouts  4.67 us (3%)
  between operations  1.69 us (1%)
    ppermute x12, starting transfers between devices, shifts(): lax.ppermute(array, name, [(i, (i + k) % n) for i in range(n)])  53.9 us
    ppermute x12, waiting for transfers between devices, shifts(): lax.ppermute(array, name, [(i, (i + k) % n) for i in range(n)])  17.1 us
    all_to_all x3, starting transfers between devices, swap_line(): lax.all_to_all(array, CHIPS, split_axis=0, concat_axis=0, axis_index_grou...  15 us
    ppermute x3, starting transfers between devices, mirror(): return lax.ppermute(array, CHIPS, MIRROR)  12.6 us
    ppermute x3, waiting for transfers between devices, mirror(): return lax.ppermute(array, CHIPS, MIRROR)  8.13 us
    all_to_all x3, waiting for transfers between devices, swap_line(): lax.all_to_all(array, CHIPS, split_axis=0, concat_axis=0, axis_index_grou...  5.93 us
    unnamed x16, local copies, waits for them, and re-layouts  4.67 us
    pallas_call x7, Pallas kernels, call(): pl.pallas_call(kernel, out_shape=[jax.ShapeDtypeStruct(shape, dtype) for...  4.09 us
  transfers between devices with their start and end apart: 20, of which 10 were waited for; matrix products, arithmetic and copies ran while one was open for 0% of the time, Pallas kernels for 4%

profile of v4, /device:TPU:6, one launch (start us, length us, event | category | flops | bytes accessed | tf_op | source)
XLA Modules:
  0.0 136.5 jit_solution(855456546156029368)
XLA Ops:
  0.6 2.6 %shard_map.102 = bf16[8,128,1024]{2,1,0:T(8,128)(2,1)} custom-call(s32[1]{0:T(128)} %bitcast.core_ref, s32[1]{0:T(128)} %bitcast.1.y_ref, bf16[128,8192]{1,0:T(8,128)(2,1)} %t_ref.1), custom_call_target="tpu_custom_call" | custom-call | tf_op jit(solution)/shard_map/pallas_call | solution.py:85
  3.3 6.8 %all-to-all-start = ((bf16[8,128,1024]{2,1,0:T(8,128)(2,1)}), bf16[8,128,1024]{2,1,0:T(8,128)(2,1)S(1)}, u32[]{:S(2)}, u32[]{:S(2)}) async-start(bf16[8,128,1024]{2,1,0:T(8,128)(2,1)} %shard_map.102), calls=%async_computation | async-start | bytes 4194304 | tf_op jit(solution)/shard_map/all_to_all | solution.py:48
  10.1 5.6 %collective-permute-start = (bf16[512,512]{1,0:T(8,128)(2,1)}, bf16[512,512]{1,0:T(8,128)(2,1)}, u32[]{:S(2)}, u32[]{:S(2)}) collective-permute-start(bf16[512,512]{1,0:T(8,128)(2,1)} %bitcast.27), channel_id=1, source_target_pairs={{0,7},{1,6},{2,5},{3,4},{4,3},{5,2},{6,1},{7,0},{8,15},{9,14},{10,... | collective-permute-start | bytes 1572872 | tf_op jit(solution)/shard_map/ppermute | solution.py:54
  21.4 2.4 %collective-permute-start.2 = (bf16[4,16,512]{2,1,0:T(8,128)(2,1)}, bf16[4,16,512]{2,1,0:T(8,128)(2,1)S(1)}, u32[]{:S(2)}, u32[]{:S(2)}) collective-permute-start(bf16[4,16,512]{2,1,0:T(8,128)(2,1)} %get-tuple-element.16), channel_id=1, source_target_pairs={{0,32},{32,64},{64,96},{96,0},{1,33},{33,65},{65,97},{97,1},{2,34}... | collective-permute-start | bytes 196616 | tf_op jit(solution)/shard_map/ppermute | solution.py:176
  23.8 4.3 %collective-permute-start.3 = (bf16[4,16,512]{2,1,0:T(8,128)(2,1)}, bf16[4,16,512]{2,1,0:T(8,128)(2,1)S(1)}, u32[]{:S(2)}, u32[]{:S(2)}) collective-permute-start(bf16[4,16,512]{2,1,0:T(8,128)(2,1)} %get-tuple-element.17), channel_id=1, source_target_pairs={{0,64},{32,96},{64,0},{96,32},{1,65},{33,97},{65,1},{97,33},{2,66}... | collective-permute-start | bytes 196616 | tf_op jit(solution)/shard_map/ppermute | solution.py:176
  31.7 4.0 %collective-permute-done.4.refs_2_ = bf16[4,16,512]{2,1,0:T(8,128)(2,1)S(1)} collective-permute-done((bf16[4,16,512]{2,1,0:T(8,128)(2,1)}, bf16[4,16,512]{2,1,0:T(8,128)(2,1)S(1)}, u32[]{:S(2)}, u32[]{:S(2)}) %collective-permute-start.4) | collective-permute-done | bytes 65568 | tf_op jit(solution)/shard_map/ppermute | solution.py:176
  35.8 6.1 %collective-permute-start.5 = (bf16[16,512]{1,0:T(8,128)(2,1)S(1)}, bf16[16,512]{1,0:T(8,128)(2,1)S(1)}, u32[]{:S(2)}, u32[]{:S(2)}) collective-permute-start(bf16[16,512]{1,0:T(8,128)(2,1)S(1)} %get-tuple-element.20), channel_id=1, source_target_pairs={{0,128},{128,256},{256,384},{384,0},{1,129},{129,257},{257,385},{3... | collective-permute-start | bytes 49160 | tf_op jit(solution)/shard_map/ppermute | solution.py:176
  41.9 8.7 %collective-permute-start.6 = (bf16[16,512]{1,0:T(8,128)(2,1)S(1)}, bf16[16,512]{1,0:T(8,128)(2,1)S(1)}, u32[]{:S(2)}, u32[]{:S(2)}) collective-permute-start(bf16[16,512]{1,0:T(8,128)(2,1)S(1)} %get-tuple-element.21), channel_id=1, source_target_pairs={{0,256},{128,384},{256,0},{384,128},{1,257},{129,385},{257,1},{385... | collective-permute-start | bytes 49160 | tf_op jit(solution)/shard_map/ppermute | solution.py:176
  50.5 3.7 %collective-permute-start.7 = (bf16[16,512]{1,0:T(8,128)(2,1)S(1)}, bf16[16,512]{1,0:T(8,128)(2,1)S(1)}, u32[]{:S(2)}, u32[]{:S(2)}) collective-permute-start(bf16[16,512]{1,0:T(8,128)(2,1)S(1)} %get-tuple-element.22), channel_id=1, source_target_pairs={{0,384},{128,0},{256,128},{384,256},{1,385},{129,1},{257,129},{385... | collective-permute-start | bytes 49160 | tf_op jit(solution)/shard_map/ppermute | solution.py:176
  54.3 2.8 %collective-permute-done.7.refs_2_ = bf16[16,512]{1,0:T(8,128)(2,1)S(1)} collective-permute-done((bf16[16,512]{1,0:T(8,128)(2,1)S(1)}, bf16[16,512]{1,0:T(8,128)(2,1)S(1)}, u32[]{:S(2)}, u32[]{:S(2)}) %collective-permute-start.7) | collective-permute-done | bytes 16416 | tf_op jit(solution)/shard_map/ppermute | solution.py:176
  60.5 2.3 %shard_map.107 = bf16[8,128,512]{2,1,0:T(8,128)(2,1)S(1)} custom-call(bf16[8,128,1024]{2,1,0:T(8,128)(2,1)S(1)} %all-to-all-done.x_ref, bf16[512,512]{1,0:T(8,128)(2,1)} %collective-permute-done.wo_ref, bf16[512,512]{1,0:T(8,128)(2,1)S(1)} %bitcast.28, bf16[16,512]{1,0:T(8,128)(2,1)S(1)} %get-tuple-element.23._.refs_0_), custom_call_target="tpu_custom_call" | custom-call | tf_op jit(solution)/shard_map/pallas_call | solution.py:109
  63.7 3.9 %all-to-all-start.1 = ((bf16[8,128,512]{2,1,0:T(8,128)(2,1)}), bf16[8,128,512]{2,1,0:T(8,128)(2,1)S(1)}, u32[]{:S(2)}, u32[]{:S(2)}) async-start(bf16[8,128,512]{2,1,0:T(8,128)(2,1)} %copy-done.3), calls=%async_computation.1 | async-start | bytes 2097152 | tf_op jit(solution)/shard_map/all_to_all | solution.py:48
  67.7 4.1 %collective-permute-start.8 = (bf16[16,512]{1,0:T(8,128)(2,1)S(1)}, bf16[16,512]{1,0:T(8,128)(2,1)S(1)}, u32[]{:S(2)}, u32[]{:S(2)}) collective-permute-start(bf16[16,512]{1,0:T(8,128)(2,1)S(1)} %get-tuple-element.23._.refs_0_), channel_id=1, source_target_pairs={{0,128},{128,256},{256,384},{384,0},{1,129},{129,257},{257,385},{3... | collective-permute-start | bytes 49160 | tf_op jit(solution)/shard_map/ppermute | solution.py:176
  71.7 9.1 %collective-permute-start.9 = (bf16[16,512]{1,0:T(8,128)(2,1)S(1)}, bf16[16,512]{1,0:T(8,128)(2,1)S(1)}, u32[]{:S(2)}, u32[]{:S(2)}) collective-permute-start(bf16[16,512]{1,0:T(8,128)(2,1)S(1)} %get-tuple-element.23._.refs_0_), channel_id=1, source_target_pairs={{0,256},{128,384},{256,0},{384,128},{1,257},{129,385},{257,1},{385... | collective-permute-start | bytes 49160 | tf_op jit(solution)/shard_map/ppermute | solution.py:176
  80.8 3.7 %collective-permute-start.10 = (bf16[16,512]{1,0:T(8,128)(2,1)S(1)}, bf16[16,512]{1,0:T(8,128)(2,1)S(1)}, u32[]{:S(2)}, u32[]{:S(2)}) collective-permute-start(bf16[16,512]{1,0:T(8,128)(2,1)S(1)} %get-tuple-element.23._.refs_0_), channel_id=1, source_target_pairs={{0,384},{128,0},{256,128},{384,256},{1,385},{129,1},{257,129},{385... | collective-permute-start | bytes 49160 | tf_op jit(solution)/shard_map/ppermute | solution.py:176
  84.5 2.8 %collective-permute-done.10.refs_3_ = bf16[16,512]{1,0:T(8,128)(2,1)S(1)} collective-permute-done((bf16[16,512]{1,0:T(8,128)(2,1)S(1)}, bf16[16,512]{1,0:T(8,128)(2,1)S(1)}, u32[]{:S(2)}, u32[]{:S(2)}) %collective-permute-start.10) | collective-permute-done | bytes 16416 | tf_op jit(solution)/shard_map/ppermute | solution.py:176
  90.4 4.3 %all-to-all-start.2 = ((bf16[8,128,512]{2,1,0:T(8,128)(2,1)}), bf16[8,128,512]{2,1,0:T(8,128)(2,1)S(1)}, u32[]{:S(2)}, u32[]{:S(2)}) async-start(bf16[8,128,512]{2,1,0:T(8,128)(2,1)} %copy-done.2), calls=%async_computation.2 | async-start | bytes 2097152 | tf_op jit(solution)/shard_map/all_to_all | solution.py:48
  94.6 2.4 %collective-permute-start.13 = (bf16[4,16,512]{2,1,0:T(8,128)(2,1)S(1)}, bf16[4,16,512]{2,1,0:T(8,128)(2,1)S(1)}, u32[]{:S(2)}, u32[]{:S(2)}) collective-permute-start(bf16[4,16,512]{2,1,0:T(8,128)(2,1)S(1)} %shard_map.108._.refs_0_), channel_id=1, source_target_pairs={{0,32},{32,64},{64,96},{96,0},{1,33},{33,65},{65,97},{97,1},{2,34}... | collective-permute-start | bytes 196616 | tf_op jit(solution)/shard_map/ppermute | solution.py:176
  97.0 5.8 %collective-permute-start.14 = (bf16[4,16,512]{2,1,0:T(8,128)(2,1)S(1)}, bf16[4,16,512]{2,1,0:T(8,128)(2,1)S(1)}, u32[]{:S(2)}, u32[]{:S(2)}) collective-permute-start(bf16[4,16,512]{2,1,0:T(8,128)(2,1)S(1)} %shard_map.108._.refs_0_), channel_id=1, source_target_pairs={{0,64},{32,96},{64,0},{96,32},{1,65},{33,97},{65,1},{97,33},{2,66}... | collective-permute-start | bytes 196616 | tf_op jit(solution)/shard_map/ppermute | solution.py:176
  105.0 5.5 %collective-permute-done.15.refs_3_ = bf16[4,16,512]{2,1,0:T(8,128)(2,1)S(1)} collective-permute-done((bf16[4,16,512]{2,1,0:T(8,128)(2,1)S(1)}, bf16[4,16,512]{2,1,0:T(8,128)(2,1)S(1)}, u32[]{:S(2)}, u32[]{:S(2)}) %collective-permute-start.15) | collective-permute-done | bytes 65568 | tf_op jit(solution)/shard_map/ppermute | solution.py:176
  112.6 4.1 %all-to-all-done.2 = bf16[8,128,512]{2,1,0:T(8,128)(2,1)S(1)} async-done(((bf16[8,128,512]{2,1,0:T(8,128)(2,1)}), bf16[8,128,512]{2,1,0:T(8,128)(2,1)S(1)}, u32[]{:S(2)}, u32[]{:S(2)}) %all-to-all-start.2) | async-done | bytes 1048608 | tf_op jit(solution)/shard_map/all_to_all | solution.py:48
  117.7 2.2 %collective-permute-start.12 = (bf16[256,512]{1,0:T(8,128)(2,1)S(1)}, bf16[256,512]{1,0:T(8,128)(2,1)S(1)}, u32[]{:S(2)}, u32[]{:S(2)}) collective-permute-start(bf16[256,512]{1,0:T(8,128)(2,1)S(1)} %shard_map.112), channel_id=1, source_target_pairs={{0,7},{1,6},{2,5},{3,4},{4,3},{5,2},{6,1},{7,0},{8,15},{9,14},{10,... | collective-permute-start | bytes 786440 | tf_op jit(solution)/shard_map/ppermute | solution.py:54
  119.9 4.8 %collective-permute-start.11 = (bf16[256,512]{1,0:T(8,128)(2,1)S(1)}, bf16[256,512]{1,0:T(8,128)(2,1)S(1)}, u32[]{:S(2)}, u32[]{:S(2)}) collective-permute-start(bf16[256,512]{1,0:T(8,128)(2,1)S(1)} %shard_map.111), channel_id=1, source_target_pairs={{0,7},{1,6},{2,5},{3,4},{4,3},{5,2},{6,1},{7,0},{8,15},{9,14},{10,... | collective-permute-start | bytes 786440 | tf_op jit(solution)/shard_map/ppermute | solution.py:54
  127.5 8.1 %collective-permute-done.11 = bf16[256,512]{1,0:T(8,128)(2,1)S(1)} collective-permute-done((bf16[256,512]{1,0:T(8,128)(2,1)S(1)}, bf16[256,512]{1,0:T(8,128)(2,1)S(1)}, u32[]{:S(2)}, u32[]{:S(2)}) %collective-permute-start.11) | collective-permute-done | bytes 262176 | tf_op jit(solution)/shard_map/ppermute | solution.py:54
  (46 shorter events, 24.8 us)
Async XLA Ops:
  3.3 13.1 %copy-start = (bf16[1,2,512,512]{3,2,1,0:T(8,128)(2,1)S(1)}, bf16[1,2,512,512]{3,2,1,0:T(8,128)(2,1)}, u32[]{:S(2)}) copy-start(bf16[1,2,512,512]{3,2,1,0:T(8,128)(2,1)} %param.10) | copy-start | bytes 3145732
  3.3 56.1 %all-to-all-start = ((bf16[8,128,1024]{2,1,0:T(8,128)(2,1)}), bf16[8,128,1024]{2,1,0:T(8,128)(2,1)S(1)}, u32[]{:S(2)}, u32[]{:S(2)}) async-start(bf16[8,128,1024]{2,1,0:T(8,128)(2,1)} %shard_map.102), calls=%async_computation | async-start | bytes 4194304 | tf_op jit(solution)/shard_map/all_to_all | solution.py:48
  10.1 49.3 %collective-permute-start = (bf16[512,512]{1,0:T(8,128)(2,1)}, bf16[512,512]{1,0:T(8,128)(2,1)}, u32[]{:S(2)}, u32[]{:S(2)}) collective-permute-start(bf16[512,512]{1,0:T(8,128)(2,1)} %bitcast.27), channel_id=1, source_target_pairs={{0,7},{1,6},{2,5},{3,4},{4,3},{5,2},{6,1},{7,0},{8,15},{9,14},{10,... | collective-permute-start | bytes 1572872 | tf_op jit(solution)/shard_map/ppermute | solution.py:54
  17.1 3.6 %collective-permute-start.1 = (bf16[4,4,16,512]{3,2,1,0:T(8,128)(2,1)}, bf16[4,4,16,512]{3,2,1,0:T(8,128)(2,1)S(1)}, u32[]{:S(2)}, u32[]{:S(2)}) collective-permute-start(bf16[4,4,16,512]{3,2,1,0:T(8,128)(2,1)} %shard_map.103), channel_id=1, source_target_pairs={{0,16},{16,0},{1,17},{17,1},{2,18},{18,2},{3,19},{19,3},{4,20},{20... | collective-permute-start | bytes 786440 | tf_op jit(solution)/shard_map/ppermute | solution.py:298
  21.4 8.7 %collective-permute-start.2 = (bf16[4,16,512]{2,1,0:T(8,128)(2,1)}, bf16[4,16,512]{2,1,0:T(8,128)(2,1)S(1)}, u32[]{:S(2)}, u32[]{:S(2)}) collective-permute-start(bf16[4,16,512]{2,1,0:T(8,128)(2,1)} %get-tuple-element.16), channel_id=1, source_target_pairs={{0,32},{32,64},{64,96},{96,0},{1,33},{33,65},{65,97},{97,1},{2,34}... | collective-permute-start | bytes 196616 | tf_op jit(solution)/shard_map/ppermute | solution.py:176
  23.8 7.9 %collective-permute-start.3 = (bf16[4,16,512]{2,1,0:T(8,128)(2,1)}, bf16[4,16,512]{2,1,0:T(8,128)(2,1)S(1)}, u32[]{:S(2)}, u32[]{:S(2)}) collective-permute-start(bf16[4,16,512]{2,1,0:T(8,128)(2,1)} %get-tuple-element.17), channel_id=1, source_target_pairs={{0,64},{32,96},{64,0},{96,32},{1,65},{33,97},{65,1},{97,33},{2,66}... | collective-permute-start | bytes 196616 | tf_op jit(solution)/shard_map/ppermute | solution.py:176
  28.2 7.6 %collective-permute-start.4 = (bf16[4,16,512]{2,1,0:T(8,128)(2,1)}, bf16[4,16,512]{2,1,0:T(8,128)(2,1)S(1)}, u32[]{:S(2)}, u32[]{:S(2)}) collective-permute-start(bf16[4,16,512]{2,1,0:T(8,128)(2,1)} %get-tuple-element.18), channel_id=1, source_target_pairs={{0,96},{32,0},{64,32},{96,64},{1,97},{33,1},{65,33},{97,65},{2,98}... | collective-permute-start | bytes 196616 | tf_op jit(solution)/shard_map/ppermute | solution.py:176
  35.8 18.5 %collective-permute-start.5 = (bf16[16,512]{1,0:T(8,128)(2,1)S(1)}, bf16[16,512]{1,0:T(8,128)(2,1)S(1)}, u32[]{:S(2)}, u32[]{:S(2)}) collective-permute-start(bf16[16,512]{1,0:T(8,128)(2,1)S(1)} %get-tuple-element.20), channel_id=1, source_target_pairs={{0,128},{128,256},{256,384},{384,0},{1,129},{129,257},{257,385},{3... | collective-permute-start | bytes 49160 | tf_op jit(solution)/shard_map/ppermute | solution.py:176
  41.9 12.4 %collective-permute-start.6 = (bf16[16,512]{1,0:T(8,128)(2,1)S(1)}, bf16[16,512]{1,0:T(8,128)(2,1)S(1)}, u32[]{:S(2)}, u32[]{:S(2)}) collective-permute-start(bf16[16,512]{1,0:T(8,128)(2,1)S(1)} %get-tuple-element.21), channel_id=1, source_target_pairs={{0,256},{128,384},{256,0},{384,128},{1,257},{129,385},{257,1},{385... | collective-permute-start | bytes 49160 | tf_op jit(solution)/shard_map/ppermute | solution.py:176
  50.5 6.5 %collective-permute-start.7 = (bf16[16,512]{1,0:T(8,128)(2,1)S(1)}, bf16[16,512]{1,0:T(8,128)(2,1)S(1)}, u32[]{:S(2)}, u32[]{:S(2)}) collective-permute-start(bf16[16,512]{1,0:T(8,128)(2,1)S(1)} %get-tuple-element.22), channel_id=1, source_target_pairs={{0,384},{128,0},{256,128},{384,256},{1,385},{129,1},{257,129},{385... | collective-permute-start | bytes 49160 | tf_op jit(solution)/shard_map/ppermute | solution.py:176
  59.4 1.0 copy-start.4
  63.7 25.4 %copy-start.5 = (bf16[128,512]{1,0:T(8,128)(2,1)S(1)}, bf16[128,512]{1,0:T(8,128)(2,1)}, u32[]{:S(2)}) copy-start(bf16[128,512]{1,0:T(8,128)(2,1)} %c_ref.1) | copy-start | bytes 393220
  63.7 25.4 %all-to-all-start.1 = ((bf16[8,128,512]{2,1,0:T(8,128)(2,1)}), bf16[8,128,512]{2,1,0:T(8,128)(2,1)S(1)}, u32[]{:S(2)}, u32[]{:S(2)}) async-start(bf16[8,128,512]{2,1,0:T(8,128)(2,1)} %copy-done.3), calls=%async_computation.1 | async-start | bytes 2097152 | tf_op jit(solution)/shard_map/all_to_all | solution.py:48
  67.7 16.8 %collective-permute-start.8 = (bf16[16,512]{1,0:T(8,128)(2,1)S(1)}, bf16[16,512]{1,0:T(8,128)(2,1)S(1)}, u32[]{:S(2)}, u32[]{:S(2)}) collective-permute-start(bf16[16,512]{1,0:T(8,128)(2,1)S(1)} %get-tuple-element.23._.refs_0_), channel_id=1, source_target_pairs={{0,128},{128,256},{256,384},{384,0},{1,129},{129,257},{257,385},{3... | collective-permute-start | bytes 49160 | tf_op jit(solution)/shard_map/ppermute | solution.py:176
  71.7 12.8 %collective-permute-start.9 = (bf16[16,512]{1,0:T(8,128)(2,1)S(1)}, bf16[16,512]{1,0:T(8,128)(2,1)S(1)}, u32[]{:S(2)}, u32[]{:S(2)}) collective-permute-start(bf16[16,512]{1,0:T(8,128)(2,1)S(1)} %get-tuple-element.23._.refs_0_), channel_id=1, source_target_pairs={{0,256},{128,384},{256,0},{384,128},{1,257},{129,385},{257,1},{385... | collective-permute-start | bytes 49160 | tf_op jit(solution)/shard_map/ppermute | solution.py:176
  80.8 6.5 %collective-permute-start.10 = (bf16[16,512]{1,0:T(8,128)(2,1)S(1)}, bf16[16,512]{1,0:T(8,128)(2,1)S(1)}, u32[]{:S(2)}, u32[]{:S(2)}) collective-permute-start(bf16[16,512]{1,0:T(8,128)(2,1)S(1)} %get-tuple-element.23._.refs_0_), channel_id=1, source_target_pairs={{0,384},{128,0},{256,128},{384,256},{1,385},{129,1},{257,129},{385... | collective-permute-start | bytes 49160 | tf_op jit(solution)/shard_map/ppermute | solution.py:176
  90.4 26.4 %all-to-all-start.2 = ((bf16[8,128,512]{2,1,0:T(8,128)(2,1)}), bf16[8,128,512]{2,1,0:T(8,128)(2,1)S(1)}, u32[]{:S(2)}, u32[]{:S(2)}) async-start(bf16[8,128,512]{2,1,0:T(8,128)(2,1)} %copy-done.2), calls=%async_computation.2 | async-start | bytes 2097152 | tf_op jit(solution)/shard_map/all_to_all | solution.py:48
  94.6 10.1 %collective-permute-start.13 = (bf16[4,16,512]{2,1,0:T(8,128)(2,1)S(1)}, bf16[4,16,512]{2,1,0:T(8,128)(2,1)S(1)}, u32[]{:S(2)}, u32[]{:S(2)}) collective-permute-start(bf16[4,16,512]{2,1,0:T(8,128)(2,1)S(1)} %shard_map.108._.refs_0_), channel_id=1, source_target_pairs={{0,32},{32,64},{64,96},{96,0},{1,33},{33,65},{65,97},{97,1},{2,34}... | collective-permute-start | bytes 196616 | tf_op jit(solution)/shard_map/ppermute | solution.py:176
  97.0 8.0 %collective-permute-start.14 = (bf16[4,16,512]{2,1,0:T(8,128)(2,1)S(1)}, bf16[4,16,512]{2,1,0:T(8,128)(2,1)S(1)}, u32[]{:S(2)}, u32[]{:S(2)}) collective-permute-start(bf16[4,16,512]{2,1,0:T(8,128)(2,1)S(1)} %shard_map.108._.refs_0_), channel_id=1, source_target_pairs={{0,64},{32,96},{64,0},{96,32},{1,65},{33,97},{65,1},{97,33},{2,66}... | collective-permute-start | bytes 196616 | tf_op jit(solution)/shard_map/ppermute | solution.py:176
  102.8 7.7 %collective-permute-start.15 = (bf16[4,16,512]{2,1,0:T(8,128)(2,1)S(1)}, bf16[4,16,512]{2,1,0:T(8,128)(2,1)S(1)}, u32[]{:S(2)}, u32[]{:S(2)}) collective-permute-start(bf16[4,16,512]{2,1,0:T(8,128)(2,1)S(1)} %shard_map.108._.refs_0_), channel_id=1, source_target_pairs={{0,96},{32,0},{64,32},{96,64},{1,97},{33,1},{65,33},{97,65},{2,98}... | collective-permute-start | bytes 196616 | tf_op jit(solution)/shard_map/ppermute | solution.py:176
  110.5 14.2 %collective-permute-start.16 = (bf16[4,4,16,512]{3,2,1,0:T(8,128)(2,1)S(1)}, bf16[4,4,16,512]{3,2,1,0:T(8,128)(2,1)}, u32[]{:S(2)}, u32[]{:S(2)}) collective-permute-start(bf16[4,4,16,512]{3,2,1,0:T(8,128)(2,1)S(1)} %shard_map.113.m_ref), channel_id=1, source_target_pairs={{0,16},{16,0},{1,17},{17,1},{2,18},{18,2},{3,19},{19,3},{4,20},{20... | collective-permute-start | bytes 786440 | tf_op jit(solution)/shard_map/ppermute | solution.py:310
  117.2 7.6 %copy-start.1 = (bf16[1,2,512,512]{3,2,1,0:T(8,128)(2,1)S(1)}, bf16[1,2,512,512]{3,2,1,0:T(8,128)(2,1)}, u32[]{:S(2)}) copy-start(bf16[1,2,512,512]{3,2,1,0:T(8,128)(2,1)} %param.10) | copy-start | bytes 3145732
  117.7 9.8 %collective-permute-start.12 = (bf16[256,512]{1,0:T(8,128)(2,1)S(1)}, bf16[256,512]{1,0:T(8,128)(2,1)S(1)}, u32[]{:S(2)}, u32[]{:S(2)}) collective-permute-start(bf16[256,512]{1,0:T(8,128)(2,1)S(1)} %shard_map.112), channel_id=1, source_target_pairs={{0,7},{1,6},{2,5},{3,4},{4,3},{5,2},{6,1},{7,0},{8,15},{9,14},{10,... | collective-permute-start | bytes 786440 | tf_op jit(solution)/shard_map/ppermute | solution.py:54
  119.9 15.7 %collective-permute-start.11 = (bf16[256,512]{1,0:T(8,128)(2,1)S(1)}, bf16[256,512]{1,0:T(8,128)(2,1)S(1)}, u32[]{:S(2)}, u32[]{:S(2)}) collective-permute-start(bf16[256,512]{1,0:T(8,128)(2,1)S(1)} %shard_map.111), channel_id=1, source_target_pairs={{0,7},{1,6},{2,5},{3,4},{4,3},{5,2},{6,1},{7,0},{8,15},{9,14},{10,... | collective-permute-start | bytes 786440 | tf_op jit(solution)/shard_map/ppermute | solution.py:54
  (4 other events, 3.6 us)

commit v5 on v4

--- a/solution.py
+++ b/solution.py
@@ -35,7 +35,7 @@
 
 
 LINES = [
-    [rank(core, z, half * LINE + p) for z in range(NZ) for p in range(LINE)]
+    [rank(core, z, half * LINE + p) for p in range(LINE) for z in range(NZ)]
     for core in range(2)
     for half in range(NY // LINE)
 ]
@@ -61,9 +61,9 @@
         half, _ = place(core_ref[0], y_ref[0])
         loads, stores = [], []
         for j in range(GROUP):
-            turned = half * LINE + j % LINE
+            turned = half * LINE + j // NZ
             for k, at in enumerate((NY - 1 - turned, turned)):
-                block = (j // LINE) * NY + (at + SHIFT * core_ref[0]) % NY
+                block = (j % NZ) * NY + (at + SHIFT * core_ref[0]) % NY
                 cols = pl.ds(pl.multiple_of(block * feat, feat), feat)
                 loads.append(
                     pltpu.make_async_copy(
@@ -96,23 +96,28 @@
     )(core[None], y[None], tokens)
 
 
-def project(x, w_other, w, after):
+def project(x, w_other, w, *after):
     n, rows, feat2 = x.shape
     feat, cols = w.shape
-
-    def kernel(x_ref, wo_ref, w_ref, _, o_ref):
-        for j in range(n):
-            acc = jnp.dot(x_ref[j, :, :feat], wo_ref[...], preferred_element_type=f32)
-            acc += jnp.dot(x_ref[j, :, feat:], w_ref[...], preferred_element_type=f32)
-            o_ref[j] = acc.astype(bf16)
-
-    return pl.pallas_call(
-        kernel,
-        out_shape=jax.ShapeDtypeStruct((n, rows, cols), bf16),
-        in_specs=[VMEM] * 3 + [ANY],
+    step = 256
+
+    def kernel(x_ref, wo_ref, w_ref, *refs):
+        o_ref, both = refs[len(after) :]
+        both[:feat] = wo_ref[...]
+        both[feat:] = w_ref[...]
+        for i in range(n * rows // step):
+            at = slice(i * step, (i + 1) * step)
+            o_ref[at] = jnp.dot(x_ref[at], both[...], preferred_element_type=f32).astype(bf16)
+
+    out = pl.pallas_call(
+        kernel,
+        out_shape=jax.ShapeDtypeStruct((n * rows, cols), bf16),
+        in_specs=[VMEM] * 3 + [ANY] * len(after),
         out_specs=VMEM,
+        scratch_shapes=[pltpu.VMEM((feat2, cols), bf16)],
         compiler_params=PARAMS,
-    )(x, w_other, w, after)
+    )(x.reshape(n * rows, feat2), w_other, w, *after)
+    return out.reshape(n, rows, cols)
 
 
 def gate(parts, cotangent, after):
@@ -202,11 +207,12 @@
     return call(kernel, out, [fragments, away], [due, core, x])
 
 
-def z_terms(mine, away, z):
+def z_terms(mine, away, z, w):
     nz, own, cols = mine.shape
 
     def kernel(z_ref, m_ref, *refs):
-        ins, outs = refs[: len(away)], refs[len(away) :]
+        ins, outs = refs[: len(away)], refs[len(away) + 1 :]
+        outs[nz][...] = refs[len(away)][...]
         for k in range(nz):
             at = (z_ref[0] + k) % nz
             term = m_ref[at]
@@ -214,8 +220,8 @@
                 term += ref[at].astype(f32)
             outs[k][...] = term.astype(outs[k].dtype)
 
-    out = [((own, cols), f32)] + [((own, cols), bf16)] * (nz - 1)
-    return call(kernel, out, [mine, *away], [z])
+    out = [((own, cols), f32)] + [((own, cols), bf16)] * (nz - 1) + [(w.shape, bf16)]
+    return call(kernel, out, [mine, *away, w], [z])
 
 
 def update(mine, away, outer, moment, due, rate, count):
@@ -297,10 +303,11 @@
     local = fragments.reshape((NFRAG, *sizes, feat // nrep, cols))
     away = lax.ppermute(first_terms(local, due, core), "c", SWAP)
     mine, *sent = x_terms(local, away, due, core, xx)
-    mine, *sent = z_terms(mine, shifts(sent, "x"), zh)
-    new_outer, new_momentum, half = update(mine, shifts(sent, "zh"), outer_params, momentum, due, rate, nrep)
-
-    parts = swap_line(project(x, w_other, w, half))
+    mine, *sent, w = z_terms(mine, shifts(sent, "x"), zh, w)
+    got = shifts(sent, "zh")
+    parts = swap_line(project(x, w_other, w, *got))
+    new_outer, new_momentum, half = update(mine, got, outer_params, momentum, due, rate, nrep)
+
     line = z_rows(half, shifts([half] * 3, "zh"), zh)
     grads = swap_line(gate(parts, cotangent, line)).reshape(GROUP * rows, cols)
     plane = x_rows(line, shifts([line] * 3, "x"), xx)

time: 138 us -> 139 us (level)
  the two profiles are of different devices: /device:TPU:6 before, /device:TPU:8 now
where the time goes in v5:
time: 139 us; the launch traced here: 138 us
  starting transfers between devices  96.3 us (69%)
  waiting for transfers between devices  24.1 us (17%)
  Pallas kernels  10.9 us (8%)
  local copies, waits for them, and re-layouts  3.63 us (3%)
  between operations  1.71 us (1%)
    ppermute x12, starting transfers between devices, shifts(): lax.ppermute(array, name, [(i, (i + k) % n) for i in range(n)])  58.8 us
    all_to_all x3, starting transfers between devices, swap_line(): lax.all_to_all(array, CHIPS, split_axis=0, concat_axis=0, axis_index_grou...  22 us
    ppermute x12, waiting for transfers between devices, shifts(): lax.ppermute(array, name, [(i, (i + k) % n) for i in range(n)])  11.7 us
    ppermute x3, starting transfers between devices, mirror(): return lax.ppermute(array, CHIPS, MIRROR)  11.7 us
    ppermute x3, waiting for transfers between devices, mirror(): return lax.ppermute(array, CHIPS, MIRROR)  8.2 us
    pallas_call x7, Pallas kernels, call(): pl.pallas_call(kernel, out_shape=[jax.ShapeDtypeStruct(shape, dtype) for...  4.13 us
    unnamed x20, local copies, waits for them, and re-layouts  3.63 us
  transfers between devices with their start and end apart: 20, of which 10 were waited for; matrix products, arithmetic and copies ran while one was open for 0% of the time, Pallas kernels for 4%

profile of v5, /device:TPU:8, one launch (start us, length us, event | category | flops | bytes accessed | tf_op | source)
XLA Modules:
  0.0 137.6 jit_solution(6581509540621403756)
XLA Ops:
  0.6 2.6 %shard_map.102 = bf16[8,128,1024]{2,1,0:T(8,128)(2,1)} custom-call(s32[1]{0:T(128)} %bitcast.core_ref, s32[1]{0:T(128)} %bitcast.1.y_ref, bf16[128,8192]{1,0:T(8,128)(2,1)} %t_ref.1), custom_call_target="tpu_custom_call" | custom-call | tf_op jit(solution)/shard_map/pallas_call | solution.py:85
  3.3 9.5 %all-to-all-start = ((bf16[8,128,1024]{2,1,0:T(8,128)(2,1)}), bf16[8,128,1024]{2,1,0:T(8,128)(2,1)S(1)}, u32[]{:S(2)}, u32[]{:S(2)}) async-start(bf16[8,128,1024]{2,1,0:T(8,128)(2,1)} %shard_map.102), calls=%async_computation | async-start | bytes 4194304 | tf_op jit(solution)/shard_map/all_to_all | solution.py:48
  12.8 2.8 %collective-permute-start = (bf16[512,512]{1,0:T(8,128)(2,1)}, bf16[512,512]{1,0:T(8,128)(2,1)}, u32[]{:S(2)}, u32[]{:S(2)}) collective-permute-start(bf16[512,512]{1,0:T(8,128)(2,1)} %bitcast.30), channel_id=1, source_target_pairs={{0,7},{1,6},{2,5},{3,4},{4,3},{5,2},{6,1},{7,0},{8,15},{9,14},{10,... | collective-permute-start | bytes 1572872 | tf_op jit(solution)/shard_map/ppermute | solution.py:54
  21.3 3.4 %collective-permute-start.2 = (bf16[4,16,512]{2,1,0:T(8,128)(2,1)}, bf16[4,16,512]{2,1,0:T(8,128)(2,1)S(1)}, u32[]{:S(2)}, u32[]{:S(2)}) collective-permute-start(bf16[4,16,512]{2,1,0:T(8,128)(2,1)} %get-tuple-element.17), channel_id=1, source_target_pairs={{0,32},{32,64},{64,96},{96,0},{1,33},{33,65},{65,97},{97,1},{2,34}... | collective-permute-start | bytes 196616 | tf_op jit(solution)/shard_map/ppermute | solution.py:181
  24.7 4.6 %collective-permute-start.3 = (bf16[4,16,512]{2,1,0:T(8,128)(2,1)}, bf16[4,16,512]{2,1,0:T(8,128)(2,1)S(1)}, u32[]{:S(2)}, u32[]{:S(2)}) collective-permute-start(bf16[4,16,512]{2,1,0:T(8,128)(2,1)} %get-tuple-element.18), channel_id=1, source_target_pairs={{0,64},{32,96},{64,0},{96,32},{1,65},{33,97},{65,1},{97,33},{2,66}... | collective-permute-start | bytes 196616 | tf_op jit(solution)/shard_map/ppermute | solution.py:181
  29.3 3.3 %collective-permute-start.4 = (bf16[4,16,512]{2,1,0:T(8,128)(2,1)}, bf16[4,16,512]{2,1,0:T(8,128)(2,1)S(1)}, u32[]{:S(2)}, u32[]{:S(2)}) collective-permute-start(bf16[4,16,512]{2,1,0:T(8,128)(2,1)} %get-tuple-element.19), channel_id=1, source_target_pairs={{0,96},{32,0},{64,32},{96,64},{1,97},{33,1},{65,33},{97,65},{2,98}... | collective-permute-start | bytes 196616 | tf_op jit(solution)/shard_map/ppermute | solution.py:181
  32.7 3.0 %collective-permute-done.4.refs_2_ = bf16[4,16,512]{2,1,0:T(8,128)(2,1)S(1)} collective-permute-done((bf16[4,16,512]{2,1,0:T(8,128)(2,1)}, bf16[4,16,512]{2,1,0:T(8,128)(2,1)S(1)}, u32[]{:S(2)}, u32[]{:S(2)}) %collective-permute-start.4) | collective-permute-done | bytes 65568 | tf_op jit(solution)/shard_map/ppermute | solution.py:181
  37.4 6.1 %collective-permute-start.5 = (bf16[16,512]{1,0:T(8,128)(2,1)S(1)}, bf16[16,512]{1,0:T(8,128)(2,1)S(1)}, u32[]{:S(2)}, u32[]{:S(2)}) collective-permute-start(bf16[16,512]{1,0:T(8,128)(2,1)S(1)} %get-tuple-element.21), channel_id=1, source_target_pairs={{0,128},{128,256},{256,384},{384,0},{1,129},{129,257},{257,385},{3... | collective-permute-start | bytes 49160 | tf_op jit(solution)/shard_map/ppermute | solution.py:181
  43.5 8.7 %collective-permute-start.6 = (bf16[16,512]{1,0:T(8,128)(2,1)S(1)}, bf16[16,512]{1,0:T(8,128)(2,1)S(1)}, u32[]{:S(2)}, u32[]{:S(2)}) collective-permute-start(bf16[16,512]{1,0:T(8,128)(2,1)S(1)} %get-tuple-element.22), channel_id=1, source_target_pairs={{0,256},{128,384},{256,0},{384,128},{1,257},{129,385},{257,1},{385... | collective-permute-start | bytes 49160 | tf_op jit(solution)/shard_map/ppermute | solution.py:181
  52.2 3.7 %collective-permute-start.7 = (bf16[16,512]{1,0:T(8,128)(2,1)S(1)}, bf16[16,512]{1,0:T(8,128)(2,1)S(1)}, u32[]{:S(2)}, u32[]{:S(2)}) collective-permute-start(bf16[16,512]{1,0:T(8,128)(2,1)S(1)} %get-tuple-element.23), channel_id=1, source_target_pairs={{0,384},{128,0},{256,128},{384,256},{1,385},{129,1},{257,129},{385... | collective-permute-start | bytes 49160 | tf_op jit(solution)/shard_map/ppermute | solution.py:181
  55.9 2.8 %collective-permute-done.7.refs_2_ = bf16[16,512]{1,0:T(8,128)(2,1)S(1)} collective-permute-done((bf16[16,512]{1,0:T(8,128)(2,1)S(1)}, bf16[16,512]{1,0:T(8,128)(2,1)S(1)}, u32[]{:S(2)}, u32[]{:S(2)}) %collective-permute-start.7) | collective-permute-done | bytes 16416 | tf_op jit(solution)/shard_map/ppermute | solution.py:181
  62.1 6.8 %all-to-all-start.1 = ((bf16[8,128,512]{2,1,0:T(8,128)(2,1)}), bf16[8,128,512]{2,1,0:T(8,128)(2,1)S(1)}, u32[]{:S(2)}, u32[]{:S(2)}) async-start(bf16[8,128,512]{2,1,0:T(8,128)(2,1)} %bitcast.29), calls=%async_computation.1 | async-start | bytes 2097152 | tf_op jit(solution)/shard_map/all_to_all | solution.py:48
  69.6 5.5 %collective-permute-start.8 = (bf16[16,512]{1,0:T(8,128)(2,1)S(1)}, bf16[16,512]{1,0:T(8,128)(2,1)S(1)}, u32[]{:S(2)}, u32[]{:S(2)}) collective-permute-start(bf16[16,512]{1,0:T(8,128)(2,1)S(1)} %get-tuple-element.25.refs_0_), channel_id=1, source_target_pairs={{0,128},{128,256},{256,384},{384,0},{1,129},{129,257},{257,385},{3... | collective-permute-start | bytes 49160 | tf_op jit(solution)/shard_map/ppermute | solution.py:181
  75.2 8.4 %collective-permute-start.9 = (bf16[16,512]{1,0:T(8,128)(2,1)S(1)}, bf16[16,512]{1,0:T(8,128)(2,1)S(1)}, u32[]{:S(2)}, u32[]{:S(2)}) collective-permute-start(bf16[16,512]{1,0:T(8,128)(2,1)S(1)} %get-tuple-element.25.refs_0_), channel_id=1, source_target_pairs={{0,256},{128,384},{256,0},{384,128},{1,257},{129,385},{257,1},{385... | collective-permute-start | bytes 49160 | tf_op jit(solution)/shard_map/ppermute | solution.py:181
  83.6 3.7 %collective-permute-start.10 = (bf16[16,512]{1,0:T(8,128)(2,1)S(1)}, bf16[16,512]{1,0:T(8,128)(2,1)S(1)}, u32[]{:S(2)}, u32[]{:S(2)}) collective-permute-start(bf16[16,512]{1,0:T(8,128)(2,1)S(1)} %get-tuple-element.25.refs_0_), channel_id=1, source_target_pairs={{0,384},{128,0},{256,128},{384,256},{1,385},{129,1},{257,129},{385... | collective-permute-start | bytes 49160 | tf_op jit(solution)/shard_map/ppermute | solution.py:181
  91.4 5.7 %all-to-all-start.2 = ((bf16[8,128,512]{2,1,0:T(8,128)(2,1)}), bf16[8,128,512]{2,1,0:T(8,128)(2,1)S(1)}, u32[]{:S(2)}, u32[]{:S(2)}) async-start(bf16[8,128,512]{2,1,0:T(8,128)(2,1)} %copy-done.2), calls=%async_computation.2 | async-start | bytes 2097152 | tf_op jit(solution)/shard_map/all_to_all | solution.py:48
  97.1 3.4 %collective-permute-start.13 = (bf16[4,16,512]{2,1,0:T(8,128)(2,1)S(1)}, bf16[4,16,512]{2,1,0:T(8,128)(2,1)S(1)}, u32[]{:S(2)}, u32[]{:S(2)}) collective-permute-start(bf16[4,16,512]{2,1,0:T(8,128)(2,1)S(1)} %shard_map.108._.refs_0_), channel_id=1, source_target_pairs={{0,32},{32,64},{64,96},{96,0},{1,33},{33,65},{65,97},{97,1},{2,34}... | collective-permute-start | bytes 196616 | tf_op jit(solution)/shard_map/ppermute | solution.py:181
  100.5 4.6 %collective-permute-start.14 = (bf16[4,16,512]{2,1,0:T(8,128)(2,1)S(1)}, bf16[4,16,512]{2,1,0:T(8,128)(2,1)S(1)}, u32[]{:S(2)}, u32[]{:S(2)}) collective-permute-start(bf16[4,16,512]{2,1,0:T(8,128)(2,1)S(1)} %shard_map.108._.refs_0_), channel_id=1, source_target_pairs={{0,64},{32,96},{64,0},{96,32},{1,65},{33,97},{65,1},{97,33},{2,66}... | collective-permute-start | bytes 196616 | tf_op jit(solution)/shard_map/ppermute | solution.py:181
  105.2 3.4 %collective-permute-start.15 = (bf16[4,16,512]{2,1,0:T(8,128)(2,1)S(1)}, bf16[4,16,512]{2,1,0:T(8,128)(2,1)S(1)}, u32[]{:S(2)}, u32[]{:S(2)}) collective-permute-start(bf16[4,16,512]{2,1,0:T(8,128)(2,1)S(1)} %shard_map.108._.refs_0_), channel_id=1, source_target_pairs={{0,96},{32,0},{64,32},{96,64},{1,97},{33,1},{65,33},{97,65},{2,98}... | collective-permute-start | bytes 196616 | tf_op jit(solution)/shard_map/ppermute | solution.py:181
  108.6 2.9 %collective-permute-done.15.refs_3_ = bf16[4,16,512]{2,1,0:T(8,128)(2,1)S(1)} collective-permute-done((bf16[4,16,512]{2,1,0:T(8,128)(2,1)S(1)}, bf16[4,16,512]{2,1,0:T(8,128)(2,1)S(1)}, u32[]{:S(2)}, u32[]{:S(2)}) %collective-permute-start.15) | collective-permute-done | bytes 65568 | tf_op jit(solution)/shard_map/ppermute | solution.py:181
  116.9 4.5 %collective-permute-start.12 = (bf16[256,512]{1,0:T(8,128)(2,1)S(1)}, bf16[256,512]{1,0:T(8,128)(2,1)S(1)}, u32[]{:S(2)}, u32[]{:S(2)}) collective-permute-start(bf16[256,512]{1,0:T(8,128)(2,1)S(1)} %shard_map.112), channel_id=1, source_target_pairs={{0,7},{1,6},{2,5},{3,4},{4,3},{5,2},{6,1},{7,0},{8,15},{9,14},{10,... | collective-permute-start | bytes 786440 | tf_op jit(solution)/shard_map/ppermute | solution.py:54
  121.4 4.3 %collective-permute-start.11 = (bf16[256,512]{1,0:T(8,128)(2,1)S(1)}, bf16[256,512]{1,0:T(8,128)(2,1)S(1)}, u32[]{:S(2)}, u32[]{:S(2)}) collective-permute-start(bf16[256,512]{1,0:T(8,128)(2,1)S(1)} %shard_map.111), channel_id=1, source_target_pairs={{0,7},{1,6},{2,5},{3,4},{4,3},{5,2},{6,1},{7,0},{8,15},{9,14},{10,... | collective-permute-start | bytes 786440 | tf_op jit(solution)/shard_map/ppermute | solution.py:54
  128.5 2.6 %collective-permute-done.12 = bf16[256,512]{1,0:T(8,128)(2,1)S(1)} collective-permute-done((bf16[256,512]{1,0:T(8,128)(2,1)S(1)}, bf16[256,512]{1,0:T(8,128)(2,1)S(1)}, u32[]{:S(2)}, u32[]{:S(2)}) %collective-permute-start.12) | collective-permute-done | bytes 262176 | tf_op jit(solution)/shard_map/ppermute | solution.py:54
  131.1 5.6 %collective-permute-done.11 = bf16[256,512]{1,0:T(8,128)(2,1)S(1)} collective-permute-done((bf16[256,512]{1,0:T(8,128)(2,1)S(1)}, bf16[256,512]{1,0:T(8,128)(2,1)S(1)}, u32[]{:S(2)}, u32[]{:S(2)}) %collective-permute-start.11) | collective-permute-done | bytes 262176 | tf_op jit(solution)/shard_map/ppermute | solution.py:54
  (50 shorter events, 23.9 us)
Async XLA Ops:
  3.3 13.0 %copy-start = (bf16[1,2,512,512]{3,2,1,0:T(8,128)(2,1)S(1)}, bf16[1,2,512,512]{3,2,1,0:T(8,128)(2,1)}, u32[]{:S(2)}) copy-start(bf16[1,2,512,512]{3,2,1,0:T(8,128)(2,1)} %param.10) | copy-start | bytes 3145732
  3.3 55.5 %all-to-all-start = ((bf16[8,128,1024]{2,1,0:T(8,128)(2,1)}), bf16[8,128,1024]{2,1,0:T(8,128)(2,1)S(1)}, u32[]{:S(2)}, u32[]{:S(2)}) async-start(bf16[8,128,1024]{2,1,0:T(8,128)(2,1)} %shard_map.102), calls=%async_computation | async-start | bytes 4194304 | tf_op jit(solution)/shard_map/all_to_all | solution.py:48
  12.8 46.0 %collective-permute-start = (bf16[512,512]{1,0:T(8,128)(2,1)}, bf16[512,512]{1,0:T(8,128)(2,1)}, u32[]{:S(2)}, u32[]{:S(2)}) collective-permute-start(bf16[512,512]{1,0:T(8,128)(2,1)} %bitcast.30), channel_id=1, source_target_pairs={{0,7},{1,6},{2,5},{3,4},{4,3},{5,2},{6,1},{7,0},{8,15},{9,14},{10,... | collective-permute-start | bytes 1572872 | tf_op jit(solution)/shard_map/ppermute | solution.py:54
  17.0 3.6 %collective-permute-start.1 = (bf16[4,4,16,512]{3,2,1,0:T(8,128)(2,1)}, bf16[4,4,16,512]{3,2,1,0:T(8,128)(2,1)S(1)}, u32[]{:S(2)}, u32[]{:S(2)}) collective-permute-start(bf16[4,4,16,512]{3,2,1,0:T(8,128)(2,1)} %shard_map.103), channel_id=1, source_target_pairs={{0,16},{16,0},{1,17},{17,1},{2,18},{18,2},{3,19},{19,3},{4,20},{20... | collective-permute-start | bytes 786440 | tf_op jit(solution)/shard_map/ppermute | solution.py:304
  21.3 11.4 %collective-permute-start.2 = (bf16[4,16,512]{2,1,0:T(8,128)(2,1)}, bf16[4,16,512]{2,1,0:T(8,128)(2,1)S(1)}, u32[]{:S(2)}, u32[]{:S(2)}) collective-permute-start(bf16[4,16,512]{2,1,0:T(8,128)(2,1)} %get-tuple-element.17), channel_id=1, source_target_pairs={{0,32},{32,64},{64,96},{96,0},{1,33},{33,65},{65,97},{97,1},{2,34}... | collective-permute-start | bytes 196616 | tf_op jit(solution)/shard_map/ppermute | solution.py:181
  24.7 8.0 %collective-permute-start.3 = (bf16[4,16,512]{2,1,0:T(8,128)(2,1)}, bf16[4,16,512]{2,1,0:T(8,128)(2,1)S(1)}, u32[]{:S(2)}, u32[]{:S(2)}) collective-permute-start(bf16[4,16,512]{2,1,0:T(8,128)(2,1)} %get-tuple-element.18), channel_id=1, source_target_pairs={{0,64},{32,96},{64,0},{96,32},{1,65},{33,97},{65,1},{97,33},{2,66}... | collective-permute-start | bytes 196616 | tf_op jit(solution)/shard_map/ppermute | solution.py:181
  29.3 6.4 %collective-permute-start.4 = (bf16[4,16,512]{2,1,0:T(8,128)(2,1)}, bf16[4,16,512]{2,1,0:T(8,128)(2,1)S(1)}, u32[]{:S(2)}, u32[]{:S(2)}) collective-permute-start(bf16[4,16,512]{2,1,0:T(8,128)(2,1)} %get-tuple-element.19), channel_id=1, source_target_pairs={{0,96},{32,0},{64,32},{96,64},{1,97},{33,1},{65,33},{97,65},{2,98}... | collective-permute-start | bytes 196616 | tf_op jit(solution)/shard_map/ppermute | solution.py:181
  37.4 18.4 %collective-permute-start.5 = (bf16[16,512]{1,0:T(8,128)(2,1)S(1)}, bf16[16,512]{1,0:T(8,128)(2,1)S(1)}, u32[]{:S(2)}, u32[]{:S(2)}) collective-permute-start(bf16[16,512]{1,0:T(8,128)(2,1)S(1)} %get-tuple-element.21), channel_id=1, source_target_pairs={{0,128},{128,256},{256,384},{384,0},{1,129},{129,257},{257,385},{3... | collective-permute-start | bytes 49160 | tf_op jit(solution)/shard_map/ppermute | solution.py:181
  43.5 12.3 %collective-permute-start.6 = (bf16[16,512]{1,0:T(8,128)(2,1)S(1)}, bf16[16,512]{1,0:T(8,128)(2,1)S(1)}, u32[]{:S(2)}, u32[]{:S(2)}) collective-permute-start(bf16[16,512]{1,0:T(8,128)(2,1)S(1)} %get-tuple-element.22), channel_id=1, source_target_pairs={{0,256},{128,384},{256,0},{384,128},{1,257},{129,385},{257,1},{385... | collective-permute-start | bytes 49160 | tf_op jit(solution)/shard_map/ppermute | solution.py:181
  52.2 6.5 %collective-permute-start.7 = (bf16[16,512]{1,0:T(8,128)(2,1)S(1)}, bf16[16,512]{1,0:T(8,128)(2,1)S(1)}, u32[]{:S(2)}, u32[]{:S(2)}) collective-permute-start(bf16[16,512]{1,0:T(8,128)(2,1)S(1)} %get-tuple-element.23), channel_id=1, source_target_pairs={{0,384},{128,0},{256,128},{384,256},{1,385},{129,1},{257,129},{385... | collective-permute-start | bytes 49160 | tf_op jit(solution)/shard_map/ppermute | solution.py:181
  62.0 6.9 %copy-start.9 = (f32[16,512]{1,0:T(8,128)S(1)}, f32[16,512]{1,0:T(8,128)}, u32[]{:S(2)}) copy-start(f32[16,512]{1,0:T(8,128)} %copy-done.8) | copy-start | bytes 98308
  62.0 28.2 %copy-start.5 = (bf16[128,512]{1,0:T(8,128)(2,1)S(1)}, bf16[128,512]{1,0:T(8,128)(2,1)}, u32[]{:S(2)}) copy-start(bf16[128,512]{1,0:T(8,128)(2,1)} %c_ref.1) | copy-start | bytes 393220
  62.1 28.2 %all-to-all-start.1 = ((bf16[8,128,512]{2,1,0:T(8,128)(2,1)}), bf16[8,128,512]{2,1,0:T(8,128)(2,1)S(1)}, u32[]{:S(2)}, u32[]{:S(2)}) async-start(bf16[8,128,512]{2,1,0:T(8,128)(2,1)} %bitcast.29), calls=%async_computation.1 | async-start | bytes 2097152 | tf_op jit(solution)/shard_map/all_to_all | solution.py:48
  69.6 19.0 %collective-permute-start.8 = (bf16[16,512]{1,0:T(8,128)(2,1)S(1)}, bf16[16,512]{1,0:T(8,128)(2,1)S(1)}, u32[]{:S(2)}, u32[]{:S(2)}) collective-permute-start(bf16[16,512]{1,0:T(8,128)(2,1)S(1)} %get-tuple-element.25.refs_0_), channel_id=1, source_target_pairs={{0,128},{128,256},{256,384},{384,0},{1,129},{129,257},{257,385},{3... | collective-permute-start | bytes 49160 | tf_op jit(solution)/shard_map/ppermute | solution.py:181
  75.2 14.2 %collective-permute-start.9 = (bf16[16,512]{1,0:T(8,128)(2,1)S(1)}, bf16[16,512]{1,0:T(8,128)(2,1)S(1)}, u32[]{:S(2)}, u32[]{:S(2)}) collective-permute-start(bf16[16,512]{1,0:T(8,128)(2,1)S(1)} %get-tuple-element.25.refs_0_), channel_id=1, source_target_pairs={{0,256},{128,384},{256,0},{384,128},{1,257},{129,385},{257,1},{385... | collective-permute-start | bytes 49160 | tf_op jit(solution)/shard_map/ppermute | solution.py:181
  83.6 6.6 %collective-permute-start.10 = (bf16[16,512]{1,0:T(8,128)(2,1)S(1)}, bf16[16,512]{1,0:T(8,128)(2,1)S(1)}, u32[]{:S(2)}, u32[]{:S(2)}) collective-permute-start(bf16[16,512]{1,0:T(8,128)(2,1)S(1)} %get-tuple-element.25.refs_0_), channel_id=1, source_target_pairs={{0,384},{128,0},{256,128},{384,256},{1,385},{129,1},{257,129},{385... | collective-permute-start | bytes 49160 | tf_op jit(solution)/shard_map/ppermute | solution.py:181
  91.4 24.5 %all-to-all-start.2 = ((bf16[8,128,512]{2,1,0:T(8,128)(2,1)}), bf16[8,128,512]{2,1,0:T(8,128)(2,1)S(1)}, u32[]{:S(2)}, u32[]{:S(2)}) async-start(bf16[8,128,512]{2,1,0:T(8,128)(2,1)} %copy-done.2), calls=%async_computation.2 | async-start | bytes 2097152 | tf_op jit(solution)/shard_map/all_to_all | solution.py:48
  97.1 11.4 %collective-permute-start.13 = (bf16[4,16,512]{2,1,0:T(8,128)(2,1)S(1)}, bf16[4,16,512]{2,1,0:T(8,128)(2,1)S(1)}, u32[]{:S(2)}, u32[]{:S(2)}) collective-permute-start(bf16[4,16,512]{2,1,0:T(8,128)(2,1)S(1)} %shard_map.108._.refs_0_), channel_id=1, source_target_pairs={{0,32},{32,64},{64,96},{96,0},{1,33},{33,65},{65,97},{97,1},{2,34}... | collective-permute-start | bytes 196616 | tf_op jit(solution)/shard_map/ppermute | solution.py:181
  100.5 8.1 %collective-permute-start.14 = (bf16[4,16,512]{2,1,0:T(8,128)(2,1)S(1)}, bf16[4,16,512]{2,1,0:T(8,128)(2,1)S(1)}, u32[]{:S(2)}, u32[]{:S(2)}) collective-permute-start(bf16[4,16,512]{2,1,0:T(8,128)(2,1)S(1)} %shard_map.108._.refs_0_), channel_id=1, source_target_pairs={{0,64},{32,96},{64,0},{96,32},{1,65},{33,97},{65,1},{97,33},{2,66}... | collective-permute-start | bytes 196616 | tf_op jit(solution)/shard_map/ppermute | solution.py:181
  105.2 6.3 %collective-permute-start.15 = (bf16[4,16,512]{2,1,0:T(8,128)(2,1)S(1)}, bf16[4,16,512]{2,1,0:T(8,128)(2,1)S(1)}, u32[]{:S(2)}, u32[]{:S(2)}) collective-permute-start(bf16[4,16,512]{2,1,0:T(8,128)(2,1)S(1)} %shard_map.108._.refs_0_), channel_id=1, source_target_pairs={{0,96},{32,0},{64,32},{96,64},{1,97},{33,1},{65,33},{97,65},{2,98}... | collective-permute-start | bytes 196616 | tf_op jit(solution)/shard_map/ppermute | solution.py:181
  111.5 14.2 %collective-permute-start.16 = (bf16[4,4,16,512]{3,2,1,0:T(8,128)(2,1)S(1)}, bf16[4,4,16,512]{3,2,1,0:T(8,128)(2,1)}, u32[]{:S(2)}, u32[]{:S(2)}) collective-permute-start(bf16[4,4,16,512]{3,2,1,0:T(8,128)(2,1)S(1)} %shard_map.113.m_ref), channel_id=1, source_target_pairs={{0,16},{16,0},{1,17},{17,1},{2,18},{18,2},{3,19},{19,3},{4,20},{20... | collective-permute-start | bytes 786440 | tf_op jit(solution)/shard_map/ppermute | solution.py:317
  116.4 9.4 %copy-start.1 = (bf16[1,2,512,512]{3,2,1,0:T(8,128)(2,1)S(1)}, bf16[1,2,512,512]{3,2,1,0:T(8,128)(2,1)}, u32[]{:S(2)}) copy-start(bf16[1,2,512,512]{3,2,1,0:T(8,128)(2,1)} %param.10) | copy-start | bytes 3145732
  116.9 14.2 %collective-permute-start.12 = (bf16[256,512]{1,0:T(8,128)(2,1)S(1)}, bf16[256,512]{1,0:T(8,128)(2,1)S(1)}, u32[]{:S(2)}, u32[]{:S(2)}) collective-permute-start(bf16[256,512]{1,0:T(8,128)(2,1)S(1)} %shard_map.112), channel_id=1, source_target_pairs={{0,7},{1,6},{2,5},{3,4},{4,3},{5,2},{6,1},{7,0},{8,15},{9,14},{10,... | collective-permute-start | bytes 786440 | tf_op jit(solution)/shard_map/ppermute | solution.py:54
  121.4 15.2 %collective-permute-start.11 = (bf16[256,512]{1,0:T(8,128)(2,1)S(1)}, bf16[256,512]{1,0:T(8,128)(2,1)S(1)}, u32[]{:S(2)}, u32[]{:S(2)}) collective-permute-start(bf16[256,512]{1,0:T(8,128)(2,1)S(1)} %shard_map.111), channel_id=1, source_target_pairs={{0,7},{1,6},{2,5},{3,4},{4,3},{5,2},{6,1},{7,0},{8,15},{9,14},{10,... | collective-permute-start | bytes 786440 | tf_op jit(solution)/shard_map/ppermute | solution.py:54
  (6 other events, 17.4 us)

commit v6 on v5

--- a/solution.py
+++ b/solution.py
@@ -35,7 +35,7 @@
 
 
 LINES = [
-    [rank(core, z, half * LINE + p) for p in range(LINE) for z in range(NZ)]
+    [rank(core, z, half * LINE + p) for z in range(NZ) for p in range(LINE)]
     for core in range(2)
     for half in range(NY // LINE)
 ]
@@ -61,9 +61,9 @@
         half, _ = place(core_ref[0], y_ref[0])
         loads, stores = [], []
         for j in range(GROUP):
-            turned = half * LINE + j // NZ
+            turned = half * LINE + j % LINE
             for k, at in enumerate((NY - 1 - turned, turned)):
-                block = (j % NZ) * NY + (at + SHIFT * core_ref[0]) % NY
+                block = (j // LINE) * NY + (at + SHIFT * core_ref[0]) % NY
                 cols = pl.ds(pl.multiple_of(block * feat, feat), feat)
                 loads.append(
                     pltpu.make_async_copy(
@@ -96,13 +96,12 @@
     )(core[None], y[None], tokens)
 
 
-def project(x, w_other, w, *after):
+def project(x, w_other, w, after):
     n, rows, feat2 = x.shape
     feat, cols = w.shape
     step = 256
 
-    def kernel(x_ref, wo_ref, w_ref, *refs):
-        o_ref, both = refs[len(after) :]
+    def kernel(x_ref, wo_ref, w_ref, _, o_ref, both):
         both[:feat] = wo_ref[...]
         both[feat:] = w_ref[...]
         for i in range(n * rows // step):
@@ -112,11 +111,11 @@
     out = pl.pallas_call(
         kernel,
         out_shape=jax.ShapeDtypeStruct((n * rows, cols), bf16),
-        in_specs=[VMEM] * 3 + [ANY] * len(after),
+        in_specs=[VMEM] * 3 + [ANY],
         out_specs=VMEM,
         scratch_shapes=[pltpu.VMEM((feat2, cols), bf16)],
         compiler_params=PARAMS,
-    )(x.reshape(n * rows, feat2), w_other, w, *after)
+    )(x.reshape(n * rows, feat2), w_other, w, after)
     return out.reshape(n, rows, cols)
 
 
@@ -193,10 +192,11 @@
     return call(kernel, [((nz, nx, own, cols), bf16)], [fragments], [due, core])[0]
 
 
-def x_terms(fragments, away, due, core, x):
+def x_terms(fragments, away, due, core, x, *ahead):
     nz, nx, nc, own, cols = fragments.shape[1:]
 
-    def kernel(due_ref, core_ref, x_ref, f_ref, a_ref, *outs):
+    def kernel(due_ref, core_ref, x_ref, f_ref, a_ref, *refs):
+        outs = refs[len(ahead) :]
         for k in range(nx):
             at = (x_ref[0] + k) % nx
             for i in range(nz):
@@ -204,7 +204,7 @@
                 outs[k][i] = term.astype(outs[k].dtype)
 
     out = [((nz, own, cols), f32)] + [((nz, own, cols), bf16)] * (nx - 1)
-    return call(kernel, out, [fragments, away], [due, core, x])
+    return call(kernel, out, [fragments, away, *ahead], [due, core, x])
 
 
 def z_terms(mine, away, z, w):
@@ -302,12 +302,11 @@
     nrep = sizes[0] * sizes[1] * sizes[2]
     local = fragments.reshape((NFRAG, *sizes, feat // nrep, cols))
     away = lax.ppermute(first_terms(local, due, core), "c", SWAP)
-    mine, *sent = x_terms(local, away, due, core, xx)
+    mine, *sent = x_terms(local, away, due, core, xx, outer_params, momentum)
     mine, *sent, w = z_terms(mine, shifts(sent, "x"), zh, w)
-    got = shifts(sent, "zh")
-    parts = swap_line(project(x, w_other, w, *got))
-    new_outer, new_momentum, half = update(mine, got, outer_params, momentum, due, rate, nrep)
-
+    new_outer, new_momentum, half = update(mine, shifts(sent, "zh"), outer_params, momentum, due, rate, nrep)
+
+    parts = swap_line(project(x, w_other, w, half))
     line = z_rows(half, shifts([half] * 3, "zh"), zh)
     grads = swap_line(gate(parts, cotangent, line)).reshape(GROUP * rows, cols)
     plane = x_rows(line, shifts([line] * 3, "x"), xx)

time: 139 us -> 139 us (level)
  the two profiles are of different devices: /device:TPU:8 before, /device:TPU:6 now
where the time goes in v6:
time: 139 us; the launch traced here: 138 us
  starting transfers between devices  85.5 us (62%)
  waiting for transfers between devices  34.6 us (25%)
  Pallas kernels  10.9 us (8%)
  local copies, waits for them, and re-layouts  4.58 us (3%)
  between operations  1.7 us (1%)
    ppermute x12, starting transfers between devices, shifts(): lax.ppermute(array, name, [(i, (i + k) % n) for i in range(n)])  50.4 us
    ppermute x12, waiting for transfers between devices, shifts(): lax.ppermute(array, name, [(i, (i + k) % n) for i in range(n)])  17.4 us
    all_to_all x3, starting transfers between devices, swap_line(): lax.all_to_all(array, CHIPS, split_axis=0, concat_axis=0, axis_index_grou...  17 us
    ppermute x3, starting transfers between devices, mirror(): return lax.ppermute(array, CHIPS, MIRROR)  12.6 us
    ppermute x3, waiting for transfers between devices, mirror(): return lax.ppermute(array, CHIPS, MIRROR)  7.95 us
    all_to_all x3, waiting for transfers between devices, swap_line(): lax.all_to_all(array, CHIPS, split_axis=0, concat_axis=0, axis_index_grou...  7.5 us
    unnamed x20, local copies, waits for them, and re-layouts  4.58 us
    pallas_call x7, Pallas kernels, call(): pl.pallas_call(kernel, out_shape=[jax.ShapeDtypeStruct(shape, dtype) for...  4.12 us
  transfers between devices with their start and end apart: 20, of which 10 were waited for; matrix products, arithmetic and copies ran while one was open for 0% of the time, Pallas kernels for 4%

profile of v6, /device:TPU:6, one launch (start us, length us, event | category | flops | bytes accessed | tf_op | source)
XLA Modules:
  0.0 138.2 jit_solution(13838745690566099333)
XLA Ops:
  0.6 2.6 %shard_map.102 = bf16[8,128,1024]{2,1,0:T(8,128)(2,1)} custom-call(s32[1]{0:T(128)} %bitcast.core_ref, s32[1]{0:T(128)} %bitcast.1.y_ref, bf16[128,8192]{1,0:T(8,128)(2,1)} %t_ref.1), custom_call_target="tpu_custom_call" | custom-call | tf_op jit(solution)/shard_map/pallas_call | solution.py:85
  3.3 6.8 %all-to-all-start = ((bf16[8,128,1024]{2,1,0:T(8,128)(2,1)}), bf16[8,128,1024]{2,1,0:T(8,128)(2,1)S(1)}, u32[]{:S(2)}, u32[]{:S(2)}) async-start(bf16[8,128,1024]{2,1,0:T(8,128)(2,1)} %shard_map.102), calls=%async_computation | async-start | bytes 4194304 | tf_op jit(solution)/shard_map/all_to_all | solution.py:48
  10.1 5.6 %collective-permute-start = (bf16[512,512]{1,0:T(8,128)(2,1)}, bf16[512,512]{1,0:T(8,128)(2,1)}, u32[]{:S(2)}, u32[]{:S(2)}) collective-permute-start(bf16[512,512]{1,0:T(8,128)(2,1)} %bitcast.30), channel_id=1, source_target_pairs={{0,7},{1,6},{2,5},{3,4},{4,3},{5,2},{6,1},{7,0},{8,15},{9,14},{10,... | collective-permute-start | bytes 1572872 | tf_op jit(solution)/shard_map/ppermute | solution.py:54
  22.1 2.4 %collective-permute-start.2 = (bf16[4,16,512]{2,1,0:T(8,128)(2,1)}, bf16[4,16,512]{2,1,0:T(8,128)(2,1)S(1)}, u32[]{:S(2)}, u32[]{:S(2)}) collective-permute-start(bf16[4,16,512]{2,1,0:T(8,128)(2,1)} %get-tuple-element.17), channel_id=1, source_target_pairs={{0,32},{32,64},{64,96},{96,0},{1,33},{33,65},{65,97},{97,1},{2,34}... | collective-permute-start | bytes 196616 | tf_op jit(solution)/shard_map/ppermute | solution.py:180
  24.5 4.3 %collective-permute-start.3 = (bf16[4,16,512]{2,1,0:T(8,128)(2,1)}, bf16[4,16,512]{2,1,0:T(8,128)(2,1)S(1)}, u32[]{:S(2)}, u32[]{:S(2)}) collective-permute-start(bf16[4,16,512]{2,1,0:T(8,128)(2,1)} %get-tuple-element.18), channel_id=1, source_target_pairs={{0,64},{32,96},{64,0},{96,32},{1,65},{33,97},{65,1},{97,33},{2,66}... | collective-permute-start | bytes 196616 | tf_op jit(solution)/shard_map/ppermute | solution.py:180
  32.4 4.0 %collective-permute-done.4.refs_2_ = bf16[4,16,512]{2,1,0:T(8,128)(2,1)S(1)} collective-permute-done((bf16[4,16,512]{2,1,0:T(8,128)(2,1)}, bf16[4,16,512]{2,1,0:T(8,128)(2,1)S(1)}, u32[]{:S(2)}, u32[]{:S(2)}) %collective-permute-start.4) | collective-permute-done | bytes 65568 | tf_op jit(solution)/shard_map/ppermute | solution.py:180
  38.4 6.1 %collective-permute-start.5 = (bf16[16,512]{1,0:T(8,128)(2,1)S(1)}, bf16[16,512]{1,0:T(8,128)(2,1)S(1)}, u32[]{:S(2)}, u32[]{:S(2)}) collective-permute-start(bf16[16,512]{1,0:T(8,128)(2,1)S(1)} %get-tuple-element.22), channel_id=1, source_target_pairs={{0,128},{128,256},{256,384},{384,0},{1,129},{129,257},{257,385},{3... | collective-permute-start | bytes 49160 | tf_op jit(solution)/shard_map/ppermute | solution.py:180
  44.5 8.7 %collective-permute-start.6 = (bf16[16,512]{1,0:T(8,128)(2,1)S(1)}, bf16[16,512]{1,0:T(8,128)(2,1)S(1)}, u32[]{:S(2)}, u32[]{:S(2)}) collective-permute-start(bf16[16,512]{1,0:T(8,128)(2,1)S(1)} %get-tuple-element.23), channel_id=1, source_target_pairs={{0,256},{128,384},{256,0},{384,128},{1,257},{129,385},{257,1},{385... | collective-permute-start | bytes 49160 | tf_op jit(solution)/shard_map/ppermute | solution.py:180
  53.2 3.7 %collective-permute-start.7 = (bf16[16,512]{1,0:T(8,128)(2,1)S(1)}, bf16[16,512]{1,0:T(8,128)(2,1)S(1)}, u32[]{:S(2)}, u32[]{:S(2)}) collective-permute-start(bf16[16,512]{1,0:T(8,128)(2,1)S(1)} %get-tuple-element.24), channel_id=1, source_target_pairs={{0,384},{128,0},{256,128},{384,256},{1,385},{129,1},{257,129},{385... | collective-permute-start | bytes 49160 | tf_op jit(solution)/shard_map/ppermute | solution.py:180
  56.9 2.8 %collective-permute-done.7.refs_2_ = bf16[16,512]{1,0:T(8,128)(2,1)S(1)} collective-permute-done((bf16[16,512]{1,0:T(8,128)(2,1)S(1)}, bf16[16,512]{1,0:T(8,128)(2,1)S(1)}, u32[]{:S(2)}, u32[]{:S(2)}) %collective-permute-start.7) | collective-permute-done | bytes 16416 | tf_op jit(solution)/shard_map/ppermute | solution.py:180
  60.4 2.3 %shard_map.107 = bf16[1024,512]{1,0:T(8,128)(2,1)S(1)} custom-call(bf16[1024,1024]{1,0:T(8,128)(2,1)S(1)} %bitcast.19, bf16[512,512]{1,0:T(8,128)(2,1)} %collective-permute-done.wo_ref, bf16[512,512]{1,0:T(8,128)(2,1)S(1)} %get-tuple-element.20.w_ref, bf16[16,512]{1,0:T(8,128)(2,1)S(1)} %get-tuple-element.25._.refs_0_), custom_call_target="tpu_custom_call" | custom-call | tf_op jit(solution)/shard_map/pallas_call | solution.py:111
  63.7 4.3 %all-to-all-start.1 = ((bf16[8,128,512]{2,1,0:T(8,128)(2,1)}), bf16[8,128,512]{2,1,0:T(8,128)(2,1)S(1)}, u32[]{:S(2)}, u32[]{:S(2)}) async-start(bf16[8,128,512]{2,1,0:T(8,128)(2,1)} %bitcast.29), calls=%async_computation.1 | async-start | bytes 2097152 | tf_op jit(solution)/shard_map/all_to_all | solution.py:48
  67.9 3.3 %collective-permute-start.8 = (bf16[16,512]{1,0:T(8,128)(2,1)S(1)}, bf16[16,512]{1,0:T(8,128)(2,1)S(1)}, u32[]{:S(2)}, u32[]{:S(2)}) collective-permute-start(bf16[16,512]{1,0:T(8,128)(2,1)S(1)} %get-tuple-element.25._.refs_0_), channel_id=1, source_target_pairs={{0,128},{128,256},{256,384},{384,0},{1,129},{129,257},{257,385},{3... | collective-permute-start | bytes 49160 | tf_op jit(solution)/shard_map/ppermute | solution.py:180
  71.3 8.5 %collective-permute-start.9 = (bf16[16,512]{1,0:T(8,128)(2,1)S(1)}, bf16[16,512]{1,0:T(8,128)(2,1)S(1)}, u32[]{:S(2)}, u32[]{:S(2)}) collective-permute-start(bf16[16,512]{1,0:T(8,128)(2,1)S(1)} %get-tuple-element.25._.refs_0_), channel_id=1, source_target_pairs={{0,256},{128,384},{256,0},{384,128},{1,257},{129,385},{257,1},{385... | collective-permute-start | bytes 49160 | tf_op jit(solution)/shard_map/ppermute | solution.py:180
  79.8 3.7 %collective-permute-start.10 = (bf16[16,512]{1,0:T(8,128)(2,1)S(1)}, bf16[16,512]{1,0:T(8,128)(2,1)S(1)}, u32[]{:S(2)}, u32[]{:S(2)}) collective-permute-start(bf16[16,512]{1,0:T(8,128)(2,1)S(1)} %get-tuple-element.25._.refs_0_), channel_id=1, source_target_pairs={{0,384},{128,0},{256,128},{384,256},{1,385},{129,1},{257,129},{385... | collective-permute-start | bytes 49160 | tf_op jit(solution)/shard_map/ppermute | solution.py:180
  83.5 3.1 %collective-permute-done.10.refs_3_ = bf16[16,512]{1,0:T(8,128)(2,1)S(1)} collective-permute-done((bf16[16,512]{1,0:T(8,128)(2,1)S(1)}, bf16[16,512]{1,0:T(8,128)(2,1)S(1)}, u32[]{:S(2)}, u32[]{:S(2)}) %collective-permute-start.10) | collective-permute-done | bytes 16416 | tf_op jit(solution)/shard_map/ppermute | solution.py:180
  88.6 5.9 %all-to-all-start.2 = ((bf16[8,128,512]{2,1,0:T(8,128)(2,1)}), bf16[8,128,512]{2,1,0:T(8,128)(2,1)S(1)}, u32[]{:S(2)}, u32[]{:S(2)}) async-start(bf16[8,128,512]{2,1,0:T(8,128)(2,1)} %copy-done.2), calls=%async_computation.2 | async-start | bytes 2097152 | tf_op jit(solution)/shard_map/all_to_all | solution.py:48
  94.5 2.4 %collective-permute-start.13 = (bf16[4,16,512]{2,1,0:T(8,128)(2,1)S(1)}, bf16[4,16,512]{2,1,0:T(8,128)(2,1)S(1)}, u32[]{:S(2)}, u32[]{:S(2)}) collective-permute-start(bf16[4,16,512]{2,1,0:T(8,128)(2,1)S(1)} %shard_map.108._.refs_0_), channel_id=1, source_target_pairs={{0,32},{32,64},{64,96},{96,0},{1,33},{33,65},{65,97},{97,1},{2,34}... | collective-permute-start | bytes 196616 | tf_op jit(solution)/shard_map/ppermute | solution.py:180
  96.9 3.6 %collective-permute-start.14 = (bf16[4,16,512]{2,1,0:T(8,128)(2,1)S(1)}, bf16[4,16,512]{2,1,0:T(8,128)(2,1)S(1)}, u32[]{:S(2)}, u32[]{:S(2)}) collective-permute-start(bf16[4,16,512]{2,1,0:T(8,128)(2,1)S(1)} %shard_map.108._.refs_0_), channel_id=1, source_target_pairs={{0,64},{32,96},{64,0},{96,32},{1,65},{33,97},{65,1},{97,33},{2,66}... | collective-permute-start | bytes 196616 | tf_op jit(solution)/shard_map/ppermute | solution.py:180
  104.6 3.7 %collective-permute-done.15.refs_3_ = bf16[4,16,512]{2,1,0:T(8,128)(2,1)S(1)} collective-permute-done((bf16[4,16,512]{2,1,0:T(8,128)(2,1)S(1)}, bf16[4,16,512]{2,1,0:T(8,128)(2,1)S(1)}, u32[]{:S(2)}, u32[]{:S(2)}) %collective-permute-start.15) | collective-permute-done | bytes 65568 | tf_op jit(solution)/shard_map/ppermute | solution.py:180
  108.3 3.5 %collective-permute-start.16 = (bf16[4,4,16,512]{3,2,1,0:T(8,128)(2,1)S(1)}, bf16[4,4,16,512]{3,2,1,0:T(8,128)(2,1)}, u32[]{:S(2)}, u32[]{:S(2)}) collective-permute-start(bf16[4,4,16,512]{3,2,1,0:T(8,128)(2,1)S(1)} %shard_map.113.m_ref), channel_id=1, source_target_pairs={{0,16},{16,0},{1,17},{17,1},{2,18},{18,2},{3,19},{19,3},{4,20},{20... | collective-permute-start | bytes 786440 | tf_op jit(solution)/shard_map/ppermute | solution.py:316
  111.9 6.7 %all-to-all-done.2 = bf16[8,128,512]{2,1,0:T(8,128)(2,1)S(1)} async-done(((bf16[8,128,512]{2,1,0:T(8,128)(2,1)}), bf16[8,128,512]{2,1,0:T(8,128)(2,1)S(1)}, u32[]{:S(2)}, u32[]{:S(2)}) %all-to-all-start.2) | async-done | bytes 1048608 | tf_op jit(solution)/shard_map/all_to_all | solution.py:48
  121.4 5.1 %collective-permute-start.11 = (bf16[256,512]{1,0:T(8,128)(2,1)S(1)}, bf16[256,512]{1,0:T(8,128)(2,1)S(1)}, u32[]{:S(2)}, u32[]{:S(2)}) collective-permute-start(bf16[256,512]{1,0:T(8,128)(2,1)S(1)} %shard_map.111), channel_id=1, source_target_pairs={{0,7},{1,6},{2,5},{3,4},{4,3},{5,2},{6,1},{7,0},{8,15},{9,14},{10,... | collective-permute-start | bytes 786440 | tf_op jit(solution)/shard_map/ppermute | solution.py:54
  129.3 7.9 %collective-permute-done.11 = bf16[256,512]{1,0:T(8,128)(2,1)S(1)} collective-permute-done((bf16[256,512]{1,0:T(8,128)(2,1)S(1)}, bf16[256,512]{1,0:T(8,128)(2,1)S(1)}, u32[]{:S(2)}, u32[]{:S(2)}) %collective-permute-start.11) | collective-permute-done | bytes 262176 | tf_op jit(solution)/shard_map/ppermute | solution.py:54
  (50 shorter events, 25.4 us)
Async XLA Ops:
  3.3 13.1 %copy-start = (bf16[1,2,512,512]{3,2,1,0:T(8,128)(2,1)S(1)}, bf16[1,2,512,512]{3,2,1,0:T(8,128)(2,1)}, u32[]{:S(2)}) copy-start(bf16[1,2,512,512]{3,2,1,0:T(8,128)(2,1)} %param.10) | copy-start | bytes 3145732
  3.3 17.5 %copy-start.5 = (f32[2,16,512]{2,1,0:T(8,128)S(1)}, f32[2,16,512]{2,1,0:T(8,128)}, u32[]{:S(2)}) copy-start(f32[2,16,512]{2,1,0:T(8,128)} %refs_3_.1) | copy-start | bytes 196612
  3.3 17.5 %copy-start.6 = (f32[2,16,512]{2,1,0:T(8,128)S(1)}, f32[2,16,512]{2,1,0:T(8,128)}, u32[]{:S(2)}) copy-start(f32[2,16,512]{2,1,0:T(8,128)} %refs_4_.1) | copy-start | bytes 196612
  3.3 57.1 %all-to-all-start = ((bf16[8,128,1024]{2,1,0:T(8,128)(2,1)}), bf16[8,128,1024]{2,1,0:T(8,128)(2,1)S(1)}, u32[]{:S(2)}, u32[]{:S(2)}) async-start(bf16[8,128,1024]{2,1,0:T(8,128)(2,1)} %shard_map.102), calls=%async_computation | async-start | bytes 4194304 | tf_op jit(solution)/shard_map/all_to_all | solution.py:48
  10.1 50.3 %collective-permute-start = (bf16[512,512]{1,0:T(8,128)(2,1)}, bf16[512,512]{1,0:T(8,128)(2,1)}, u32[]{:S(2)}, u32[]{:S(2)}) collective-permute-start(bf16[512,512]{1,0:T(8,128)(2,1)} %bitcast.30), channel_id=1, source_target_pairs={{0,7},{1,6},{2,5},{3,4},{4,3},{5,2},{6,1},{7,0},{8,15},{9,14},{10,... | collective-permute-start | bytes 1572872 | tf_op jit(solution)/shard_map/ppermute | solution.py:54
  17.1 3.6 %collective-permute-start.1 = (bf16[4,4,16,512]{3,2,1,0:T(8,128)(2,1)}, bf16[4,4,16,512]{3,2,1,0:T(8,128)(2,1)S(1)}, u32[]{:S(2)}, u32[]{:S(2)}) collective-permute-start(bf16[4,4,16,512]{3,2,1,0:T(8,128)(2,1)} %shard_map.103), channel_id=1, source_target_pairs={{0,16},{16,0},{1,17},{17,1},{2,18},{18,2},{3,19},{19,3},{4,20},{20... | collective-permute-start | bytes 786440 | tf_op jit(solution)/shard_map/ppermute | solution.py:304
  22.1 8.7 %collective-permute-start.2 = (bf16[4,16,512]{2,1,0:T(8,128)(2,1)}, bf16[4,16,512]{2,1,0:T(8,128)(2,1)S(1)}, u32[]{:S(2)}, u32[]{:S(2)}) collective-permute-start(bf16[4,16,512]{2,1,0:T(8,128)(2,1)} %get-tuple-element.17), channel_id=1, source_target_pairs={{0,32},{32,64},{64,96},{96,0},{1,33},{33,65},{65,97},{97,1},{2,34}... | collective-permute-start | bytes 196616 | tf_op jit(solution)/shard_map/ppermute | solution.py:180
  24.5 7.9 %collective-permute-start.3 = (bf16[4,16,512]{2,1,0:T(8,128)(2,1)}, bf16[4,16,512]{2,1,0:T(8,128)(2,1)S(1)}, u32[]{:S(2)}, u32[]{:S(2)}) collective-permute-start(bf16[4,16,512]{2,1,0:T(8,128)(2,1)} %get-tuple-element.18), channel_id=1, source_target_pairs={{0,64},{32,96},{64,0},{96,32},{1,65},{33,97},{65,1},{97,33},{2,66}... | collective-permute-start | bytes 196616 | tf_op jit(solution)/shard_map/ppermute | solution.py:180
  28.8 7.6 %collective-permute-start.4 = (bf16[4,16,512]{2,1,0:T(8,128)(2,1)}, bf16[4,16,512]{2,1,0:T(8,128)(2,1)S(1)}, u32[]{:S(2)}, u32[]{:S(2)}) collective-permute-start(bf16[4,16,512]{2,1,0:T(8,128)(2,1)} %get-tuple-element.19), channel_id=1, source_target_pairs={{0,96},{32,0},{64,32},{96,64},{1,97},{33,1},{65,33},{97,65},{2,98}... | collective-permute-start | bytes 196616 | tf_op jit(solution)/shard_map/ppermute | solution.py:180
  38.4 18.5 %collective-permute-start.5 = (bf16[16,512]{1,0:T(8,128)(2,1)S(1)}, bf16[16,512]{1,0:T(8,128)(2,1)S(1)}, u32[]{:S(2)}, u32[]{:S(2)}) collective-permute-start(bf16[16,512]{1,0:T(8,128)(2,1)S(1)} %get-tuple-element.22), channel_id=1, source_target_pairs={{0,128},{128,256},{256,384},{384,0},{1,129},{129,257},{257,385},{3... | collective-permute-start | bytes 49160 | tf_op jit(solution)/shard_map/ppermute | solution.py:180
  44.5 12.4 %collective-permute-start.6 = (bf16[16,512]{1,0:T(8,128)(2,1)S(1)}, bf16[16,512]{1,0:T(8,128)(2,1)S(1)}, u32[]{:S(2)}, u32[]{:S(2)}) collective-permute-start(bf16[16,512]{1,0:T(8,128)(2,1)S(1)} %get-tuple-element.23), channel_id=1, source_target_pairs={{0,256},{128,384},{256,0},{384,128},{1,257},{129,385},{257,1},{385... | collective-permute-start | bytes 49160 | tf_op jit(solution)/shard_map/ppermute | solution.py:180
  53.2 6.5 %collective-permute-start.7 = (bf16[16,512]{1,0:T(8,128)(2,1)S(1)}, bf16[16,512]{1,0:T(8,128)(2,1)S(1)}, u32[]{:S(2)}, u32[]{:S(2)}) collective-permute-start(bf16[16,512]{1,0:T(8,128)(2,1)S(1)} %get-tuple-element.24), channel_id=1, source_target_pairs={{0,384},{128,0},{256,128},{384,256},{1,385},{129,1},{257,129},{385... | collective-permute-start | bytes 49160 | tf_op jit(solution)/shard_map/ppermute | solution.py:180
  63.7 23.7 %copy-start.7 = (bf16[128,512]{1,0:T(8,128)(2,1)S(1)}, bf16[128,512]{1,0:T(8,128)(2,1)}, u32[]{:S(2)}) copy-start(bf16[128,512]{1,0:T(8,128)(2,1)} %c_ref.1) | copy-start | bytes 393220
  63.7 23.7 %all-to-all-start.1 = ((bf16[8,128,512]{2,1,0:T(8,128)(2,1)}), bf16[8,128,512]{2,1,0:T(8,128)(2,1)S(1)}, u32[]{:S(2)}, u32[]{:S(2)}) async-start(bf16[8,128,512]{2,1,0:T(8,128)(2,1)} %bitcast.29), calls=%async_computation.1 | async-start | bytes 2097152 | tf_op jit(solution)/shard_map/all_to_all | solution.py:48
  67.9 15.5 %collective-permute-start.8 = (bf16[16,512]{1,0:T(8,128)(2,1)S(1)}, bf16[16,512]{1,0:T(8,128)(2,1)S(1)}, u32[]{:S(2)}, u32[]{:S(2)}) collective-permute-start(bf16[16,512]{1,0:T(8,128)(2,1)S(1)} %get-tuple-element.25._.refs_0_), channel_id=1, source_target_pairs={{0,128},{128,256},{256,384},{384,0},{1,129},{129,257},{257,385},{3... | collective-permute-start | bytes 49160 | tf_op jit(solution)/shard_map/ppermute | solution.py:180
  71.3 12.2 %collective-permute-start.9 = (bf16[16,512]{1,0:T(8,128)(2,1)S(1)}, bf16[16,512]{1,0:T(8,128)(2,1)S(1)}, u32[]{:S(2)}, u32[]{:S(2)}) collective-permute-start(bf16[16,512]{1,0:T(8,128)(2,1)S(1)} %get-tuple-element.25._.refs_0_), channel_id=1, source_target_pairs={{0,256},{128,384},{256,0},{384,128},{1,257},{129,385},{257,1},{385... | collective-permute-start | bytes 49160 | tf_op jit(solution)/shard_map/ppermute | solution.py:180
  79.8 6.8 %collective-permute-start.10 = (bf16[16,512]{1,0:T(8,128)(2,1)S(1)}, bf16[16,512]{1,0:T(8,128)(2,1)S(1)}, u32[]{:S(2)}, u32[]{:S(2)}) collective-permute-start(bf16[16,512]{1,0:T(8,128)(2,1)S(1)} %get-tuple-element.25._.refs_0_), channel_id=1, source_target_pairs={{0,384},{128,0},{256,128},{384,256},{1,385},{129,1},{257,129},{385... | collective-permute-start | bytes 49160 | tf_op jit(solution)/shard_map/ppermute | solution.py:180
  88.6 29.9 %all-to-all-start.2 = ((bf16[8,128,512]{2,1,0:T(8,128)(2,1)}), bf16[8,128,512]{2,1,0:T(8,128)(2,1)S(1)}, u32[]{:S(2)}, u32[]{:S(2)}) async-start(bf16[8,128,512]{2,1,0:T(8,128)(2,1)} %copy-done.2), calls=%async_computation.2 | async-start | bytes 2097152 | tf_op jit(solution)/shard_map/all_to_all | solution.py:48
  94.5 8.0 %collective-permute-start.13 = (bf16[4,16,512]{2,1,0:T(8,128)(2,1)S(1)}, bf16[4,16,512]{2,1,0:T(8,128)(2,1)S(1)}, u32[]{:S(2)}, u32[]{:S(2)}) collective-permute-start(bf16[4,16,512]{2,1,0:T(8,128)(2,1)S(1)} %shard_map.108._.refs_0_), channel_id=1, source_target_pairs={{0,32},{32,64},{64,96},{96,0},{1,33},{33,65},{65,97},{97,1},{2,34}... | collective-permute-start | bytes 196616 | tf_op jit(solution)/shard_map/ppermute | solution.py:180
  96.9 7.7 %collective-permute-start.14 = (bf16[4,16,512]{2,1,0:T(8,128)(2,1)S(1)}, bf16[4,16,512]{2,1,0:T(8,128)(2,1)S(1)}, u32[]{:S(2)}, u32[]{:S(2)}) collective-permute-start(bf16[4,16,512]{2,1,0:T(8,128)(2,1)S(1)} %shard_map.108._.refs_0_), channel_id=1, source_target_pairs={{0,64},{32,96},{64,0},{96,32},{1,65},{33,97},{65,1},{97,33},{2,66}... | collective-permute-start | bytes 196616 | tf_op jit(solution)/shard_map/ppermute | solution.py:180
  100.5 7.8 %collective-permute-start.15 = (bf16[4,16,512]{2,1,0:T(8,128)(2,1)S(1)}, bf16[4,16,512]{2,1,0:T(8,128)(2,1)S(1)}, u32[]{:S(2)}, u32[]{:S(2)}) collective-permute-start(bf16[4,16,512]{2,1,0:T(8,128)(2,1)S(1)} %shard_map.108._.refs_0_), channel_id=1, source_target_pairs={{0,96},{32,0},{64,32},{96,64},{1,97},{33,1},{65,33},{97,65},{2,98}... | collective-permute-start | bytes 196616 | tf_op jit(solution)/shard_map/ppermute | solution.py:180
  108.3 18.3 %collective-permute-start.16 = (bf16[4,4,16,512]{3,2,1,0:T(8,128)(2,1)S(1)}, bf16[4,4,16,512]{3,2,1,0:T(8,128)(2,1)}, u32[]{:S(2)}, u32[]{:S(2)}) collective-permute-start(bf16[4,4,16,512]{3,2,1,0:T(8,128)(2,1)S(1)} %shard_map.113.m_ref), channel_id=1, source_target_pairs={{0,16},{16,0},{1,17},{17,1},{2,18},{18,2},{3,19},{19,3},{4,20},{20... | collective-permute-start | bytes 786440 | tf_op jit(solution)/shard_map/ppermute | solution.py:316
  119.5 9.8 %collective-permute-start.12 = (bf16[256,512]{1,0:T(8,128)(2,1)S(1)}, bf16[256,512]{1,0:T(8,128)(2,1)S(1)}, u32[]{:S(2)}, u32[]{:S(2)}) collective-permute-start(bf16[256,512]{1,0:T(8,128)(2,1)S(1)} %shard_map.112), channel_id=1, source_target_pairs={{0,7},{1,6},{2,5},{3,4},{4,3},{5,2},{6,1},{7,0},{8,15},{9,14},{10,... | collective-permute-start | bytes 786440 | tf_op jit(solution)/shard_map/ppermute | solution.py:54
  121.4 15.8 %collective-permute-start.11 = (bf16[256,512]{1,0:T(8,128)(2,1)S(1)}, bf16[256,512]{1,0:T(8,128)(2,1)S(1)}, u32[]{:S(2)}, u32[]{:S(2)}) collective-permute-start(bf16[256,512]{1,0:T(8,128)(2,1)S(1)} %shard_map.111), channel_id=1, source_target_pairs={{0,7},{1,6},{2,5},{3,4},{4,3},{5,2},{6,1},{7,0},{8,15},{9,14},{10,... | collective-permute-start | bytes 786440 | tf_op jit(solution)/shard_map/ppermute | solution.py:54
  (6 other events, 12.1 us)
